TPU v7x, 512 devices: a whole 4x8x8 slice. The times are simulated.
512 devices in a mesh: outer: 64 (over z_lo, y, core), inner: 8 (over z_hi, x).
Axes of the slice: x: 4, y: 8, z: 8 (z_hi: 2, z_lo: 4; z = z_hi * 4 + z_lo), core: 2. Of those that a mesh axis runs over, the one named last changes fastest.
Arguments:
- query_nope: bfloat16 [65536, 2048], P(('outer', 'inner')), may hold values from -400 to 400
- query_rope: bfloat16 [65536, 1024], P(('outer', 'inner')), may hold values from -6 to 6
- latent: bfloat16 [65536, 512], P(('outer', 'inner')), may hold values from -6 to 6
- key_rope: bfloat16 [65536, 64], P(('outer', 'inner')), may hold values from -6 to 6
- teacher_query: bfloat16 [65536, 2048], P(('outer', 'inner')), may hold values from -400 to 400
- teacher_key: bfloat16 [65536, 2048], P(('outer', 'inner')), may hold values from -6 to 6
- up_weight: bfloat16 [16, 128, 512], replicated, may hold values from -0.25 to 0.25
- kl_weight: float32 [65536, 16], P(('outer', 'inner')), may hold values from 30 to 300
- key_back: int32 [512], P(('outer', 'inner')), may hold values from 0 to 3, as said below
- valid_len: int32 [512], replicated, may hold values from 1 to 128, as said below
Outputs:
- d_query_nope: bfloat16 [65536, 2048], P(('outer', 'inner'))
- d_query_rope: bfloat16 [65536, 1024], P(('outer', 'inner'))
- d_latent: float32 [65536, 512], P(('outer', 'inner'))
- d_key_rope: float32 [65536, 64], P(('outer', 'inner'))
Inputs may be any that keep to these rules, and one draw needn't show every extreme that they name: key_back[b] <= b, and some block has key_back equal to 3. `valid_len`: some block is full.
All inputs are finite; a program needn't handle non-finite values.
Results may differ from a plain program's by a relative error of at most 0.012.
The roundings to bfloat16 on the way count: a program that leaves them out, or rounds other values in their place, can miss the bound.
Values may be sent and summed in bfloat16 or wider, within the bound.
No kernel may reach another device: no remote copies, remote signals or barrier semaphores. Data moves between devices by JAX's collectives and lax.ppermute only.
A program may use at most 64 MiB of HBM per device.

v0:
```python
import math

import jax
import jax.numpy as jnp
from jax import lax
from jax.sharding import PartitionSpec as P

HEADS = 16
HEAD = 128
ROPE = 64
TEACHER_HEAD = 128
SPAN = 4


def shifted(block, axis, distance):
    devices = range(lax.axis_size(axis))
    route = [(i - distance, i) for i in devices if i - distance in devices]
    return lax.ppermute(block, axis, route)


def slot_mask(reach_back, slot_lengths, own_length, tok_count, span_count):
    query_pos = jnp.arange(tok_count, dtype=jnp.int32)[:, None, None]
    key_pos = jnp.arange(tok_count, dtype=jnp.int32)[None, None, :]
    distance = (span_count - 1 - jnp.arange(span_count, dtype=jnp.int32))[None, :, None]
    allowed = (
        (distance <= reach_back)
        & (key_pos < slot_lengths[None, :, None])
        & ((distance > 0) | (key_pos <= query_pos))
    )
    live = jnp.arange(tok_count, dtype=jnp.int32) < own_length
    return (allowed.reshape(tok_count, span_count * tok_count), live)


def masked_softmax(logits, allowed):
    masked = jnp.where(allowed, logits, -1e30)
    highest = jnp.max(masked, axis=-1, keepdims=True)
    powers = jnp.where(allowed, jnp.exp(masked - highest), 0.0)
    return powers / jnp.sum(powers, axis=-1, keepdims=True)


def block_grads(
    nope_rows,
    rope_rows,
    latent_keys,
    rope_keys,
    teach_rows,
    teach_keys,
    up_weight,
    row_weight,
    allowed,
    live,
):
    tok_count = nope_rows.shape[0]
    key_count = latent_keys.shape[0]
    factor_student = 1.0 / math.sqrt(HEAD + ROPE)
    factor_teacher = 1.0 / math.sqrt(TEACHER_HEAD)
    nope_h = nope_rows.reshape(tok_count, HEADS, HEAD)
    rope_h = rope_rows.reshape(tok_count, HEADS, ROPE)
    teach_h = teach_rows.reshape(tok_count, HEADS, TEACHER_HEAD)
    tkeys_h = teach_keys.reshape(key_count, HEADS, TEACHER_HEAD)
    absorbed = jnp.einsum(
        "thd,hdl->thl", nope_h, up_weight, preferred_element_type=jnp.float32
    ).astype(jnp.bfloat16)
    student = (
        jnp.einsum("thl,kl->htk", absorbed, latent_keys, preferred_element_type=jnp.float32)
        + jnp.einsum("thr,kr->htk", rope_h, rope_keys, preferred_element_type=jnp.float32)
    ) * factor_student
    teacher = (
        jnp.einsum("thd,khd->htk", teach_h, tkeys_h, preferred_element_type=jnp.float32)
        * factor_teacher
    )
    p_student = masked_softmax(student, allowed[None])
    p_teacher = masked_softmax(teacher, allowed[None])
    coeff = (row_weight.T * live.astype(jnp.float32)[None, :])[:, :, None]
    grad_logit = (coeff * (p_student - p_teacher)).astype(jnp.bfloat16)
    d_absorbed = (
        jnp.einsum("htk,kl->thl", grad_logit, latent_keys, preferred_element_type=jnp.float32)
        * factor_student
    ).astype(jnp.bfloat16)
    d_nope = jnp.einsum(
        "thl,hdl->thd", d_absorbed, up_weight, preferred_element_type=jnp.float32
    ).astype(jnp.bfloat16)
    d_rope_q = (
        jnp.einsum("htk,kr->thr", grad_logit, rope_keys, preferred_element_type=jnp.float32)
        * factor_student
    ).astype(jnp.bfloat16)
    d_latent = (
        jnp.einsum("htk,thl->kl", grad_logit, absorbed, preferred_element_type=jnp.float32)
        * factor_student
    )
    d_rope_k = (
        jnp.einsum("htk,thr->kr", grad_logit, rope_h, preferred_element_type=jnp.float32)
        * factor_student
    )
    return (
        d_nope.reshape(tok_count, HEADS * HEAD),
        d_rope_q.reshape(tok_count, HEADS * ROPE),
        d_latent,
        d_rope_k,
    )


def on_device(
    query_nope,
    query_rope,
    latent,
    key_rope,
    teacher_query,
    teacher_key,
    up_weight,
    kl_weight,
    key_back,
    valid_len,
):
    tok_count = latent.shape[0]
    block_count = valid_len.shape[0]
    position = lax.axis_index(("outer", "inner"))
    arrived = [(latent, key_rope, teacher_key)]
    for distance in range(1, SPAN):
        arrived.append(shifted((latent, key_rope, teacher_key), ("outer", "inner"), distance))
    ordered = arrived[::-1]
    latent_keys = jnp.concatenate([entry[0] for entry in ordered], axis=0)
    rope_keys = jnp.concatenate([entry[1] for entry in ordered], axis=0)
    teach_keys = jnp.concatenate([entry[2] for entry in ordered], axis=0)
    slot_block = jnp.maximum(position - (SPAN - 1 - jnp.arange(SPAN, dtype=jnp.int32)), 0)
    matches = jnp.arange(block_count, dtype=jnp.int32)[None, :] == slot_block[:, None]
    slot_lengths = jnp.sum(jnp.where(matches, valid_len[None, :], 0), axis=1)
    allowed, live = slot_mask(key_back[0], slot_lengths, slot_lengths[SPAN - 1], tok_count, SPAN)
    d_nope, d_rope_q, d_latent, d_rope_k = block_grads(
        query_nope,
        query_rope,
        latent_keys,
        rope_keys,
        teacher_query,
        teach_keys,
        up_weight,
        kl_weight,
        allowed,
        live,
    )

    def portion(values, distance):
        return values[(SPAN - 1 - distance) * tok_count : (SPAN - distance) * tok_count]

    summed_latent = portion(d_latent, 0)
    summed_rope = portion(d_rope_k, 0)
    for distance in range(1, SPAN):
        returned = (
            shifted(
                portion(d_latent, distance).astype(jnp.bfloat16), ("outer", "inner"), -distance
            ).astype(jnp.float32),
            shifted(
                portion(d_rope_k, distance).astype(jnp.bfloat16), ("outer", "inner"), -distance
            ).astype(jnp.float32),
        )
        summed_latent = summed_latent + returned[0]
        summed_rope = summed_rope + returned[1]
    return (d_nope, d_rope_q, summed_latent, summed_rope)


def solution(mesh):
    placed = (
        P(("outer", "inner"), None),
        P(("outer", "inner"), None),
        P(("outer", "inner"), None),
        P(("outer", "inner"), None),
        P(("outer", "inner"), None),
        P(("outer", "inner"), None),
        P(),
        P(("outer", "inner"), None),
        P(("outer", "inner")),
        P(),
    )
    return jax.shard_map(
        on_device,
        mesh=mesh,
        in_specs=placed,
        out_specs=(
            P(("outer", "inner"), None),
            P(("outer", "inner"), None),
            P(("outer", "inner"), None),
            P(("outer", "inner"), None),
        ),
        check_vma=False,
    )
```

profile of v0, /device:TPU:74, one launch (start us, length us, event | category | flops | bytes accessed | tf_op | source)
XLA Modules:
  0.0 210.7 jit_solution(14186297889910919270)
XLA Ops:
  0.6 0.0 copy-start
  0.7 4.2 %collective-permute-start.4 = (bf16[128,64]{0,1:T(8,128)(2,1)}, bf16[128,64]{0,1:T(8,128)(2,1)S(1)}, u32[]{:S(2)}, u32[]{:S(2)}) collective-permute-start(bf16[128,64]{0,1:T(8,128)(2,1)} %param.13), channel_id=1, source_target_pairs={{0,2},{1,3},{2,4},{3,5},{4,6},{5,7},{6,8},{7,9},{8,10},{9,11},{10,... | collective-permute-start | bytes 49160 | tf_op jit(solution)/shard_map/ppermute | solution.py:18
  4.8 10.9 %collective-permute-start.3 = (bf16[128,64]{0,1:T(8,128)(2,1)}, bf16[128,64]{0,1:T(8,128)(2,1)S(1)}, u32[]{:S(2)}, u32[]{:S(2)}) collective-permute-start(bf16[128,64]{0,1:T(8,128)(2,1)} %param.13), channel_id=1, source_target_pairs={{0,3},{1,4},{2,5},{3,6},{4,7},{5,8},{6,9},{7,10},{8,11},{9,12},{10... | collective-permute-start | bytes 49160 | tf_op jit(solution)/shard_map/ppermute | solution.py:18
  15.7 1.3 copy.44
  17.0 2.5 %collective-permute-start.8 = (bf16[128,2048]{0,1:T(8,128)(2,1)S(1)}, bf16[128,2048]{0,1:T(8,128)(2,1)S(1)}, u32[]{:S(2)}, u32[]{:S(2)}) collective-permute-start(bf16[128,2048]{0,1:T(8,128)(2,1)S(1)} %copy.44), channel_id=1, source_target_pairs={{0,1},{1,2},{2,3},{3,4},{4,5},{5,6},{6,7},{7,8},{8,9},{9,10},{10,1... | collective-permute-start | bytes 1572872 | tf_op jit(solution)/shard_map/ppermute | solution.py:18
  19.5 3.4 %collective-permute-start.7 = (bf16[128,2048]{0,1:T(8,128)(2,1)S(1)}, bf16[128,2048]{0,1:T(8,128)(2,1)}, u32[]{:S(2)}, u32[]{:S(2)}) collective-permute-start(bf16[128,2048]{0,1:T(8,128)(2,1)S(1)} %copy.44), channel_id=1, source_target_pairs={{0,2},{1,3},{2,4},{3,5},{4,6},{5,7},{6,8},{7,9},{8,10},{9,11},{10,... | collective-permute-start | bytes 1572872 | tf_op jit(solution)/shard_map/ppermute | solution.py:18
  23.0 6.3 %collective-permute-start.6 = (bf16[128,2048]{0,1:T(8,128)(2,1)S(1)}, bf16[128,2048]{0,1:T(8,128)(2,1)}, u32[]{:S(2)}, u32[]{:S(2)}) collective-permute-start(bf16[128,2048]{0,1:T(8,128)(2,1)S(1)} %copy.44), channel_id=1, source_target_pairs={{0,3},{1,4},{2,5},{3,6},{4,7},{5,8},{6,9},{7,10},{8,11},{9,12},{10... | collective-permute-start | bytes 1572872 | tf_op jit(solution)/shard_map/ppermute | solution.py:18
  30.0 0.9 select_reduce_fusion
  30.9 0.6 slice.33
  31.4 0.6 compare_convert_fusion
  32.1 0.1 lt.36
  32.2 0.6 fusion.32
  32.8 1.3 multiply_bitcast_fusion
  34.1 3.2 %convolution_convert_fusion = bf16[16,512,128]{2,1,0:T(8,128)(2,1)} fusion(bf16[16,128,512]{2,1,0:T(8,128)(2,1)S(1)} %copy-done, bf16[128,2048]{1,0:T(8,128)(2,1)} %param.10), kind=kOutput, calls=%fused_computation.18 | convolution fusion | flops 269484032 | bytes 4718592 | tf_op jit(solution)/shard_map/thd,hdl->thl/dot_general | solution.py:61
  37.2 0.6 broadcast_bitcast_fusion
  37.8 4.3 %collective-permute-start.5 = (bf16[128,64]{0,1:T(8,128)(2,1)S(1)}, bf16[128,64]{0,1:T(8,128)(2,1)S(1)}, u32[]{:S(2)}, u32[]{:S(2)}) collective-permute-start(bf16[128,64]{0,1:T(8,128)(2,1)S(1)} %copy-done.4), channel_id=1, source_target_pairs={{0,1},{1,2},{2,3},{3,4},{4,5},{5,6},{6,7},{7,8},{8,9},{9,10},{10,1... | collective-permute-start | bytes 49160 | tf_op jit(solution)/shard_map/ppermute | solution.py:18
  42.2 1.1 copy.43
  43.3 0.9 fusion.28
  44.2 0.0 copy-start.6
  44.2 3.8 %collective-permute-start.1 = (bf16[128,512]{1,0:T(8,128)(2,1)}, bf16[128,512]{1,0:T(8,128)(2,1)}, u32[]{:S(2)}, u32[]{:S(2)}) collective-permute-start(bf16[128,512]{1,0:T(8,128)(2,1)} %param.12), channel_id=1, source_target_pairs={{0,2},{1,3},{2,4},{3,5},{4,6},{5,7},{6,8},{7,9},{8,10},{9,11},{10,... | collective-permute-start | bytes 393224 | tf_op jit(solution)/shard_map/ppermute | solution.py:18
  48.0 0.0 copy-start.7
  48.0 50.8 %collective-permute-start = (bf16[128,512]{1,0:T(8,128)(2,1)}, bf16[128,512]{1,0:T(8,128)(2,1)}, u32[]{:S(2)}, u32[]{:S(2)}) collective-permute-start(bf16[128,512]{1,0:T(8,128)(2,1)} %param.12), channel_id=1, source_target_pairs={{0,3},{1,4},{2,5},{3,6},{4,7},{5,8},{6,9},{7,10},{8,11},{9,12},{10... | collective-permute-start | bytes 393224 | tf_op jit(solution)/shard_map/ppermute | solution.py:18
  98.8 0.0 copy-start.3
  98.8 2.7 %fusion.31 = f32[512,128,16]{1,0,2:T(8,128)} fusion(bf16[128,16,64]{0,2,1:T(8,128)(2,1)S(1)} %bitcast.106, bf16[128,64]{0,1:T(8,128)(2,1)S(1)} %copy-done.4, bf16[128,64]{0,1:T(8,128)(2,1)S(1)} %collective-permute-done.5, bf16[128,64]{0,1:T(8,128)(2,1)S(1)} %collective-permute-done.4, bf16[128,64]{0,1:T(8,128)(2,1)S(1)} %collective-permute-done.3), kind=kOutput, calls=%fused_computation.43 | convolution fusion | flops 134479872 | bytes 4521984 | tf_op jit(solution)/shard_map/thr,kr->htk/dot_general | solution.py:66
  101.5 2.1 collective-permute-start.2
  103.6 1.4 pad_maximum_fusion
  105.1 0.8 fusion.21
  105.9 1.9 copy-done.2
  107.8 4.0 %exponential_select_fusion = f32[16,128,512]{1,2,0:T(8,128)} fusion(f32[16,512,128]{2,1,0:T(8,128)S(1)} %fusion.21, pred[128,512]{0,1:T(8,128)(4,1)S(1)} %fusion.28), kind=kOutput, calls=%fused_computation.8 | output fusion | flops 6294015 | bytes 8454144 | tf_op jit(solution)/shard_map/sub | solution.py:37
  111.8 7.9 %fusion = f32[16,128,512]{1,2,0:T(8,128)} fusion(f32[16,512,128]{2,1,0:T(8,128)} %copy-done.2, pred[128,512]{0,1:T(8,128)(4,1)S(1)} %fusion.28), kind=kOutput, calls=%fused_computation | output fusion | flops 6296574 | bytes 8454144 | tf_op jit(solution)/shard_map/div | solution.py:38
  119.7 10.3 %multiply_convert_fusion.1 = bf16[16,128,512]{1,2,0:T(8,128)(2,1)} fusion(f32[16,128,512]{1,2,0:T(8,128)} %exponential_select_fusion, f32[16,128,512]{1,2,0:T(8,128)} %fusion, f32[16,128]{1,0:T(8,128)S(1)} %copy-done.8, pred[128,512]{0,1:T(8,128)(4,1)S(1)} %fusion.28, f32[512,128,16]{1,0,2:T(8,128)} %fusion.31, ...), kind=kOutput, calls=%fused_computation.7 | convolution fusion | flops 1086329856 | bytes 17375232 | tf_op jit(solution)/shard_map/div | solution.py:38
  130.0 4.6 %fusion.51 = (bf16[512,512]{1,0:T(8,128)(2,1)S(1)}, f32[512,512]{1,0:T(8,128)}) fusion(bf16[16,128,512]{1,2,0:T(8,128)(2,1)} %multiply_convert_fusion.1, bf16[16,512,128]{2,1,0:T(8,128)(2,1)} %convolution_convert_fusion), kind=kOutput, calls=%fused_computation.68 | convolution fusion | flops 1074266112 | bytes 5767168 | tf_op jit(solution)/shard_map/htk,thl->kl/dot_general | solution.py:88
  134.6 0.8 fusion.52
  135.4 0.6 fusion.50
  136.0 3.9 %collective-permute-start.12 = (bf16[128,64]{0,1:T(8,128)(2,1)}, bf16[128,64]{0,1:T(8,128)(2,1)}, u32[]{:S(2)}, u32[]{:S(2)}) collective-permute-start(bf16[128,64]{0,1:T(8,128)(2,1)} %get-tuple-element.19), channel_id=1, source_target_pairs={{1,0},{2,1},{3,2},{4,3},{5,4},{6,5},{7,6},{8,7},{9,8},{10,9},{11,1... | collective-permute-start | bytes 49160 | tf_op jit(solution)/shard_map/ppermute | solution.py:18
  139.9 1.9 collective-permute-start.14
  141.9 21.4 %collective-permute-start.13 = (bf16[128,64]{0,1:T(8,128)(2,1)}, bf16[128,64]{0,1:T(8,128)(2,1)}, u32[]{:S(2)}, u32[]{:S(2)}) collective-permute-start(bf16[128,64]{0,1:T(8,128)(2,1)} %get-tuple-element.21), channel_id=1, source_target_pairs={{2,0},{3,1},{4,2},{5,3},{6,4},{7,5},{8,6},{9,7},{10,8},{11,9},{12,... | collective-permute-start | bytes 49160 | tf_op jit(solution)/shard_map/ppermute | solution.py:18
  163.2 3.7 %fusion.18 = bf16[16,128,128]{1,2,0:T(8,128)(2,1)S(1)} fusion(bf16[16,128,512]{2,1,0:T(8,128)(2,1)S(1)} %copy-done, bf16[16,128,512]{1,2,0:T(8,128)(2,1)} %multiply_convert_fusion.1, bf16[128,512]{1,0:T(8,128)(2,1)} %param.12, bf16[128,512]{1,0:T(8,128)(2,1)} %collective-permute-done.2, bf16[128,512]{1,0:T(8,128)(2,1)} %collective-permute-done.1, ...), kind=kOutput, calls=%fused_computation.22 | convolution fusion | flops 1346633728 | bytes 5242880 | tf_op jit(solution)/shard_map/thl,hdl->thd/dot_general | solution.py:80
  167.0 2.1 %fusion.19 = bf16[64,16,128]{2,0,1:T(8,128)(2,1)S(1)} fusion(bf16[16,128,512]{1,2,0:T(8,128)(2,1)} %multiply_convert_fusion.1, bf16[128,64]{0,1:T(8,128)(2,1)S(1)} %copy-done.4, bf16[128,64]{0,1:T(8,128)(2,1)} %copy-done.7, bf16[128,64]{0,1:T(8,128)(2,1)} %copy-done.5, bf16[128,64]{0,1:T(8,128)(2,1)} %copy-done.6), kind=kOutput, calls=%fused_computation.24 | convolution fusion | flops 134742016 | bytes 2424832 | tf_op jit(solution)/shard_map/htk,kr->thr/dot_general | solution.py:84
  169.1 0.8 fusion.49
  169.9 0.8 copy.56
  170.7 1.0 copy.55
  171.7 11.8 %collective-permute-start.9 = (bf16[128,512]{1,0:T(8,128)(2,1)}, bf16[128,512]{1,0:T(8,128)(2,1)S(1)}, u32[]{:S(2)}, u32[]{:S(2)}) collective-permute-start(bf16[128,512]{1,0:T(8,128)(2,1)} %get-tuple-element.16), channel_id=1, source_target_pairs={{1,0},{2,1},{3,2},{4,3},{5,4},{6,5},{7,6},{8,7},{9,8},{10,9},{11,1... | collective-permute-start | bytes 393224 | tf_op jit(solution)/shard_map/ppermute | solution.py:18
  183.6 16.8 %collective-permute-start.11 = (bf16[128,512]{1,0:T(8,128)(2,1)}, bf16[128,512]{1,0:T(8,128)(2,1)S(1)}, u32[]{:S(2)}, u32[]{:S(2)}) collective-permute-start(bf16[128,512]{1,0:T(8,128)(2,1)} %get-tuple-element.17), channel_id=1, source_target_pairs={{3,0},{4,1},{5,2},{6,3},{7,4},{8,5},{9,6},{10,7},{11,8},{12,9},{13... | collective-permute-start | bytes 393224 | tf_op jit(solution)/shard_map/ppermute | solution.py:18
  200.4 3.4 %collective-permute-start.10 = (bf16[128,512]{1,0:T(8,128)(2,1)}, bf16[128,512]{1,0:T(8,128)(2,1)S(1)}, u32[]{:S(2)}, u32[]{:S(2)}) collective-permute-start(bf16[128,512]{1,0:T(8,128)(2,1)} %get-tuple-element.18), channel_id=1, source_target_pairs={{2,0},{3,1},{4,2},{5,3},{6,4},{7,5},{8,6},{9,7},{10,8},{11,9},{12,... | collective-permute-start | bytes 393224 | tf_op jit(solution)/shard_map/ppermute | solution.py:18
  203.8 1.4 fusion.30
  205.2 3.8 %collective-permute-done.10 = bf16[128,512]{1,0:T(8,128)(2,1)S(1)} collective-permute-done((bf16[128,512]{1,0:T(8,128)(2,1)}, bf16[128,512]{1,0:T(8,128)(2,1)S(1)}, u32[]{:S(2)}, u32[]{:S(2)}) %collective-permute-start.10) | collective-permute-done | bytes 131104 | tf_op jit(solution)/shard_map/ppermute | solution.py:18
  208.9 1.7 fusion.27
  (31 shorter events, 0.1 us)
Async XLA Ops:
  0.6 33.4 %copy-start = (bf16[16,128,512]{2,1,0:T(8,128)(2,1)S(1)}, bf16[16,128,512]{2,1,0:T(8,128)(2,1)}, u32[]{:S(2)}) copy-start(bf16[16,128,512]{2,1,0:T(8,128)(2,1)} %param.16) | copy-start | bytes 6291460
  0.6 37.2 %copy-start.4 = (bf16[128,64]{0,1:T(8,128)(2,1)S(1)}, bf16[128,64]{0,1:T(8,128)(2,1)}, u32[]{:S(2)}) copy-start(bf16[128,64]{0,1:T(8,128)(2,1)} %param.13) | copy-start | bytes 49156
  0.7 37.1 %collective-permute-start.4 = (bf16[128,64]{0,1:T(8,128)(2,1)}, bf16[128,64]{0,1:T(8,128)(2,1)S(1)}, u32[]{:S(2)}, u32[]{:S(2)}) collective-permute-start(bf16[128,64]{0,1:T(8,128)(2,1)} %param.13), channel_id=1, source_target_pairs={{0,2},{1,3},{2,4},{3,5},{4,6},{5,7},{6,8},{7,9},{8,10},{9,11},{10,... | collective-permute-start | bytes 49160 | tf_op jit(solution)/shard_map/ppermute | solution.py:18
  4.8 39.3 %collective-permute-start.3 = (bf16[128,64]{0,1:T(8,128)(2,1)}, bf16[128,64]{0,1:T(8,128)(2,1)S(1)}, u32[]{:S(2)}, u32[]{:S(2)}) collective-permute-start(bf16[128,64]{0,1:T(8,128)(2,1)} %param.13), channel_id=1, source_target_pairs={{0,3},{1,4},{2,5},{3,6},{4,7},{5,8},{6,9},{7,10},{8,11},{9,12},{10... | collective-permute-start | bytes 49160 | tf_op jit(solution)/shard_map/ppermute | solution.py:18
  17.0 84.4 %collective-permute-start.8 = (bf16[128,2048]{0,1:T(8,128)(2,1)S(1)}, bf16[128,2048]{0,1:T(8,128)(2,1)S(1)}, u32[]{:S(2)}, u32[]{:S(2)}) collective-permute-start(bf16[128,2048]{0,1:T(8,128)(2,1)S(1)} %copy.44), channel_id=1, source_target_pairs={{0,1},{1,2},{2,3},{3,4},{4,5},{5,6},{6,7},{7,8},{8,9},{9,10},{10,1... | collective-permute-start | bytes 1572872 | tf_op jit(solution)/shard_map/ppermute | solution.py:18
  19.5 84.0 %collective-permute-start.7 = (bf16[128,2048]{0,1:T(8,128)(2,1)S(1)}, bf16[128,2048]{0,1:T(8,128)(2,1)}, u32[]{:S(2)}, u32[]{:S(2)}) collective-permute-start(bf16[128,2048]{0,1:T(8,128)(2,1)S(1)} %copy.44), channel_id=1, source_target_pairs={{0,2},{1,3},{2,4},{3,5},{4,6},{5,7},{6,8},{7,9},{8,10},{9,11},{10,... | collective-permute-start | bytes 1572872 | tf_op jit(solution)/shard_map/ppermute | solution.py:18
  23.0 80.6 %collective-permute-start.6 = (bf16[128,2048]{0,1:T(8,128)(2,1)S(1)}, bf16[128,2048]{0,1:T(8,128)(2,1)}, u32[]{:S(2)}, u32[]{:S(2)}) collective-permute-start(bf16[128,2048]{0,1:T(8,128)(2,1)S(1)} %copy.44), channel_id=1, source_target_pairs={{0,3},{1,4},{2,5},{3,6},{4,7},{5,8},{6,9},{7,10},{8,11},{9,12},{10... | collective-permute-start | bytes 1572872 | tf_op jit(solution)/shard_map/ppermute | solution.py:18
  37.8 67.2 %copy-start.5 = (bf16[128,64]{0,1:T(8,128)(2,1)}, bf16[128,64]{0,1:T(8,128)(2,1)S(1)}, u32[]{:S(2)}) copy-start(bf16[128,64]{0,1:T(8,128)(2,1)S(1)} %collective-permute-done.4) | copy-start | bytes 49156
  37.8 10.2 %collective-permute-start.5 = (bf16[128,64]{0,1:T(8,128)(2,1)S(1)}, bf16[128,64]{0,1:T(8,128)(2,1)S(1)}, u32[]{:S(2)}, u32[]{:S(2)}) collective-permute-start(bf16[128,64]{0,1:T(8,128)(2,1)S(1)} %copy-done.4), channel_id=1, source_target_pairs={{0,1},{1,2},{2,3},{3,4},{4,5},{5,6},{6,7},{7,8},{8,9},{9,10},{10,1... | collective-permute-start | bytes 49160 | tf_op jit(solution)/shard_map/ppermute | solution.py:18
  44.2 60.9 %copy-start.6 = (bf16[128,64]{0,1:T(8,128)(2,1)}, bf16[128,64]{0,1:T(8,128)(2,1)S(1)}, u32[]{:S(2)}) copy-start(bf16[128,64]{0,1:T(8,128)(2,1)S(1)} %collective-permute-done.3) | copy-start | bytes 49156
  44.2 75.5 %collective-permute-start.1 = (bf16[128,512]{1,0:T(8,128)(2,1)}, bf16[128,512]{1,0:T(8,128)(2,1)}, u32[]{:S(2)}, u32[]{:S(2)}) collective-permute-start(bf16[128,512]{1,0:T(8,128)(2,1)} %param.12), channel_id=1, source_target_pairs={{0,2},{1,3},{2,4},{3,5},{4,6},{5,7},{6,8},{7,9},{8,10},{9,11},{10,... | collective-permute-start | bytes 393224 | tf_op jit(solution)/shard_map/ppermute | solution.py:18
  48.0 57.1 %copy-start.7 = (bf16[128,64]{0,1:T(8,128)(2,1)}, bf16[128,64]{0,1:T(8,128)(2,1)S(1)}, u32[]{:S(2)}) copy-start(bf16[128,64]{0,1:T(8,128)(2,1)S(1)} %collective-permute-done.5) | copy-start | bytes 49156
  48.0 71.7 %collective-permute-start = (bf16[128,512]{1,0:T(8,128)(2,1)}, bf16[128,512]{1,0:T(8,128)(2,1)}, u32[]{:S(2)}, u32[]{:S(2)}) collective-permute-start(bf16[128,512]{1,0:T(8,128)(2,1)} %param.12), channel_id=1, source_target_pairs={{0,3},{1,4},{2,5},{3,6},{4,7},{5,8},{6,9},{7,10},{8,11},{9,12},{10... | collective-permute-start | bytes 393224 | tf_op jit(solution)/shard_map/ppermute | solution.py:18
  98.8 6.3 %copy-start.3 = (bf16[128,2048]{1,0:T(8,128)(2,1)S(1)}, bf16[128,2048]{1,0:T(8,128)(2,1)}, u32[]{:S(2)}) copy-start(bf16[128,2048]{1,0:T(8,128)(2,1)} %param.14) | copy-start | bytes 1572868
  101.5 18.2 %collective-permute-start.2 = (bf16[128,512]{1,0:T(8,128)(2,1)}, bf16[128,512]{1,0:T(8,128)(2,1)}, u32[]{:S(2)}, u32[]{:S(2)}) collective-permute-start(bf16[128,512]{1,0:T(8,128)(2,1)} %param.12), channel_id=1, source_target_pairs={{0,1},{1,2},{2,3},{3,4},{4,5},{5,6},{6,7},{7,8},{8,9},{9,10},{10,1... | collective-permute-start | bytes 393224 | tf_op jit(solution)/shard_map/ppermute | solution.py:18
  105.8 1.9 copy-start.2
  111.8 7.9 %copy-start.8 = (f32[16,128]{1,0:T(8,128)S(1)}, f32[16,128]{1,0:T(8,128)}, u32[]{:S(2)}) copy-start(f32[16,128]{1,0:T(8,128)} %multiply_bitcast_fusion) | copy-start | bytes 24580
  130.0 4.6 %copy-start.1 = (bf16[16,128,512]{1,2,0:T(8,128)(2,1)S(1)}, bf16[16,128,512]{1,2,0:T(8,128)(2,1)}, u32[]{:S(2)}) copy-start(bf16[16,128,512]{1,2,0:T(8,128)(2,1)} %multiply_convert_fusion.1) | copy-start | bytes 6291460
  136.0 64.3 %collective-permute-start.12 = (bf16[128,64]{0,1:T(8,128)(2,1)}, bf16[128,64]{0,1:T(8,128)(2,1)}, u32[]{:S(2)}, u32[]{:S(2)}) collective-permute-start(bf16[128,64]{0,1:T(8,128)(2,1)} %get-tuple-element.19), channel_id=1, source_target_pairs={{1,0},{2,1},{3,2},{4,3},{5,4},{6,5},{7,6},{8,7},{9,8},{10,9},{11,1... | collective-permute-start | bytes 49160 | tf_op jit(solution)/shard_map/ppermute | solution.py:18
  139.9 63.8 %collective-permute-start.14 = (bf16[128,64]{0,1:T(8,128)(2,1)}, bf16[128,64]{0,1:T(8,128)(2,1)}, u32[]{:S(2)}, u32[]{:S(2)}) collective-permute-start(bf16[128,64]{0,1:T(8,128)(2,1)} %get-tuple-element.20), channel_id=1, source_target_pairs={{3,0},{4,1},{5,2},{6,3},{7,4},{8,5},{9,6},{10,7},{11,8},{12,9},{13... | collective-permute-start | bytes 49160 | tf_op jit(solution)/shard_map/ppermute | solution.py:18
  141.9 61.9 %collective-permute-start.13 = (bf16[128,64]{0,1:T(8,128)(2,1)}, bf16[128,64]{0,1:T(8,128)(2,1)}, u32[]{:S(2)}, u32[]{:S(2)}) collective-permute-start(bf16[128,64]{0,1:T(8,128)(2,1)} %get-tuple-element.21), channel_id=1, source_target_pairs={{2,0},{3,1},{4,2},{5,3},{6,4},{7,5},{8,6},{9,7},{10,8},{11,9},{12,... | collective-permute-start | bytes 49160 | tf_op jit(solution)/shard_map/ppermute | solution.py:18
  171.7 33.4 %collective-permute-start.9 = (bf16[128,512]{1,0:T(8,128)(2,1)}, bf16[128,512]{1,0:T(8,128)(2,1)S(1)}, u32[]{:S(2)}, u32[]{:S(2)}) collective-permute-start(bf16[128,512]{1,0:T(8,128)(2,1)} %get-tuple-element.16), channel_id=1, source_target_pairs={{1,0},{2,1},{3,2},{4,3},{5,4},{6,5},{7,6},{8,7},{9,8},{10,9},{11,1... | collective-permute-start | bytes 393224 | tf_op jit(solution)/shard_map/ppermute | solution.py:18
  183.6 21.6 %collective-permute-start.11 = (bf16[128,512]{1,0:T(8,128)(2,1)}, bf16[128,512]{1,0:T(8,128)(2,1)S(1)}, u32[]{:S(2)}, u32[]{:S(2)}) collective-permute-start(bf16[128,512]{1,0:T(8,128)(2,1)} %get-tuple-element.17), channel_id=1, source_target_pairs={{3,0},{4,1},{5,2},{6,3},{7,4},{8,5},{9,6},{10,7},{11,8},{12,9},{13... | collective-permute-start | bytes 393224 | tf_op jit(solution)/shard_map/ppermute | solution.py:18
  200.4 8.6 %collective-permute-start.10 = (bf16[128,512]{1,0:T(8,128)(2,1)}, bf16[128,512]{1,0:T(8,128)(2,1)S(1)}, u32[]{:S(2)}, u32[]{:S(2)}) collective-permute-start(bf16[128,512]{1,0:T(8,128)(2,1)} %get-tuple-element.18), channel_id=1, source_target_pairs={{2,0},{3,1},{4,2},{5,3},{6,4},{7,5},{8,6},{9,7},{10,8},{11,9},{12,... | collective-permute-start | bytes 393224 | tf_op jit(solution)/shard_map/ppermute | solution.py:18
where the time goes:
time: 212 us; the launch traced here: 211 us
  starting transfers between devices  147 us (69%)
  matrix products  28.1 us (13%)
  other arithmetic  20.7 us (10%)
  local copies, waits for them, and re-layouts  8.88 us (4%)
  waiting for transfers between devices  3.82 us (2%)
    ppermute x15, starting transfers between devices, shifted(): return lax.ppermute(block, axis, route)  147 us
    div x1, matrix products, masked_softmax(): return powers / jnp.sum(powers, axis=-1, keepdims=True)  10.3 us
    div x1, other arithmetic, masked_softmax(): return powers / jnp.sum(powers, axis=-1, keepdims=True)  7.87 us
    unnamed x22, local copies, waits for them, and re-layouts  6.25 us
    dot_general x1, matrix products, block_grads(): jnp.einsum('htk,thl->kl', grad_logit, absorbed, preferred_element_type=jn...  4.63 us
  transfers between devices with their start and end apart: 15, of which 1 were waited for; matrix products, arithmetic and copies ran while one was open for 18% of the time, Pallas kernels for 0%

commit v1 on v0

v1 whole, which is shorter than its diff:
```python
import functools
import math

import jax
import jax.numpy as jnp
from jax import lax
from jax.experimental import pallas as pl
from jax.experimental.pallas import tpu as pltpu
from jax.sharding import PartitionSpec as P

HEADS = 16
HEAD = 128
LATENT = 512
ROPE = 64
TOK = 128
SPAN = 4
KEYS = SPAN * TOK
WIDE = LATENT + 2 * ROPE
PAIRS = HEADS // 2
FIRST = 3
RING = 4
AXES = ("outer", "inner")
F_STUDENT = 1.0 / math.sqrt(HEAD + ROPE)
F_TEACHER = 1.0 / math.sqrt(HEAD)
LOG2E = math.log2(math.e)
VMEM_LIMIT = 48 * 1024 * 1024

NN = (((1,), (0,)), ((), ()))
NT = (((1,), (1,)), ((), ()))


def dot(a, b, dims=NN):
    return lax.dot_general(a, b, dims, preferred_element_type=jnp.float32)


def along_x(step, sources):
    def route(count):
        return [
            (b, b - b % RING + (b + step) % RING) for b in range(count) if b % RING in sources
        ]

    return route


def next_run(count):
    return [(b, b + RING) for b in range(count - RING)]


def permute(value, route):
    return lax.ppermute(value, AXES, route(lax.axis_size(AXES)))


def softmax_parts(logits):
    powers = jnp.exp2(logits - jnp.max(logits, axis=0, keepdims=True))
    return powers, jnp.sum(powers, axis=0, keepdims=True)


def from_slots(place, sources, act):
    own, own1, own2, rotated, crossed, back, around = sources
    act(0, own)
    for distance, here, earlier, first in ((1, own1, around, 1), (2, own2, back, 2), (3, rotated, crossed, 3)):
        pl.when(place >= first)(functools.partial(act, distance, here))
        pl.when(place < first)(functools.partial(act, distance, earlier))


def student_kernel(
    scalar_ref, length_ref, nope_ref, rope_ref, up_ref, kl_ref, *refs
):
    sources, (mixed_ref, p_ref, bias_ref, coeff_ref, lr_ref, lrt_ref, sems) = refs[:7], refs[7:]
    step = pl.program_id(0)
    position = scalar_ref[0]
    starts = [HEADS * HEAD] * 3 + [FIRST * 2 * HEAD] * 4
    place = position % RING

    @pl.when(step == 0)
    def _():
        columns = dict(zip(map(id, sources), starts))

        def copy(distance, source):
            return pltpu.make_async_copy(
                source.at[:, pl.ds(columns[id(source)], WIDE)],
                lr_ref.at[pl.ds(distance * TOK, TOK)],
                sems.at[distance],
            )

        from_slots(place, sources, lambda distance, source: copy(distance, source).start())
        query = lax.broadcasted_iota(jnp.int32, (TOK, TOK), 1)
        key = lax.broadcasted_iota(jnp.int32, (TOK, TOK), 0)
        for distance in range(SPAN):
            length = length_ref[jnp.maximum(position - distance, 0)]
            length = jnp.where(distance <= scalar_ref[1], length, 0)
            allowed = key < length
            if distance == 0:
                allowed = allowed & (key <= query)
            bias_ref[pl.ds(distance * TOK, TOK), :] = jnp.where(allowed, 0.0, -1e30)
        live = lax.broadcasted_iota(jnp.int32, (HEADS, TOK), 1) < length_ref[position]
        coeff_ref[...] = jnp.where(live, kl_ref[...].T, 0.0)
        for distance in range(SPAN):
            copy(distance, sources[0] if distance < 3 else sources[3]).wait()
        lrt_ref[...] = lr_ref[...].T

    lane = lax.broadcasted_iota(jnp.int32, (TOK, 2 * ROPE), 1)
    rope = rope_ref[...]
    for half in range(2):
        rows = pl.ds(half * TOK, TOK)
        absorbed = dot(nope_ref[:, pl.ds(half * HEAD, HEAD)], up_ref[half])
        mixed_ref[rows, pl.ds(0, LATENT)] = absorbed.astype(jnp.bfloat16)
        kept = (lane < ROPE) if half == 0 else (lane >= ROPE)
        mixed_ref[rows, pl.ds(LATENT, 2 * ROPE)] = jnp.where(kept, rope, jnp.zeros_like(rope))
    logits = dot(lr_ref[...], mixed_ref[...], NT)
    for half in range(2):
        columns = slice(half * TOK, (half + 1) * TOK)
        powers, total = softmax_parts(logits[:, columns] * (F_STUDENT * LOG2E) + bias_ref[...])
        weight = coeff_ref[pl.ds(2 * step + half, 1), :]
        p_ref[:, columns] = powers * (weight / total)


def teacher_kernel(first, pairs, last, scalar_ref, *refs):
    sources, refs = refs[:7], refs[7:]
    (query_ref, p_ref, bias_ref, coeff_ref, mixed_ref), refs = refs[:5], refs[5:]
    if last:
        sum_ref, g_ref, own_ref, *sent_refs = refs[:6]
    else:
        g_ref, sum_out_ref = refs[:2]
    acc_ref, keys_ref, diagonal_ref, sems = refs[-4:]
    step = pl.program_id(0)
    place = scalar_ref[0] % RING
    starts = [first * 2 * HEAD] * 3 + [0] * 4
    columns = dict(zip(map(id, sources), starts))

    def copy(pair, distance, source):
        return pltpu.make_async_copy(
            source.at[:, pl.ds(columns[id(source)] + pair * 2 * HEAD, 2 * HEAD)],
            keys_ref.at[pair, pl.ds(distance * TOK, TOK)],
            sems.at[pair, distance],
        )

    @pl.when(step == 0)
    def _():
        for pair in range(pairs):
            from_slots(
                place, sources, lambda distance, source, pair=pair: copy(pair, distance, source).start()
            )
        diagonal_ref[...] = jnp.zeros_like(diagonal_ref)
        if last:
            acc_ref[...] = sum_ref[...]
        else:
            acc_ref[...] = jnp.zeros_like(acc_ref)

    for half in range(2):
        block = pl.ds(half * HEAD, HEAD)
        diagonal_ref[block, block] = query_ref[:, block]
    for pair in range(pairs):

        @pl.when(step == pair)
        def _(pair=pair):
            for distance in range(SPAN):
                copy(pair, distance, sources[0] if distance < 3 else sources[3]).wait()

    logits = dot(keys_ref[step], diagonal_ref[...], NT)
    for half in range(2):
        cols = slice(half * TOK, (half + 1) * TOK)
        powers, total = softmax_parts(logits[:, cols] * (F_TEACHER * LOG2E) + bias_ref[...])
        weight = coeff_ref[pl.ds(2 * (first + step) + half, 1), :]
        g_ref[:, cols] = (p_ref[:, cols] - powers * (weight / total)).astype(jnp.bfloat16)
    acc_ref[...] += dot(g_ref[...], mixed_ref[...])

    @pl.when(step == pairs - 1)
    def _():
        if last:
            own_ref[...] = acc_ref[pl.ds(0, TOK), :] * F_STUDENT
            for distance in range(1, SPAN):
                sent_refs[distance - 1][...] = (
                    acc_ref[pl.ds(distance * TOK, TOK), :] * F_STUDENT
                ).astype(jnp.bfloat16)
        else:
            sum_out_ref[...] = acc_ref[...]


def query_kernel(g_ref, lrt_ref, up_ref, nope_out_ref, rope_out_ref):
    grads = (dot(lrt_ref[...], g_ref[...]) * F_STUDENT).astype(jnp.bfloat16)
    ropes = []
    for half in range(2):
        block = slice(half * TOK, (half + 1) * TOK)
        turned = dot(up_ref[half], grads[:LATENT, block])
        nope_out_ref[:, block] = turned.T.astype(jnp.bfloat16)
        ropes.append(grads[LATENT + half * ROPE : LATENT + (half + 1) * ROPE, block])
    rope_out_ref[...] = jnp.concatenate(ropes, axis=0).astype(jnp.float32).T.astype(jnp.bfloat16)


def shape(*dims, dtype=jnp.bfloat16):
    return jax.ShapeDtypeStruct(dims, dtype)


SMEM = pl.BlockSpec(memory_space=pltpu.SMEM)
ANY = pl.BlockSpec(memory_space=pl.ANY)


def whole(*dims):
    return pl.BlockSpec(dims, lambda i: (0,) * len(dims))


def params():
    return pltpu.CompilerParams(
        dimension_semantics=("arbitrary",), vmem_limit_bytes=VMEM_LIMIT
    )


def student_call(scalars, valid_len, nope, rope, up_weight, kl_weight, sources):
    return pl.pallas_call(
        student_kernel,
        grid=(PAIRS,),
        in_specs=[
            SMEM,
            SMEM,
            pl.BlockSpec((TOK, 2 * HEAD), lambda i: (0, i)),
            pl.BlockSpec((TOK, 2 * ROPE), lambda i: (0, i)),
            pl.BlockSpec((2, HEAD, LATENT), lambda i: (i, 0, 0)),
            whole(TOK, HEADS),
        ]
        + [ANY] * 7,
        out_specs=[
            pl.BlockSpec((2 * TOK, WIDE), lambda i: (i, 0)),
            pl.BlockSpec((KEYS, 2 * TOK), lambda i: (0, i)),
            whole(KEYS, TOK),
            whole(HEADS, TOK),
            whole(KEYS, WIDE),
            whole(WIDE, KEYS),
        ],
        out_shape=[
            shape(HEADS * TOK, WIDE),
            shape(KEYS, HEADS * TOK, dtype=jnp.float32),
            shape(KEYS, TOK, dtype=jnp.float32),
            shape(HEADS, TOK, dtype=jnp.float32),
            shape(KEYS, WIDE),
            shape(WIDE, KEYS),
        ],
        scratch_shapes=[pltpu.SemaphoreType.DMA((SPAN,))],
        compiler_params=params(),
        cost_estimate=pl.CostEstimate(
            flops=2 * HEADS * TOK * (HEAD * LATENT + KEYS * WIDE),
            bytes_accessed=12_000_000,
            transcendentals=HEADS * TOK * KEYS,
        ),
    )(scalars, valid_len, nope, rope, up_weight, kl_weight, *sources)


def teacher_call(first, pairs, last, scalars, sources, teacher_query, p, bias, coeff, mixed, summed=None):
    outs = [(pl.BlockSpec((KEYS, 2 * TOK), lambda i: (0, i)), shape(KEYS, pairs * 2 * TOK))]
    if last:
        outs.append((whole(TOK, WIDE), shape(TOK, WIDE, dtype=jnp.float32)))
        outs += [(whole(TOK, WIDE), shape(TOK, WIDE))] * 3
    else:
        outs.append((whole(KEYS, WIDE), shape(KEYS, WIDE, dtype=jnp.float32)))
    return pl.pallas_call(
        functools.partial(teacher_kernel, first, pairs, last),
        grid=(pairs,),
        in_specs=[SMEM]
        + [ANY] * 7
        + [
            pl.BlockSpec((TOK, 2 * HEAD), lambda i: (0, first + i)),
            pl.BlockSpec((KEYS, 2 * TOK), lambda i: (0, first + i)),
            whole(KEYS, TOK),
            whole(HEADS, TOK),
            pl.BlockSpec((2 * TOK, WIDE), lambda i: (first + i, 0)),
        ]
        + ([whole(KEYS, WIDE)] if last else []),
        out_specs=[spec for spec, _ in outs],
        out_shape=[form for _, form in outs],
        scratch_shapes=[
            pltpu.VMEM((KEYS, WIDE), jnp.float32),
            pltpu.VMEM((pairs, KEYS, 2 * HEAD), jnp.bfloat16),
            pltpu.VMEM((2 * TOK, 2 * HEAD), jnp.bfloat16),
            pltpu.SemaphoreType.DMA((pairs, SPAN)),
        ],
        compiler_params=params(),
        cost_estimate=pl.CostEstimate(
            flops=4 * pairs * TOK * KEYS * (2 * HEAD + WIDE),
            bytes_accessed=pairs * 1_500_000,
            transcendentals=2 * pairs * TOK * KEYS,
        ),
    )(scalars, *sources, teacher_query, p, bias, coeff, mixed, *([summed] if last else []))


def query_call(first, pairs, g, lrt, up_weight):
    return pl.pallas_call(
        query_kernel,
        grid=(pairs,),
        in_specs=[
            pl.BlockSpec((KEYS, 2 * TOK), lambda i: (0, i)),
            whole(WIDE, KEYS),
            pl.BlockSpec((2, HEAD, LATENT), lambda i: (first + i, 0, 0)),
        ],
        out_specs=[
            pl.BlockSpec((TOK, 2 * HEAD), lambda i: (0, i)),
            pl.BlockSpec((TOK, 2 * ROPE), lambda i: (0, i)),
        ],
        out_shape=[shape(TOK, pairs * 2 * HEAD), shape(TOK, pairs * 2 * ROPE)],
        compiler_params=params(),
        cost_estimate=pl.CostEstimate(
            flops=4 * pairs * TOK * LATENT * (WIDE + HEAD),
            bytes_accessed=pairs * 800_000,
            transcendentals=0,
        ),
    )(g, lrt, up_weight)


def on_device(
    query_nope,
    query_rope,
    latent,
    key_rope,
    teacher_query,
    teacher_key,
    up_weight,
    kl_weight,
    key_back,
    valid_len,
):
    position = lax.axis_index(AXES)
    place = position % RING
    scalars = jnp.stack([position.astype(jnp.int32), key_back[0]])

    cut = FIRST * 2 * HEAD
    rows = jnp.concatenate([latent, key_rope, key_rope], axis=1)
    own = jnp.concatenate([teacher_key, rows], axis=1)
    parts = (jnp.concatenate([teacher_key[:, :cut], rows], axis=1), teacher_key[:, cut:])

    rotated = [permute(part, along_x(-1, (0, 1, 2, 3))) for part in parts]
    own1 = permute(own, along_x(1, (0, 1, 2)))
    own2 = permute(own, along_x(2, (0, 1)))
    chunks = []
    earlier = None
    for part, turned in zip(parts, rotated):
        leaving = jnp.where(place == RING - 1, part, turned)
        if earlier is not None:
            leaving = lax.optimization_barrier((leaving, earlier))[0]
        crossed = permute(leaving, next_run)
        back = permute(crossed, along_x(-1, (1, 2)))
        around = permute(crossed, along_x(1, (3,)))
        chunks.append((own, own1, own2, turned, crossed, back, around))
        earlier = crossed

    mixed, p, bias, coeff, _, lrt = student_call(
        scalars, valid_len, query_nope, query_rope, up_weight, kl_weight, chunks[0]
    )
    g0, summed = teacher_call(
        0, FIRST, False, scalars, chunks[0], teacher_query, p, bias, coeff, mixed
    )
    g1, kept, *sent = teacher_call(
        FIRST, PAIRS - FIRST, True, scalars, chunks[1], teacher_query, p, bias, coeff, mixed, summed
    )
    nope0, rope0 = query_call(0, FIRST, g0, lrt, up_weight)
    nope1, rope1 = query_call(FIRST, PAIRS - FIRST, g1, lrt, up_weight)

    total = kept
    for distance in range(1, SPAN):
        total = total + lax.ppermute(
            sent[distance - 1],
            AXES,
            [(b, b - distance) for b in range(distance, lax.axis_size(AXES))],
        ).astype(jnp.float32)
    d_latent = total[:, :LATENT]
    d_key_rope = total[:, LATENT : LATENT + ROPE] + total[:, LATENT + ROPE :]
    return (
        jnp.concatenate([nope0, nope1], axis=1),
        jnp.concatenate([rope0, rope1], axis=1),
        d_latent,
        d_key_rope,
    )


def solution(mesh):
    split = P(AXES, None)
    return jax.shard_map(
        on_device,
        mesh=mesh,
        in_specs=(split,) * 6 + (P(), split, P(AXES), P()),
        out_specs=(split,) * 4,
        check_vma=False,
    )
```

time: 212 us -> 152 us (0.72)
  the two profiles are of different devices: /device:TPU:74 before, /device:TPU:195 now
where the time goes in v1:
time: 152 us; the launch traced here: 151 us
  starting transfers between devices  66.4 us (44%)
  waiting for transfers between devices  38.8 us (26%)
  Pallas kernels  30.2 us (20%)
  local copies, waits for them, and re-layouts  11.2 us (7%)
  other arithmetic  2.98 us (2%)
  between operations  1.61 us (1%)
    ppermute x10, starting transfers between devices, permute(): return lax.ppermute(value, AXES, route(lax.axis_size(AXES)))  52.7 us
    ppermute x10, waiting for transfers between devices, permute(): return lax.ppermute(value, AXES, route(lax.axis_size(AXES)))  23 us
    ppermute x3, waiting for transfers between devices, on_device(): lax.ppermute(sent[distance - 1], AXES, [(b, b - distance) for b in range(...  15.8 us
    pallas_call x2, Pallas kernels, teacher_call(): pl.pallas_call(functools.partial(teacher_kernel, first, pairs, last), gri...  15 us
    ppermute x3, starting transfers between devices, on_device(): lax.ppermute(sent[distance - 1], AXES, [(b, b - distance) for b in range(...  13.8 us
    pallas_call x1, Pallas kernels, student_call(): pl.pallas_call(student_kernel, grid=(PAIRS,), in_specs=[SMEM, SMEM, pl.Bl...  9.46 us
    unnamed x25, local copies, waits for them, and re-layouts  6.53 us
    pallas_call x2, Pallas kernels, query_call(): pl.pallas_call(query_kernel, grid=(pairs,), in_specs=[pl.BlockSpec((KEYS,...  5.73 us
  transfers between devices with their start and end apart: 13, of which 5 were waited for; matrix products, arithmetic and copies ran while one was open for 4% of the time, Pallas kernels for 12%

profile of v1, /device:TPU:195, one launch (start us, length us, event | category | flops | bytes accessed | tf_op | source)
XLA Modules:
  0.0 151.2 jit_solution(14672168893996158609)
XLA Ops:
  0.6 0.0 copy-start.9
  0.6 0.9 copy.14
  1.5 1.0 slice.15
  2.5 1.0 concatenate.16
  3.5 0.0 copy-start.10
  3.5 0.0 copy-start.8
  3.5 2.2 %collective-permute-start.2 = (bf16[128,1408]{1,0:T(8,128)(2,1)S(1)}, bf16[128,1408]{1,0:T(8,128)(2,1)S(1)}, u32[]{:S(2)}, u32[]{:S(2)}) collective-permute-start(bf16[128,1408]{1,0:T(8,128)(2,1)S(1)} %concatenate.16), channel_id=1, source_target_pairs={{0,3},{1,0},{2,1},{3,2},{4,7},{5,4},{6,5},{7,6},{8,11},{9,8},{10,9... | collective-permute-start | bytes 1081352 | tf_op jit(solution)/shard_map/ppermute | solution.py:50
  5.7 1.2 concatenate.15.refs_0_
  6.9 4.1 %collective-permute-start.1 = (bf16[128,2688]{1,0:T(8,128)(2,1)S(1)}, bf16[128,2688]{1,0:T(8,128)(2,1)S(1)}, u32[]{:S(2)}, u32[]{:S(2)}) collective-permute-start(bf16[128,2688]{1,0:T(8,128)(2,1)S(1)} %concatenate.15.refs_0_), channel_id=1, source_target_pairs={{0,2},{1,3},{4,6},{5,7},{8,10},{9,11},{12,14},{13,15},{16,18},{17,... | collective-permute-start | bytes 2064392 | tf_op jit(solution)/shard_map/ppermute | solution.py:50
  11.0 1.9 %collective-permute-start = (bf16[128,2688]{1,0:T(8,128)(2,1)S(1)}, bf16[128,2688]{1,0:T(8,128)(2,1)S(1)}, u32[]{:S(2)}, u32[]{:S(2)}) collective-permute-start(bf16[128,2688]{1,0:T(8,128)(2,1)S(1)} %concatenate.15.refs_0_), channel_id=1, source_target_pairs={{0,1},{1,2},{2,3},{4,5},{5,6},{6,7},{8,9},{9,10},{10,11},{12,13},{... | collective-permute-start | bytes 2064392 | tf_op jit(solution)/shard_map/ppermute | solution.py:50
  12.9 0.8 slice.16
  13.7 3.4 %collective-permute-start.6 = (bf16[128,1280]{1,0:T(8,128)(2,1)}, bf16[128,1280]{1,0:T(8,128)(2,1)S(1)}, u32[]{:S(2)}, u32[]{:S(2)}) collective-permute-start(bf16[128,1280]{1,0:T(8,128)(2,1)} %slice.16), channel_id=1, source_target_pairs={{0,3},{1,0},{2,1},{3,2},{4,7},{5,4},{6,5},{7,6},{8,11},{9,8},{10,9... | collective-permute-start | bytes 983048 | tf_op jit(solution)/shard_map/ppermute | solution.py:50
  17.1 0.0 collective-permute-done.2.refs_3_
  17.1 7.9 %collective-permute-start.3 = (bf16[128,1408]{1,0:T(8,128)(2,1)S(1)}, bf16[128,1408]{1,0:T(8,128)(2,1)S(1)}, u32[]{:S(2)}, u32[]{:S(2)}) collective-permute-start(bf16[128,1408]{1,0:T(8,128)(2,1)S(1)} %broadcast_select_fusion), channel_id=1, source_target_pairs={{0,4},{1,5},{2,6},{3,7},{4,8},{5,9},{6,10},{7,11},{8,12},{9,13},{1... | collective-permute-start | bytes 1081352 | tf_op jit(solution)/shard_map/ppermute | solution.py:50
  25.1 9.6 %collective-permute-done.6.refs_3_ = bf16[128,1280]{1,0:T(8,128)(2,1)S(1)} collective-permute-done((bf16[128,1280]{1,0:T(8,128)(2,1)}, bf16[128,1280]{1,0:T(8,128)(2,1)S(1)}, u32[]{:S(2)}, u32[]{:S(2)}) %collective-permute-start.6) | collective-permute-done | bytes 327712 | tf_op jit(solution)/shard_map/ppermute | solution.py:50
  34.7 1.1 broadcast_select_fusion.1
  35.8 9.2 %collective-permute-done.3.refs_4_ = bf16[128,1408]{1,0:T(8,128)(2,1)S(1)} collective-permute-done((bf16[128,1408]{1,0:T(8,128)(2,1)S(1)}, bf16[128,1408]{1,0:T(8,128)(2,1)S(1)}, u32[]{:S(2)}, u32[]{:S(2)}) %collective-permute-start.3) | collective-permute-done | bytes 360480 | tf_op jit(solution)/shard_map/ppermute | solution.py:50
  45.0 7.2 %collective-permute-start.7 = (bf16[128,1280]{1,0:T(8,128)(2,1)S(1)}, bf16[128,1280]{1,0:T(8,128)(2,1)}, u32[]{:S(2)}, u32[]{:S(2)}) collective-permute-start(bf16[128,1280]{1,0:T(8,128)(2,1)S(1)} %broadcast_select_fusion.1), channel_id=1, source_target_pairs={{0,4},{1,5},{2,6},{3,7},{4,8},{5,9},{6,10},{7,11},{8,12},{9,13},{1... | collective-permute-start | bytes 983048 | tf_op jit(solution)/shard_map/ppermute | solution.py:50
  52.2 0.7 collective-permute-start.5
  52.9 9.8 %collective-permute-start.4 = (bf16[128,1408]{1,0:T(8,128)(2,1)S(1)}, bf16[128,1408]{1,0:T(8,128)(2,1)S(1)}, u32[]{:S(2)}, u32[]{:S(2)}) collective-permute-start(bf16[128,1408]{1,0:T(8,128)(2,1)S(1)} %collective-permute-done.3.refs_4_), channel_id=1, source_target_pairs={{1,0},{2,1},{5,4},{6,5},{9,8},{10,9},{13,12},{14,13},{17,16},{18,1... | collective-permute-start | bytes 1081352 | tf_op jit(solution)/shard_map/ppermute | solution.py:50
  63.4 4.2 %collective-permute-done.7.refs_4_ = bf16[128,1280]{1,0:T(8,128)(2,1)} collective-permute-done((bf16[128,1280]{1,0:T(8,128)(2,1)S(1)}, bf16[128,1280]{1,0:T(8,128)(2,1)}, u32[]{:S(2)}, u32[]{:S(2)}) %collective-permute-start.7) | collective-permute-done | bytes 327712 | tf_op jit(solution)/shard_map/ppermute | solution.py:50
  67.6 1.4 collective-permute-start.9
  69.0 14.1 %collective-permute-start.8 = (bf16[128,1280]{1,0:T(8,128)(2,1)}, bf16[128,1280]{1,0:T(8,128)(2,1)}, u32[]{:S(2)}, u32[]{:S(2)}) collective-permute-start(bf16[128,1280]{1,0:T(8,128)(2,1)} %collective-permute-done.7.refs_4_), channel_id=1, source_target_pairs={{1,0},{2,1},{5,4},{6,5},{9,8},{10,9},{13,12},{14,13},{17,16},{18,1... | collective-permute-start | bytes 983048 | tf_op jit(solution)/shard_map/ppermute | solution.py:50
  83.0 0.1 pad_add_fusion.scalar_ref
  83.1 0.7 copy.18.kl_ref
  83.9 0.0 copy-start.5
  83.9 1.1 copy-done.5
  85.0 0.8 copy-done.6
  85.8 0.9 copy-done.7
  86.8 9.5 %shard_map.129 = (bf16[2048,640]{1,0:T(8,128)(2,1)}, f32[512,2048]{1,0:T(8,128)}, f32[512,128]{1,0:T(8,128)S(1)}, f32[16,128]{1,0:T(8,128)S(1)}, bf16[512,640]{1,0:T(8,128)(2,1)}, /*index=5*/bf16[640,512]{1,0:T(8,128)(2,1)S(1)}) custom-call(s32[2]{0:T(128)S(1)} %pad_add_fusion.scalar_ref, s32[512]{0:T(512)S(1)} %copy-done.8, ...), custom_call_target="tpu_custom_call" | custom-call | flops 1610612736 | bytes 12000000 | tf_op jit(solution)/shard_map/pallas_call | solution.py:210
  96.3 0.0 copy-start
  96.3 6.0 %shard_map.130 = (bf16[512,768]{1,0:T(8,128)(2,1)S(1)}, f32[512,640]{1,0:T(8,128)}) custom-call(s32[2]{0:T(128)S(1)} %pad_add_fusion.scalar_ref, bf16[128,2688]{1,0:T(8,128)(2,1)S(1)} %concatenate.15.refs_0_, bf16[128,2688]{1,0:T(8,128)(2,1)S(1)} %collective-permute-done.refs_1_, bf16[128,2688]{1,0:T(8,128)(2,1)S(1)} %collective-permute-done.1.refs_2_, ...), custom_call_target="tpu_custom_call" | custom-call | flops 704643072 | bytes 4500000 | tf_op jit(solution)/shard_map/pallas_call | solution.py:255
  102.2 0.0 copy-start.3
  102.3 2.2 %shard_map.131 = (bf16[128,768]{1,0:T(8,128)(2,1)S(1)}, bf16[128,384]{1,0:T(8,128)(2,1)S(1)}) custom-call(bf16[512,768]{1,0:T(8,128)(2,1)S(1)} %get-tuple-element.25.g_ref, bf16[640,512]{1,0:T(8,128)(2,1)S(1)} %get-tuple-element.26.lrt_ref, bf16[16,128,512]{2,1,0:T(8,128)(2,1)S(1)} %copy-done), custom_call_target="tpu_custom_call" | custom-call | flops 603979776 | bytes 2400000 | tf_op jit(solution)/shard_map/pallas_call | solution.py:286
  104.5 9.0 %shard_map.132 = (bf16[512,1280]{1,0:T(8,128)(2,1)}, f32[128,640]{1,0:T(8,128)S(1)}, bf16[128,640]{1,0:T(8,128)(2,1)S(1)}, bf16[128,640]{1,0:T(8,128)(2,1)S(1)}, bf16[128,640]{1,0:T(8,128)(2,1)S(1)}) custom-call(s32[2]{0:T(128)S(1)} %pad_add_fusion.scalar_ref, bf16[128,2688]{1,0:T(8,128)(2,1)S(1)} %concatenate.15.refs_0_, ...), custom_call_target="tpu_custom_call" | custom-call | flops 1174405120 | bytes 7500000 | tf_op jit(solution)/shard_map/pallas_call | solution.py:255
  113.5 1.3 copy-done.4
  114.8 3.6 %shard_map.133 = (bf16[128,1280]{1,0:T(8,128)(2,1)S(1)}, bf16[128,640]{1,0:T(8,128)(2,1)S(1)}) custom-call(bf16[512,1280]{1,0:T(8,128)(2,1)S(1)} %copy-done.4, bf16[640,512]{1,0:T(8,128)(2,1)S(1)} %get-tuple-element.26.lrt_ref, bf16[16,128,512]{2,1,0:T(8,128)(2,1)S(1)} %copy-done), custom_call_target="tpu_custom_call" | custom-call | flops 1006632960 | bytes 4000000 | tf_op jit(solution)/shard_map/pallas_call | solution.py:286
  118.4 1.9 %collective-permute-start.10 = (bf16[128,640]{1,0:T(8,128)(2,1)S(1)}, bf16[128,640]{1,0:T(8,128)(2,1)S(1)}, u32[]{:S(2)}, u32[]{:S(2)}) collective-permute-start(bf16[128,640]{1,0:T(8,128)(2,1)S(1)} %get-tuple-element.35), channel_id=1, source_target_pairs={{1,0},{2,1},{3,2},{4,3},{5,4},{6,5},{7,6},{8,7},{9,8},{10,9},{11,1... | collective-permute-start | bytes 491528 | tf_op jit(solution)/shard_map/ppermute | solution.py:358
  120.3 8.5 %collective-permute-start.11 = (bf16[128,640]{1,0:T(8,128)(2,1)S(1)}, bf16[128,640]{1,0:T(8,128)(2,1)S(1)}, u32[]{:S(2)}, u32[]{:S(2)}) collective-permute-start(bf16[128,640]{1,0:T(8,128)(2,1)S(1)} %get-tuple-element.36), channel_id=1, source_target_pairs={{2,0},{3,1},{4,2},{5,3},{6,4},{7,5},{8,6},{9,7},{10,8},{11,9},{12,... | collective-permute-start | bytes 491528 | tf_op jit(solution)/shard_map/ppermute | solution.py:358
  128.8 3.4 %collective-permute-start.12 = (bf16[128,640]{1,0:T(8,128)(2,1)S(1)}, bf16[128,640]{1,0:T(8,128)(2,1)S(1)}, u32[]{:S(2)}, u32[]{:S(2)}) collective-permute-start(bf16[128,640]{1,0:T(8,128)(2,1)S(1)} %get-tuple-element.37), channel_id=1, source_target_pairs={{3,0},{4,1},{5,2},{6,3},{7,4},{8,5},{9,6},{10,7},{11,8},{12,9},{13... | collective-permute-start | bytes 491528 | tf_op jit(solution)/shard_map/ppermute | solution.py:358
  132.2 0.8 pad_maximum_fusion
  133.0 0.7 pad_maximum_fusion.1
  133.8 4.0 %collective-permute-done.11 = bf16[128,640]{1,0:T(8,128)(2,1)S(1)} collective-permute-done((bf16[128,640]{1,0:T(8,128)(2,1)S(1)}, bf16[128,640]{1,0:T(8,128)(2,1)S(1)}, u32[]{:S(2)}, u32[]{:S(2)}) %collective-permute-start.11) | collective-permute-done | bytes 163872 | tf_op jit(solution)/shard_map/ppermute | solution.py:358
  137.7 11.9 %collective-permute-done.12 = bf16[128,640]{1,0:T(8,128)(2,1)S(1)} collective-permute-done((bf16[128,640]{1,0:T(8,128)(2,1)S(1)}, bf16[128,640]{1,0:T(8,128)(2,1)S(1)}, u32[]{:S(2)}, u32[]{:S(2)}) %collective-permute-start.12) | collective-permute-done | bytes 163872 | tf_op jit(solution)/shard_map/ppermute | solution.py:358
  149.6 0.1 convert_add_fusion
  149.6 0.1 slice_add_fusion
  149.7 0.7 slice.20
  150.5 0.7 copy.19
  (20 shorter events, 0.1 us)
Async XLA Ops:
  0.6 12.3 %copy-start.9 = (bf16[128,2048]{1,0:T(8,128)(2,1)S(1)}, bf16[128,2048]{1,0:T(8,128)(2,1)}, u32[]{:S(2)}) copy-start(bf16[128,2048]{1,0:T(8,128)(2,1)} %param.15) | copy-start | bytes 1572868
  3.5 79.6 %copy-start.10 = (f32[128,16]{0,1:T(8,128)S(1)}, f32[128,16]{0,1:T(8,128)}, u32[]{:S(2)}) copy-start(f32[128,16]{0,1:T(8,128)} %param.17) | copy-start | bytes 24580
  3.5 80.4 %copy-start.8 = (s32[512]{0:T(512)S(1)}, s32[512]{0:T(512)}, u32[]{:S(2)}) copy-start(s32[512]{0:T(512)} %length_ref.1) | copy-start | bytes 6148
  3.5 13.6 %collective-permute-start.2 = (bf16[128,1408]{1,0:T(8,128)(2,1)S(1)}, bf16[128,1408]{1,0:T(8,128)(2,1)S(1)}, u32[]{:S(2)}, u32[]{:S(2)}) collective-permute-start(bf16[128,1408]{1,0:T(8,128)(2,1)S(1)} %concatenate.16), channel_id=1, source_target_pairs={{0,3},{1,0},{2,1},{3,2},{4,7},{5,4},{6,5},{7,6},{8,11},{9,8},{10,9... | collective-permute-start | bytes 1081352 | tf_op jit(solution)/shard_map/ppermute | solution.py:50
  6.9 62.1 %collective-permute-start.1 = (bf16[128,2688]{1,0:T(8,128)(2,1)S(1)}, bf16[128,2688]{1,0:T(8,128)(2,1)S(1)}, u32[]{:S(2)}, u32[]{:S(2)}) collective-permute-start(bf16[128,2688]{1,0:T(8,128)(2,1)S(1)} %concatenate.15.refs_0_), channel_id=1, source_target_pairs={{0,2},{1,3},{4,6},{5,7},{8,10},{9,11},{12,14},{13,15},{16,18},{17,... | collective-permute-start | bytes 2064392 | tf_op jit(solution)/shard_map/ppermute | solution.py:50
  11.0 72.9 %collective-permute-start = (bf16[128,2688]{1,0:T(8,128)(2,1)S(1)}, bf16[128,2688]{1,0:T(8,128)(2,1)S(1)}, u32[]{:S(2)}, u32[]{:S(2)}) collective-permute-start(bf16[128,2688]{1,0:T(8,128)(2,1)S(1)} %concatenate.15.refs_0_), channel_id=1, source_target_pairs={{0,1},{1,2},{2,3},{4,5},{5,6},{6,7},{8,9},{9,10},{10,11},{12,13},{... | collective-permute-start | bytes 2064392 | tf_op jit(solution)/shard_map/ppermute | solution.py:50
  13.7 21.0 %collective-permute-start.6 = (bf16[128,1280]{1,0:T(8,128)(2,1)}, bf16[128,1280]{1,0:T(8,128)(2,1)S(1)}, u32[]{:S(2)}, u32[]{:S(2)}) collective-permute-start(bf16[128,1280]{1,0:T(8,128)(2,1)} %slice.16), channel_id=1, source_target_pairs={{0,3},{1,0},{2,1},{3,2},{4,7},{5,4},{6,5},{7,6},{8,11},{9,8},{10,9... | collective-permute-start | bytes 983048 | tf_op jit(solution)/shard_map/ppermute | solution.py:50
  17.1 27.9 %collective-permute-start.3 = (bf16[128,1408]{1,0:T(8,128)(2,1)S(1)}, bf16[128,1408]{1,0:T(8,128)(2,1)S(1)}, u32[]{:S(2)}, u32[]{:S(2)}) collective-permute-start(bf16[128,1408]{1,0:T(8,128)(2,1)S(1)} %broadcast_select_fusion), channel_id=1, source_target_pairs={{0,4},{1,5},{2,6},{3,7},{4,8},{5,9},{6,10},{7,11},{8,12},{9,13},{1... | collective-permute-start | bytes 1081352 | tf_op jit(solution)/shard_map/ppermute | solution.py:50
  34.7 10.3 %copy-start.2 = (bf16[128,1280]{1,0:T(8,128)(2,1)}, bf16[128,1280]{1,0:T(8,128)(2,1)S(1)}, u32[]{:S(2)}) copy-start(bf16[128,1280]{1,0:T(8,128)(2,1)S(1)} %collective-permute-done.6.refs_3_) | copy-start | bytes 983044
  45.0 22.6 %collective-permute-start.7 = (bf16[128,1280]{1,0:T(8,128)(2,1)S(1)}, bf16[128,1280]{1,0:T(8,128)(2,1)}, u32[]{:S(2)}, u32[]{:S(2)}) collective-permute-start(bf16[128,1280]{1,0:T(8,128)(2,1)S(1)} %broadcast_select_fusion.1), channel_id=1, source_target_pairs={{0,4},{1,5},{2,6},{3,7},{4,8},{5,9},{6,10},{7,11},{8,12},{9,13},{1... | collective-permute-start | bytes 983048 | tf_op jit(solution)/shard_map/ppermute | solution.py:50
  52.2 31.7 %collective-permute-start.5 = (bf16[128,1408]{1,0:T(8,128)(2,1)S(1)}, bf16[128,1408]{1,0:T(8,128)(2,1)S(1)}, u32[]{:S(2)}, u32[]{:S(2)}) collective-permute-start(bf16[128,1408]{1,0:T(8,128)(2,1)S(1)} %collective-permute-done.3.refs_4_), channel_id=1, source_target_pairs={{3,0},{7,4},{11,8},{15,12},{19,16},{23,20},{27,24},{31,28},{35,32}... | collective-permute-start | bytes 1081352 | tf_op jit(solution)/shard_map/ppermute | solution.py:50
  52.9 31.0 %collective-permute-start.4 = (bf16[128,1408]{1,0:T(8,128)(2,1)S(1)}, bf16[128,1408]{1,0:T(8,128)(2,1)S(1)}, u32[]{:S(2)}, u32[]{:S(2)}) collective-permute-start(bf16[128,1408]{1,0:T(8,128)(2,1)S(1)} %collective-permute-done.3.refs_4_), channel_id=1, source_target_pairs={{1,0},{2,1},{5,4},{6,5},{9,8},{10,9},{13,12},{14,13},{17,16},{18,1... | collective-permute-start | bytes 1081352 | tf_op jit(solution)/shard_map/ppermute | solution.py:50
  67.6 36.9 %collective-permute-start.9 = (bf16[128,1280]{1,0:T(8,128)(2,1)}, bf16[128,1280]{1,0:T(8,128)(2,1)}, u32[]{:S(2)}, u32[]{:S(2)}) collective-permute-start(bf16[128,1280]{1,0:T(8,128)(2,1)} %collective-permute-done.7.refs_4_), channel_id=1, source_target_pairs={{3,0},{7,4},{11,8},{15,12},{19,16},{23,20},{27,24},{31,28},{35,32}... | collective-permute-start | bytes 983048 | tf_op jit(solution)/shard_map/ppermute | solution.py:50
  69.0 35.5 %collective-permute-start.8 = (bf16[128,1280]{1,0:T(8,128)(2,1)}, bf16[128,1280]{1,0:T(8,128)(2,1)}, u32[]{:S(2)}, u32[]{:S(2)}) collective-permute-start(bf16[128,1280]{1,0:T(8,128)(2,1)} %collective-permute-done.7.refs_4_), channel_id=1, source_target_pairs={{1,0},{2,1},{5,4},{6,5},{9,8},{10,9},{13,12},{14,13},{17,16},{18,1... | collective-permute-start | bytes 983048 | tf_op jit(solution)/shard_map/ppermute | solution.py:50
  83.9 12.4 %copy-start.1 = (bf16[128,2048]{1,0:T(8,128)(2,1)S(1)}, bf16[128,2048]{1,0:T(8,128)(2,1)}, u32[]{:S(2)}) copy-start(bf16[128,2048]{1,0:T(8,128)(2,1)} %refs_7_.3) | copy-start | bytes 1572868
  83.9 1.1 copy-start.5
  85.0 0.8 copy-start.6
  85.8 0.9 copy-start.7
  96.3 6.0 %copy-start = (bf16[16,128,512]{2,1,0:T(8,128)(2,1)S(1)}, bf16[16,128,512]{2,1,0:T(8,128)(2,1)}, u32[]{:S(2)}) copy-start(bf16[16,128,512]{2,1,0:T(8,128)(2,1)} %up_ref.5) | copy-start | bytes 6291460
  102.2 2.2 %copy-start.3 = (bf16[128,1280]{1,0:T(8,128)(2,1)S(1)}, bf16[128,1280]{1,0:T(8,128)(2,1)}, u32[]{:S(2)}) copy-start(bf16[128,1280]{1,0:T(8,128)(2,1)} %copy-done.2) | copy-start | bytes 983044
  113.5 1.3 copy-start.4
  118.4 15.4 %collective-permute-start.10 = (bf16[128,640]{1,0:T(8,128)(2,1)S(1)}, bf16[128,640]{1,0:T(8,128)(2,1)S(1)}, u32[]{:S(2)}, u32[]{:S(2)}) collective-permute-start(bf16[128,640]{1,0:T(8,128)(2,1)S(1)} %get-tuple-element.35), channel_id=1, source_target_pairs={{1,0},{2,1},{3,2},{4,3},{5,4},{6,5},{7,6},{8,7},{9,8},{10,9},{11,1... | collective-permute-start | bytes 491528 | tf_op jit(solution)/shard_map/ppermute | solution.py:358
  120.3 17.4 %collective-permute-start.11 = (bf16[128,640]{1,0:T(8,128)(2,1)S(1)}, bf16[128,640]{1,0:T(8,128)(2,1)S(1)}, u32[]{:S(2)}, u32[]{:S(2)}) collective-permute-start(bf16[128,640]{1,0:T(8,128)(2,1)S(1)} %get-tuple-element.36), channel_id=1, source_target_pairs={{2,0},{3,1},{4,2},{5,3},{6,4},{7,5},{8,6},{9,7},{10,8},{11,9},{12,... | collective-permute-start | bytes 491528 | tf_op jit(solution)/shard_map/ppermute | solution.py:358
  128.8 20.8 %collective-permute-start.12 = (bf16[128,640]{1,0:T(8,128)(2,1)S(1)}, bf16[128,640]{1,0:T(8,128)(2,1)S(1)}, u32[]{:S(2)}, u32[]{:S(2)}) collective-permute-start(bf16[128,640]{1,0:T(8,128)(2,1)S(1)} %get-tuple-element.37), channel_id=1, source_target_pairs={{3,0},{4,1},{5,2},{6,3},{7,4},{8,5},{9,6},{10,7},{11,8},{12,9},{13... | collective-permute-start | bytes 491528 | tf_op jit(solution)/shard_map/ppermute | solution.py:358

commit v2 on v0

v2 whole, which is shorter than its diff:
```python
import functools
import math

import jax
import jax.numpy as jnp
from jax import lax
from jax.experimental import pallas as pl
from jax.experimental.pallas import tpu as pltpu
from jax.sharding import PartitionSpec as P

HEADS = 16
HEAD = 128
LATENT = 512
ROPE = 64
TOK = 128
SPAN = 4
KEYS = SPAN * TOK
WIDE = LATENT + 2 * ROPE
PAIRS = HEADS // 2
FIRST = 3
CUT = FIRST * 2 * HEAD
REST = HEADS * HEAD - CUT
RING = 4
AXES = ("outer", "inner")
F_STUDENT = 1.0 / math.sqrt(HEAD + ROPE)
F_TEACHER = 1.0 / math.sqrt(HEAD)
LOG2E = math.log2(math.e)
VMEM_LIMIT = 20 * 1024 * 1024

NN = (((1,), (0,)), ((), ()))
NT = (((1,), (1,)), ((), ()))


def dot(a, b, dims=NN):
    return lax.dot_general(a, b, dims, preferred_element_type=jnp.float32)


def along_x(step, sources):
    def route(count):
        return [
            (b, b - b % RING + (b + step) % RING) for b in range(count) if b % RING in sources
        ]

    return route


def next_run(count):
    return [(b, b + RING) for b in range(count - RING)]


def permute(value, route):
    return lax.ppermute(value, AXES, route(lax.axis_size(AXES)))


def softmax_parts(logits):
    powers = jnp.exp2(logits - jnp.max(logits, axis=0, keepdims=True))
    return powers, jnp.sum(powers, axis=0, keepdims=True)


def from_slots(place, sources, act):
    if len(sources) == SPAN:
        for distance in range(SPAN):
            act(distance, sources[distance])
        return
    own, own1, own2, rotated, crossed, back, around = sources
    act(0, own)
    for distance, here, earlier in ((1, own1, around), (2, own2, back), (3, rotated, crossed)):
        pl.when(place >= distance)(functools.partial(act, distance, here))
        pl.when(place < distance)(functools.partial(act, distance, earlier))


def pack_kernel(latent_ref, rope_ref, key_ref, first_ref, rest_ref, sems):
    copies = [
        pltpu.make_async_copy(key_ref.at[:, pl.ds(0, CUT)], first_ref.at[:, pl.ds(0, CUT)], sems.at[0]),
        pltpu.make_async_copy(latent_ref, first_ref.at[:, pl.ds(CUT, LATENT)], sems.at[1]),
        pltpu.make_async_copy(key_ref.at[:, pl.ds(CUT, REST)], rest_ref, sems.at[2]),
    ]
    for copy in copies:
        copy.start()
    rope = rope_ref[...].astype(jnp.float32)
    both = jnp.concatenate([rope, rope], axis=0).T.astype(jnp.bfloat16)
    first_ref[:, CUT + LATENT :] = both
    for copy in copies:
        copy.wait()


def absorb_kernel(nope_ref, rope_ref, up_ref, mixed_ref):
    lane = lax.broadcasted_iota(jnp.int32, (TOK, 2 * ROPE), 1)
    for head in range(HEADS):
        rows = slice(head * TOK, (head + 1) * TOK)
        absorbed = dot(nope_ref[:, head * HEAD : (head + 1) * HEAD], up_ref[head])
        mixed_ref[rows, :LATENT] = absorbed.astype(jnp.bfloat16)
        rope = rope_ref[:, (head // 2) * 2 * ROPE : (head // 2 + 1) * 2 * ROPE]
        kept = (lane < ROPE) if head % 2 == 0 else (lane >= ROPE)
        mixed_ref[rows, LATENT:] = jnp.where(kept, rope, jnp.zeros_like(rope))


def student_kernel(scalar_ref, length_ref, kl_ref, mixed_ref, *refs):
    sources, (p_ref, bias_ref, coeff_ref, lrt_ref, lr_ref, sems) = refs[:SPAN], refs[SPAN:]
    position = scalar_ref[0]
    place = position % RING

    def copy(distance, source):
        return pltpu.make_async_copy(
            source.at[:, pl.ds(CUT, WIDE)],
            lr_ref.at[pl.ds(distance * TOK, TOK)],
            sems.at[distance],
        )

    from_slots(place, sources, lambda distance, source: copy(distance, source).start())
    query = lax.broadcasted_iota(jnp.int32, (TOK, TOK), 1)
    key = lax.broadcasted_iota(jnp.int32, (TOK, TOK), 0)
    for distance in range(SPAN):
        length = length_ref[jnp.maximum(position - distance, 0)]
        length = jnp.where(distance <= scalar_ref[1], length, 0)
        allowed = key < length
        if distance == 0:
            allowed = allowed & (key <= query)
        bias_ref[distance * TOK : (distance + 1) * TOK, :] = jnp.where(allowed, 0.0, -1e30)
    live = lax.broadcasted_iota(jnp.int32, (HEADS, TOK), 1) < length_ref[position]
    coeff_ref[...] = jnp.where(live, kl_ref[...], 0.0)
    for distance in range(SPAN):
        copy(distance, sources[distance]).wait()
    for pair in range(PAIRS):
        logits = dot(lr_ref[...], mixed_ref[pair * 2 * TOK : (pair + 1) * 2 * TOK, :], NT)
        for half in range(2):
            head = 2 * pair + half
            powers, total = softmax_parts(
                logits[:, half * TOK : (half + 1) * TOK] * (F_STUDENT * LOG2E) + bias_ref[...]
            )
            weight = coeff_ref[head : head + 1, :]
            p_ref[:, head * TOK : (head + 1) * TOK] = powers * (weight / total)
    lrt_ref[...] = lr_ref[...].T


def teacher_kernel(first, pairs, start, scalar_ref, *refs):
    count = len(start)
    last = first > 0
    sources, refs = refs[:count], refs[count:]
    (query_ref, p_ref, bias_ref, coeff_ref, mixed_ref), refs = refs[:5], refs[5:]
    if last:
        sum_ref, g_ref, own_ref, *sent_refs = refs[:6]
    else:
        g_ref, sum_out_ref = refs[:2]
    keys_ref, diagonal_ref, sems = refs[-3:]
    place = scalar_ref[0] % RING
    columns = dict(zip(map(id, sources), start))

    def copy(pair, distance, source):
        return pltpu.make_async_copy(
            source.at[:, pl.ds(columns[id(source)] + pair * 2 * HEAD, 2 * HEAD)],
            keys_ref.at[pair, pl.ds(distance * TOK, TOK)],
            sems.at[pair, distance],
        )

    for pair in range(pairs):
        from_slots(
            place, sources, lambda distance, source, pair=pair: copy(pair, distance, source).start()
        )
    diagonal_ref[...] = jnp.zeros_like(diagonal_ref)
    for pair in range(pairs):
        for half in range(2):
            block = slice(half * HEAD, (half + 1) * HEAD)
            head = 2 * pair + half
            diagonal_ref[pair, block, block] = query_ref[:, (2 * first + head) * HEAD : (2 * first + head + 1) * HEAD]
    for pair in range(pairs):
        for distance in range(SPAN):
            copy(pair, distance, sources[distance]).wait()
    for pair in range(pairs):
        logits = dot(keys_ref[pair], diagonal_ref[pair], NT)
        for half in range(2):
            head = 2 * pair + half
            powers, total = softmax_parts(
                logits[:, half * TOK : (half + 1) * TOK] * (F_TEACHER * LOG2E) + bias_ref[...]
            )
            full = 2 * first + head
            weight = coeff_ref[full : full + 1, :]
            student = p_ref[:, full * TOK : (full + 1) * TOK]
            g_ref[:, head * TOK : (head + 1) * TOK] = (student - powers * (weight / total)).astype(jnp.bfloat16)
    summed = dot(g_ref[...], mixed_ref[2 * first * TOK : 2 * (first + pairs) * TOK, :])
    if last:
        summed = (summed + sum_ref[...]) * F_STUDENT
        own_ref[...] = summed[:TOK]
        for distance in range(1, SPAN):
            sent_refs[distance - 1][...] = summed[distance * TOK : (distance + 1) * TOK].astype(
                jnp.bfloat16
            )
    else:
        sum_out_ref[...] = summed


def query_kernel(counts, *refs):
    g_refs, (lrt_ref, up_ref, nope_out_ref, rope_out_ref) = refs[: len(counts)], refs[len(counts) :]
    head = 0
    for g_ref, pairs in zip(g_refs, counts):
        for pair in range(pairs):
            grads = dot(lrt_ref[...], g_ref[:, pair * 2 * TOK : (pair + 1) * 2 * TOK]) * F_STUDENT
            grads = grads.astype(jnp.bfloat16)
            ropes = []
            for half in range(2):
                block = slice(half * TOK, (half + 1) * TOK)
                turned = dot(up_ref[head + half], grads[:LATENT, block])
                nope_out_ref[:, (head + half) * HEAD : (head + half + 1) * HEAD] = turned.T.astype(
                    jnp.bfloat16
                )
                ropes.append(grads[LATENT + half * ROPE : LATENT + (half + 1) * ROPE, block])
            both = jnp.concatenate(ropes, axis=0).astype(jnp.float32).T.astype(jnp.bfloat16)
            rope_out_ref[:, head * ROPE : (head + 2) * ROPE] = both
            head += 2


def shape(*dims, dtype=jnp.bfloat16):
    return jax.ShapeDtypeStruct(dims, dtype)


SMEM = pl.BlockSpec(memory_space=pltpu.SMEM)
ANY = pl.BlockSpec(memory_space=pl.ANY)
VMEM = pl.BlockSpec(memory_space=pltpu.VMEM)


def call(kernel, ins, outs, scratch, flops, accessed, exps=0, kept=True):
    return pl.pallas_call(
        kernel,
        in_specs=ins,
        out_specs=[VMEM] * len(outs),
        out_shape=[pltpu.VMEM(form.shape, form.dtype) for form in outs] if kept else outs,
        scratch_shapes=scratch,
        compiler_params=pltpu.CompilerParams(vmem_limit_bytes=VMEM_LIMIT),
        cost_estimate=pl.CostEstimate(flops=flops, bytes_accessed=accessed, transcendentals=exps),
    )


def finish_kernel(kept_ref, one_ref, two_ref, three_ref, latent_ref, rope_ref):
    total = kept_ref[...]
    for ref in (one_ref, two_ref, three_ref):
        total = total + ref[...].astype(jnp.float32)
    latent_ref[...] = total[:, :LATENT]
    turned = total[:, LATENT:].T
    rope_ref[...] = turned[:ROPE] + turned[ROPE:]


def pack_call(latent, key_rope, teacher_key):
    return call(
        pack_kernel,
        [ANY, VMEM, ANY],
        [shape(TOK, CUT + WIDE), shape(TOK, REST)],
        [pltpu.SemaphoreType.DMA((3,))],
        0,
        2_000_000,
    )(latent, key_rope.T, teacher_key)


def absorb_call(nope, rope, up_weight):
    return call(
        absorb_kernel,
        [VMEM] * 3,
        [shape(HEADS * TOK, WIDE)],
        [],
        2 * HEADS * TOK * HEAD * LATENT,
        6_000_000,
    )(nope, rope, up_weight)[0]


def student_call(scalars, valid_len, kl_weight, mixed, sources):
    return call(
        student_kernel,
        [SMEM, SMEM, VMEM, VMEM] + [ANY] * SPAN,
        [
            shape(KEYS, HEADS * TOK, dtype=jnp.float32),
            shape(KEYS, TOK, dtype=jnp.float32),
            shape(HEADS, TOK, dtype=jnp.float32),
            shape(WIDE, KEYS),
        ],
        [pltpu.VMEM((KEYS, WIDE), jnp.bfloat16), pltpu.SemaphoreType.DMA((SPAN,))],
        2 * HEADS * TOK * KEYS * WIDE,
        8_000_000,
        HEADS * TOK * KEYS,
    )(scalars, valid_len, kl_weight.T, mixed, *sources)


def teacher_call(first, pairs, start, scalars, sources, *operands):
    outs = [shape(KEYS, pairs * 2 * TOK)]
    if first > 0:
        outs += [shape(TOK, WIDE, dtype=jnp.float32)] + [shape(TOK, WIDE)] * 3
    else:
        outs += [shape(KEYS, WIDE, dtype=jnp.float32)]
    return call(
        functools.partial(teacher_kernel, first, pairs, start),
        [SMEM] + [ANY] * len(sources) + [VMEM] * len(operands),
        outs,
        [
            pltpu.VMEM((pairs, KEYS, 2 * HEAD), jnp.bfloat16),
            pltpu.VMEM((pairs, 2 * TOK, 2 * HEAD), jnp.bfloat16),
            pltpu.SemaphoreType.DMA((pairs, SPAN)),
        ],
        4 * pairs * TOK * KEYS * (2 * HEAD + WIDE),
        pairs * 1_500_000,
        2 * pairs * TOK * KEYS,
    )(scalars, *sources, *operands)


def query_call(counts, gs, lrt, up_weight):
    return call(
        functools.partial(query_kernel, counts),
        [VMEM] * (len(counts) + 2),
        [shape(TOK, HEADS * HEAD), shape(TOK, HEADS * ROPE)],
        [],
        4 * HEADS * TOK * LATENT * (KEYS + HEAD),
        6_000_000,
        kept=False,
    )(*gs, lrt, up_weight)


def finish_call(kept, received):
    return call(
        finish_kernel,
        [VMEM] * 4,
        [shape(TOK, LATENT, dtype=jnp.float32), shape(ROPE, TOK, dtype=jnp.float32)],
        [],
        0,
        1_000_000,
        kept=False,
    )(kept, *received)


def after(value, *others):
    return lax.optimization_barrier((value,) + others)[0]


def on_device(
    query_nope,
    query_rope,
    latent,
    key_rope,
    teacher_query,
    teacher_key,
    up_weight,
    kl_weight,
    key_back,
    valid_len,
):
    position = lax.axis_index(AXES)
    place = position % RING
    scalars = jnp.stack([position.astype(jnp.int32), key_back[0]])
    first, rest = pack_call(latent, key_rope, teacher_key)

    rotated = permute(rest, along_x(-1, (0, 1, 2, 3)))
    crossed_first = permute(first, next_run)
    crossed = permute(jnp.where(place == RING - 1, rest, rotated), next_run)
    later = after(rest, rotated)
    own1 = permute(later, along_x(1, (0, 1, 2)))
    own2 = permute(later, along_x(2, (0, 1)))
    everywhere = (0, 1, 2, 3)
    spread = [
        permute(jnp.where(place + step >= RING, crossed_first, first), along_x(step, everywhere))
        for step in (1, 2, 3)
    ]
    mixed = absorb_call(query_nope, query_rope, up_weight)
    chunk = (first, *spread)
    p, bias, coeff, lrt = student_call(scalars, valid_len, kl_weight, mixed, chunk)
    crossed = after(crossed, bias)
    back = permute(crossed, along_x(-1, (1, 2)))
    around = permute(crossed, along_x(1, (3,)))

    shared = (teacher_query, p, bias, coeff, mixed)
    g0, summed = teacher_call(0, FIRST, [0] * SPAN, scalars, chunk, *shared)
    chunk = (rest, own1, own2, rotated, crossed, back, around)
    g1, kept, *sent = teacher_call(FIRST, PAIRS - FIRST, [0] * 7, scalars, chunk, *shared, summed)

    received = [
        lax.ppermute(
            sent[distance - 1],
            AXES,
            [(b, b - distance) for b in range(distance, lax.axis_size(AXES))],
        )
        for distance in range(1, SPAN)
    ]
    d_nope, d_rope = query_call((FIRST, PAIRS - FIRST), (g0, g1), lrt, up_weight)
    d_latent, d_key_rope = finish_call(kept, received)
    return d_nope, d_rope, d_latent, d_key_rope.T


def solution(mesh):
    split = P(AXES, None)
    return jax.shard_map(
        on_device,
        mesh=mesh,
        in_specs=(split,) * 6 + (P(), split, P(AXES), P()),
        out_specs=(split,) * 4,
        check_vma=False,
    )
```

time: 212 us -> 115 us (0.54)
  the two profiles are of different devices: /device:TPU:74 before, /device:TPU:66 now
where the time goes in v2:
time: 115 us
  starting transfers between devices  50.1 us (44%)
  waiting for transfers between devices  42.2 us (37%)
  Pallas kernels  16.8 us (15%)
  local copies, waits for them, and re-layouts  2.84 us (2%)
  between operations  1.62 us (1%)
  other arithmetic  1.2 us (1%)
    ppermute x10, starting transfers between devices, permute(): return lax.ppermute(value, AXES, route(lax.axis_size(AXES)))  41.8 us
    ppermute x10, waiting for transfers between devices, permute(): return lax.ppermute(value, AXES, route(lax.axis_size(AXES)))  24.1 us
    ppermute x3, waiting for transfers between devices, on_device(): lax.ppermute(sent[distance - 1], AXES, [(b, b - distance) for b in range(...  18 us
    ppermute x3, starting transfers between devices, on_device(): lax.ppermute(sent[distance - 1], AXES, [(b, b - distance) for b in range(...  8.22 us
    pallas_call x2, Pallas kernels, teacher_call(): call(functools.partial(teacher_kernel, first, pairs, start), [SMEM] + [AN...  6.52 us
    pallas_call x1, Pallas kernels, query_call(): call(functools.partial(query_kernel, counts), [VMEM] * (len(counts) + 2),...  5.05 us
    pallas_call x1, Pallas kernels, student_call(): call(student_kernel, [SMEM, SMEM, VMEM, VMEM] + [ANY] * SPAN, [shape(KEYS...  3.55 us
    unnamed x18, local copies, waits for them, and re-layouts  2.84 us
  transfers between devices with their start and end apart: 13, of which 4 were waited for; matrix products, arithmetic and copies ran while one was open for 1% of the time, Pallas kernels for 10%

profile of v2, /device:TPU:66, one launch (start us, length us, event | category | flops | bytes accessed | tf_op | source)
XLA Modules:
  0.0 114.7 jit_solution(14005850221170966014)
XLA Ops:
  0.6 0.0 copy-start
  0.6 0.0 copy-start.2
  0.7 1.2 %copy-done.2 = bf16[128,2048]{1,0:T(8,128)(2,1)S(1)} copy-done((bf16[128,2048]{1,0:T(8,128)(2,1)S(1)}, bf16[128,2048]{1,0:T(8,128)(2,1)}, u32[]{:S(2)}) %copy-start.2) | copy-done | bytes 524312
  1.8 0.9 copy-done.5
  2.7 0.7 copy-done.6
  3.5 0.2 shard_map.129
  3.7 10.0 %collective-permute-start = (bf16[128,1408]{1,0:T(8,128)(2,1)S(1)}, bf16[128,1408]{1,0:T(8,128)(2,1)}, u32[]{:S(2)}, u32[]{:S(2)}) collective-permute-start(bf16[128,1408]{1,0:T(8,128)(2,1)S(1)} %get-tuple-element.23.refs_0_), channel_id=1, source_target_pairs={{0,4},{1,5},{2,6},{3,7},{4,8},{5,9},{6,10},{7,11},{8,12},{9,13},{1... | collective-permute-start | bytes 1081352 | tf_op jit(solution)/shard_map/ppermute | solution.py:52
  13.7 2.4 %collective-permute-start.4 = (bf16[128,1280]{1,0:T(8,128)(2,1)S(1)}, bf16[128,1280]{1,0:T(8,128)(2,1)S(1)}, u32[]{:S(2)}, u32[]{:S(2)}) collective-permute-start(bf16[128,1280]{1,0:T(8,128)(2,1)S(1)} %get-tuple-element.29.refs_0_), channel_id=1, source_target_pairs={{0,3},{1,0},{2,1},{3,2},{4,7},{5,4},{6,5},{7,6},{8,11},{9,8},{10,9... | collective-permute-start | bytes 983048 | tf_op jit(solution)/shard_map/ppermute | solution.py:52
  16.2 0.0 copy-start.3
  16.2 18.9 %collective-permute-done = bf16[128,1408]{1,0:T(8,128)(2,1)} collective-permute-done((bf16[128,1408]{1,0:T(8,128)(2,1)S(1)}, bf16[128,1408]{1,0:T(8,128)(2,1)}, u32[]{:S(2)}, u32[]{:S(2)}) %collective-permute-start) | collective-permute-done | bytes 360480 | tf_op jit(solution)/shard_map/ppermute | solution.py:52
  35.1 1.1 broadcast_select_fusion
  36.2 2.4 %collective-permute-start.3 = (bf16[128,1408]{1,0:T(8,128)(2,1)S(1)}, bf16[128,1408]{1,0:T(8,128)(2,1)S(1)}, u32[]{:S(2)}, u32[]{:S(2)}) collective-permute-start(bf16[128,1408]{1,0:T(8,128)(2,1)S(1)} %get-tuple-element.42), channel_id=1, source_target_pairs={{0,3},{1,0},{2,1},{3,2},{4,7},{5,4},{6,5},{7,6},{8,11},{9,8},{10,9... | collective-permute-start | bytes 1081352 | tf_op jit(solution)/shard_map/ppermute | solution.py:52
  38.7 4.3 %collective-permute-start.2 = (bf16[128,1408]{1,0:T(8,128)(2,1)S(1)}, bf16[128,1408]{1,0:T(8,128)(2,1)S(1)}, u32[]{:S(2)}, u32[]{:S(2)}) collective-permute-start(bf16[128,1408]{1,0:T(8,128)(2,1)S(1)} %get-tuple-element.43), channel_id=1, source_target_pairs={{0,2},{1,3},{2,0},{3,1},{4,6},{5,7},{6,4},{7,5},{8,10},{9,11},{10,... | collective-permute-start | bytes 1081352 | tf_op jit(solution)/shard_map/ppermute | solution.py:52
  43.0 3.7 %collective-permute-start.1 = (bf16[128,1408]{1,0:T(8,128)(2,1)S(1)}, bf16[128,1408]{1,0:T(8,128)(2,1)S(1)}, u32[]{:S(2)}, u32[]{:S(2)}) collective-permute-start(bf16[128,1408]{1,0:T(8,128)(2,1)S(1)} %get-tuple-element.44), channel_id=1, source_target_pairs={{0,1},{1,2},{2,3},{3,0},{4,5},{5,6},{6,7},{7,4},{8,9},{9,10},{10,1... | collective-permute-start | bytes 1081352 | tf_op jit(solution)/shard_map/ppermute | solution.py:52
  46.7 0.0 collective-permute-done.4.refs_3_
  46.8 8.4 %collective-permute-start.7 = (bf16[128,1280]{1,0:T(8,128)(2,1)S(1)}, bf16[128,1280]{1,0:T(8,128)(2,1)S(1)}, u32[]{:S(2)}, u32[]{:S(2)}) collective-permute-start(bf16[128,1280]{1,0:T(8,128)(2,1)S(1)} %broadcast_select_fusion.3), channel_id=1, source_target_pairs={{0,4},{1,5},{2,6},{3,7},{4,8},{5,9},{6,10},{7,11},{8,12},{9,13},{1... | collective-permute-start | bytes 983048 | tf_op jit(solution)/shard_map/ppermute | solution.py:52
  55.8 0.0 copy-done
  55.9 0.0 copy-done.4
  55.9 0.0 copy-done.3
  55.9 0.0 copy-start.7
  55.9 0.0 copy-start.8
  55.9 0.7 shard_map.130.mixed_ref.refs_8_.refs_11_
  56.6 0.1 pad_add_fusion.scalar_ref
  56.7 3.3 %collective-permute-start.6 = (bf16[128,1280]{1,0:T(8,128)(2,1)S(1)}, bf16[128,1280]{1,0:T(8,128)(2,1)S(1)}, u32[]{:S(2)}, u32[]{:S(2)}) collective-permute-start(bf16[128,1280]{1,0:T(8,128)(2,1)S(1)} %get-tuple-element.29.refs_0_), channel_id=1, source_target_pairs={{0,2},{1,3},{4,6},{5,7},{8,10},{9,11},{12,14},{13,15},{16,18},{17,... | collective-permute-start | bytes 983048 | tf_op jit(solution)/shard_map/ppermute | solution.py:52
  60.0 0.0 collective-permute-done.3.refs_3_
  60.0 1.9 %collective-permute-start.5 = (bf16[128,1280]{1,0:T(8,128)(2,1)S(1)}, bf16[128,1280]{1,0:T(8,128)(2,1)S(1)}, u32[]{:S(2)}, u32[]{:S(2)}) collective-permute-start(bf16[128,1280]{1,0:T(8,128)(2,1)S(1)} %get-tuple-element.29.refs_0_), channel_id=1, source_target_pairs={{0,1},{1,2},{2,3},{4,5},{5,6},{6,7},{8,9},{9,10},{10,11},{12,13},{... | collective-permute-start | bytes 983048 | tf_op jit(solution)/shard_map/ppermute | solution.py:52
  61.9 0.0 collective-permute-done.2.refs_2_
  61.9 0.0 collective-permute-done.1.refs_1_
  62.0 0.0 copy-done.7
  62.0 0.0 copy-start.1
  62.0 3.6 %shard_map.131 = (f32[512,2048]{1,0:T(8,128)S(1)}, f32[512,128]{1,0:T(8,128)S(1)}, f32[16,128]{1,0:T(8,128)S(1)}, bf16[640,512]{1,0:T(8,128)(2,1)S(1)}) custom-call(s32[2]{0:T(128)S(1)} %pad_add_fusion.scalar_ref, s32[512]{0:T(512)S(1)} %copy-done.8, f32[16,128]{1,0:T(8,128)S(1)} %bitcast.5, bf16[2048,640]{1,0:T(8,128)(2,1)S(1)} %shard_map.130.mixed_ref.refs_8_.refs_11_, ...), custom_call_target="tpu_custom_call" | custom-call | flops 1342177280 | bytes 8000000 | tf_op jit(solution)/shard_map/pallas_call | solution.py:265
  65.5 0.0 collective-permute-done.7.refs_4_
  65.6 0.7 collective-permute-start.9
  66.2 4.5 %collective-permute-start.8 = (bf16[128,1280]{1,0:T(8,128)(2,1)S(1)}, bf16[128,1280]{1,0:T(8,128)(2,1)S(1)}, u32[]{:S(2)}, u32[]{:S(2)}) collective-permute-start(bf16[128,1280]{1,0:T(8,128)(2,1)S(1)} %collective-permute-done.7.refs_4_), channel_id=1, source_target_pairs={{1,0},{2,1},{5,4},{6,5},{9,8},{10,9},{13,12},{14,13},{17,16},{18,1... | collective-permute-start | bytes 983048 | tf_op jit(solution)/shard_map/ppermute | solution.py:52
  70.8 2.7 %shard_map.132 = (bf16[512,768]{1,0:T(8,128)(2,1)S(1)}, f32[512,640]{1,0:T(8,128)S(1)}) custom-call(s32[2]{0:T(128)S(1)} %pad_add_fusion.scalar_ref, bf16[128,1408]{1,0:T(8,128)(2,1)S(1)} %get-tuple-element.23.refs_0_, bf16[128,1408]{1,0:T(8,128)(2,1)S(1)} %collective-permute-done.1.refs_1_, bf16[128,1408]{1,0:T(8,128)(2,1)S(1)} %collective-permute-done.2.refs_2_, ...), custom_call_target="tpu_custom_call" | custom-call | flops 704643072 | bytes 4500000 | tf_op jit(solution)/shard_map/pallas_call | solution.py:287
  73.5 0.0 collective-permute-done.6.refs_2_
  73.5 0.0 collective-permute-done.5.refs_1_
  73.5 0.0 collective-permute-done.9.refs_6_
  73.5 5.2 %collective-permute-done.8.refs_5_ = bf16[128,1280]{1,0:T(8,128)(2,1)S(1)} collective-permute-done((bf16[128,1280]{1,0:T(8,128)(2,1)S(1)}, bf16[128,1280]{1,0:T(8,128)(2,1)S(1)}, u32[]{:S(2)}, u32[]{:S(2)}) %collective-permute-start.8) | collective-permute-done | bytes 327712 | tf_op jit(solution)/shard_map/ppermute | solution.py:52
  78.7 3.9 %shard_map.133 = (bf16[512,1280]{1,0:T(8,128)(2,1)S(1)}, f32[128,640]{1,0:T(8,128)S(1)}, bf16[128,640]{1,0:T(8,128)(2,1)S(1)}, bf16[128,640]{1,0:T(8,128)(2,1)S(1)}, bf16[128,640]{1,0:T(8,128)(2,1)S(1)}) custom-call(s32[2]{0:T(128)S(1)} %pad_add_fusion.scalar_ref, bf16[128,1280]{1,0:T(8,128)(2,1)S(1)} %get-tuple-element.29.refs_0_, ...), custom_call_target="tpu_custom_call" | custom-call | flops 1174405120 | bytes 7500000 | tf_op jit(solution)/shard_map/pallas_call | solution.py:287
  82.5 4.4 %collective-permute-start.10 = (bf16[128,640]{1,0:T(8,128)(2,1)S(1)}, bf16[128,640]{1,0:T(8,128)(2,1)S(1)}, u32[]{:S(2)}, u32[]{:S(2)}) collective-permute-start(bf16[128,640]{1,0:T(8,128)(2,1)S(1)} %get-tuple-element.37), channel_id=1, source_target_pairs={{1,0},{2,1},{3,2},{4,3},{5,4},{6,5},{7,6},{8,7},{9,8},{10,9},{11,1... | collective-permute-start | bytes 491528 | tf_op jit(solution)/shard_map/ppermute | solution.py:371
  86.9 1.9 %collective-permute-start.11 = (bf16[128,640]{1,0:T(8,128)(2,1)S(1)}, bf16[128,640]{1,0:T(8,128)(2,1)S(1)}, u32[]{:S(2)}, u32[]{:S(2)}) collective-permute-start(bf16[128,640]{1,0:T(8,128)(2,1)S(1)} %get-tuple-element.38), channel_id=1, source_target_pairs={{2,0},{3,1},{4,2},{5,3},{6,4},{7,5},{8,6},{9,7},{10,8},{11,9},{12,... | collective-permute-start | bytes 491528 | tf_op jit(solution)/shard_map/ppermute | solution.py:371
  88.9 1.9 %collective-permute-start.12 = (bf16[128,640]{1,0:T(8,128)(2,1)S(1)}, bf16[128,640]{1,0:T(8,128)(2,1)S(1)}, u32[]{:S(2)}, u32[]{:S(2)}) collective-permute-start(bf16[128,640]{1,0:T(8,128)(2,1)S(1)} %get-tuple-element.39), channel_id=1, source_target_pairs={{3,0},{4,1},{5,2},{6,3},{7,4},{8,5},{9,6},{10,7},{11,8},{12,9},{13... | collective-permute-start | bytes 491528 | tf_op jit(solution)/shard_map/ppermute | solution.py:371
  90.8 5.1 %shard_map.134 = (bf16[128,2048]{1,0:T(8,128)(2,1)}, bf16[128,1024]{1,0:T(8,128)(2,1)}) custom-call(bf16[512,768]{1,0:T(8,128)(2,1)S(1)} %get-tuple-element.27.refs_0_, bf16[512,1280]{1,0:T(8,128)(2,1)S(1)} %get-tuple-element.32.refs_1_, bf16[640,512]{1,0:T(8,128)(2,1)S(1)} %get-tuple-element.33.refs_2_, bf16[16,128,512]{2,1,0:T(8,128)(2,1)S(1)} %copy-done), custom_call_target="tpu_custom_call" | custom-call | flops 2684354560 | bytes 6000000 | tf_op jit(solution)/shard_map/pallas_call | solution.py:303
  95.8 0.0 collective-permute-done.10.one_ref
  95.8 0.4 collective-permute-done.11.two_ref
  96.3 17.6 %collective-permute-done.12.three_ref = bf16[128,640]{1,0:T(8,128)(2,1)S(1)} collective-permute-done((bf16[128,640]{1,0:T(8,128)(2,1)S(1)}, bf16[128,640]{1,0:T(8,128)(2,1)S(1)}, u32[]{:S(2)}, u32[]{:S(2)}) %collective-permute-start.12) | collective-permute-done | bytes 163872 | tf_op jit(solution)/shard_map/ppermute | solution.py:371
  113.9 0.8 shard_map.135
  (6 shorter events, 0.0 us)
Async XLA Ops:
  0.6 55.2 %copy-start = (bf16[16,128,512]{2,1,0:T(8,128)(2,1)S(1)}, bf16[16,128,512]{2,1,0:T(8,128)(2,1)}, u32[]{:S(2)}) copy-start(bf16[16,128,512]{2,1,0:T(8,128)(2,1)} %refs_3_.1) | copy-start | bytes 6291460
  0.6 1.2 %copy-start.2 = (bf16[128,2048]{1,0:T(8,128)(2,1)S(1)}, bf16[128,2048]{1,0:T(8,128)(2,1)}, u32[]{:S(2)}) copy-start(bf16[128,2048]{1,0:T(8,128)(2,1)} %key_ref.1) | copy-start | bytes 1572868
  1.8 0.9 copy-start.5
  2.7 0.7 copy-start.6
  3.5 52.4 %copy-start.4 = (bf16[128,1024]{1,0:T(8,128)(2,1)S(1)}, bf16[128,1024]{1,0:T(8,128)(2,1)}, u32[]{:S(2)}) copy-start(bf16[128,1024]{1,0:T(8,128)(2,1)} %rope_ref.1) | copy-start | bytes 786436
  3.7 31.5 %collective-permute-start = (bf16[128,1408]{1,0:T(8,128)(2,1)S(1)}, bf16[128,1408]{1,0:T(8,128)(2,1)}, u32[]{:S(2)}, u32[]{:S(2)}) collective-permute-start(bf16[128,1408]{1,0:T(8,128)(2,1)S(1)} %get-tuple-element.23.refs_0_), channel_id=1, source_target_pairs={{0,4},{1,5},{2,6},{3,7},{4,8},{5,9},{6,10},{7,11},{8,12},{9,13},{1... | collective-permute-start | bytes 1081352 | tf_op jit(solution)/shard_map/ppermute | solution.py:52
  13.7 33.0 %collective-permute-start.4 = (bf16[128,1280]{1,0:T(8,128)(2,1)S(1)}, bf16[128,1280]{1,0:T(8,128)(2,1)S(1)}, u32[]{:S(2)}, u32[]{:S(2)}) collective-permute-start(bf16[128,1280]{1,0:T(8,128)(2,1)S(1)} %get-tuple-element.29.refs_0_), channel_id=1, source_target_pairs={{0,3},{1,0},{2,1},{3,2},{4,7},{5,4},{6,5},{7,6},{8,11},{9,8},{10,9... | collective-permute-start | bytes 983048 | tf_op jit(solution)/shard_map/ppermute | solution.py:52
  16.2 39.7 %copy-start.3 = (bf16[128,2048]{1,0:T(8,128)(2,1)S(1)}, bf16[128,2048]{1,0:T(8,128)(2,1)}, u32[]{:S(2)}) copy-start(bf16[128,2048]{1,0:T(8,128)(2,1)} %nope_ref.1) | copy-start | bytes 1572868
  36.2 23.8 %collective-permute-start.3 = (bf16[128,1408]{1,0:T(8,128)(2,1)S(1)}, bf16[128,1408]{1,0:T(8,128)(2,1)S(1)}, u32[]{:S(2)}, u32[]{:S(2)}) collective-permute-start(bf16[128,1408]{1,0:T(8,128)(2,1)S(1)} %get-tuple-element.42), channel_id=1, source_target_pairs={{0,3},{1,0},{2,1},{3,2},{4,7},{5,4},{6,5},{7,6},{8,11},{9,8},{10,9... | collective-permute-start | bytes 1081352 | tf_op jit(solution)/shard_map/ppermute | solution.py:52
  38.7 23.3 %collective-permute-start.2 = (bf16[128,1408]{1,0:T(8,128)(2,1)S(1)}, bf16[128,1408]{1,0:T(8,128)(2,1)S(1)}, u32[]{:S(2)}, u32[]{:S(2)}) collective-permute-start(bf16[128,1408]{1,0:T(8,128)(2,1)S(1)} %get-tuple-element.43), channel_id=1, source_target_pairs={{0,2},{1,3},{2,0},{3,1},{4,6},{5,7},{6,4},{7,5},{8,10},{9,11},{10,... | collective-permute-start | bytes 1081352 | tf_op jit(solution)/shard_map/ppermute | solution.py:52
  43.0 19.0 %collective-permute-start.1 = (bf16[128,1408]{1,0:T(8,128)(2,1)S(1)}, bf16[128,1408]{1,0:T(8,128)(2,1)S(1)}, u32[]{:S(2)}, u32[]{:S(2)}) collective-permute-start(bf16[128,1408]{1,0:T(8,128)(2,1)S(1)} %get-tuple-element.44), channel_id=1, source_target_pairs={{0,1},{1,2},{2,3},{3,0},{4,5},{5,6},{6,7},{7,4},{8,9},{9,10},{10,1... | collective-permute-start | bytes 1081352 | tf_op jit(solution)/shard_map/ppermute | solution.py:52
  46.8 18.8 %collective-permute-start.7 = (bf16[128,1280]{1,0:T(8,128)(2,1)S(1)}, bf16[128,1280]{1,0:T(8,128)(2,1)S(1)}, u32[]{:S(2)}, u32[]{:S(2)}) collective-permute-start(bf16[128,1280]{1,0:T(8,128)(2,1)S(1)} %broadcast_select_fusion.3), channel_id=1, source_target_pairs={{0,4},{1,5},{2,6},{3,7},{4,8},{5,9},{6,10},{7,11},{8,12},{9,13},{1... | collective-permute-start | bytes 983048 | tf_op jit(solution)/shard_map/ppermute | solution.py:52
  55.9 6.1 %copy-start.7 = (f32[128,16]{0,1:T(8,128)S(1)}, f32[128,16]{0,1:T(8,128)}, u32[]{:S(2)}) copy-start(f32[128,16]{0,1:T(8,128)} %param.17) | copy-start | bytes 24580
  55.9 6.1 %copy-start.8 = (s32[512]{0:T(512)S(1)}, s32[512]{0:T(512)}, u32[]{:S(2)}) copy-start(s32[512]{0:T(512)} %length_ref.1) | copy-start | bytes 6148
  56.7 16.8 %collective-permute-start.6 = (bf16[128,1280]{1,0:T(8,128)(2,1)S(1)}, bf16[128,1280]{1,0:T(8,128)(2,1)S(1)}, u32[]{:S(2)}, u32[]{:S(2)}) collective-permute-start(bf16[128,1280]{1,0:T(8,128)(2,1)S(1)} %get-tuple-element.29.refs_0_), channel_id=1, source_target_pairs={{0,2},{1,3},{4,6},{5,7},{8,10},{9,11},{12,14},{13,15},{16,18},{17,... | collective-permute-start | bytes 983048 | tf_op jit(solution)/shard_map/ppermute | solution.py:52
  60.0 13.5 %collective-permute-start.5 = (bf16[128,1280]{1,0:T(8,128)(2,1)S(1)}, bf16[128,1280]{1,0:T(8,128)(2,1)S(1)}, u32[]{:S(2)}, u32[]{:S(2)}) collective-permute-start(bf16[128,1280]{1,0:T(8,128)(2,1)S(1)} %get-tuple-element.29.refs_0_), channel_id=1, source_target_pairs={{0,1},{1,2},{2,3},{4,5},{5,6},{6,7},{8,9},{9,10},{10,11},{12,13},{... | collective-permute-start | bytes 983048 | tf_op jit(solution)/shard_map/ppermute | solution.py:52
  62.0 8.8 %copy-start.1 = (bf16[128,2048]{1,0:T(8,128)(2,1)S(1)}, bf16[128,2048]{1,0:T(8,128)(2,1)}, u32[]{:S(2)}) copy-start(bf16[128,2048]{1,0:T(8,128)(2,1)} %refs_7_.1) | copy-start | bytes 1572868
  65.6 7.9 %collective-permute-start.9 = (bf16[128,1280]{1,0:T(8,128)(2,1)S(1)}, bf16[128,1280]{1,0:T(8,128)(2,1)S(1)}, u32[]{:S(2)}, u32[]{:S(2)}) collective-permute-start(bf16[128,1280]{1,0:T(8,128)(2,1)S(1)} %collective-permute-done.7.refs_4_), channel_id=1, source_target_pairs={{3,0},{7,4},{11,8},{15,12},{19,16},{23,20},{27,24},{31,28},{35,32}... | collective-permute-start | bytes 983048 | tf_op jit(solution)/shard_map/ppermute | solution.py:52
  66.2 12.4 %collective-permute-start.8 = (bf16[128,1280]{1,0:T(8,128)(2,1)S(1)}, bf16[128,1280]{1,0:T(8,128)(2,1)S(1)}, u32[]{:S(2)}, u32[]{:S(2)}) collective-permute-start(bf16[128,1280]{1,0:T(8,128)(2,1)S(1)} %collective-permute-done.7.refs_4_), channel_id=1, source_target_pairs={{1,0},{2,1},{5,4},{6,5},{9,8},{10,9},{13,12},{14,13},{17,16},{18,1... | collective-permute-start | bytes 983048 | tf_op jit(solution)/shard_map/ppermute | solution.py:52
  82.5 13.3 %collective-permute-start.10 = (bf16[128,640]{1,0:T(8,128)(2,1)S(1)}, bf16[128,640]{1,0:T(8,128)(2,1)S(1)}, u32[]{:S(2)}, u32[]{:S(2)}) collective-permute-start(bf16[128,640]{1,0:T(8,128)(2,1)S(1)} %get-tuple-element.37), channel_id=1, source_target_pairs={{1,0},{2,1},{3,2},{4,3},{5,4},{6,5},{7,6},{8,7},{9,8},{10,9},{11,1... | collective-permute-start | bytes 491528 | tf_op jit(solution)/shard_map/ppermute | solution.py:371
  86.9 9.3 %collective-permute-start.11 = (bf16[128,640]{1,0:T(8,128)(2,1)S(1)}, bf16[128,640]{1,0:T(8,128)(2,1)S(1)}, u32[]{:S(2)}, u32[]{:S(2)}) collective-permute-start(bf16[128,640]{1,0:T(8,128)(2,1)S(1)} %get-tuple-element.38), channel_id=1, source_target_pairs={{2,0},{3,1},{4,2},{5,3},{6,4},{7,5},{8,6},{9,7},{10,8},{11,9},{12,... | collective-permute-start | bytes 491528 | tf_op jit(solution)/shard_map/ppermute | solution.py:371
  88.9 25.0 %collective-permute-start.12 = (bf16[128,640]{1,0:T(8,128)(2,1)S(1)}, bf16[128,640]{1,0:T(8,128)(2,1)S(1)}, u32[]{:S(2)}, u32[]{:S(2)}) collective-permute-start(bf16[128,640]{1,0:T(8,128)(2,1)S(1)} %get-tuple-element.39), channel_id=1, source_target_pairs={{3,0},{4,1},{5,2},{6,3},{7,4},{8,5},{9,6},{10,7},{11,8},{12,9},{13... | collective-permute-start | bytes 491528 | tf_op jit(solution)/shard_map/ppermute | solution.py:371

commit v3 on v2

--- a/solution.py
+++ b/solution.py
@@ -35,17 +35,23 @@
     return lax.dot_general(a, b, dims, preferred_element_type=jnp.float32)
 
 
-def along_x(step, sources):
+def along_x(step, sources, leaves=None):
     def route(count):
-        return [
-            (b, b - b % RING + (b + step) % RING) for b in range(count) if b % RING in sources
-        ]
+        pairs = []
+        for b in range(count):
+            if b % RING in sources:
+                to = b - b % RING + (b + step) % RING
+                if leaves is not None and b % RING in leaves and b % (2 * RING) < RING:
+                    to += 2 * RING
+                if to < count:
+                    pairs.append((b, to))
+        return pairs
 
     return route
 
 
-def next_run(count):
-    return [(b, b + RING) for b in range(count - RING)]
+def across_z(count):
+    return [(b, b ^ RING) for b in range(count)]
 
 
 def permute(value, route):
@@ -62,14 +68,17 @@
         for distance in range(SPAN):
             act(distance, sources[distance])
         return
-    own, own1, own2, rotated, crossed, back, around = sources
+    own, onward, own2, rotated, landed, back = sources
     act(0, own)
-    for distance, here, earlier in ((1, own1, around), (2, own2, back), (3, rotated, crossed)):
+    act(1, onward)
+    for distance, here, earlier in ((2, own2, back), (3, rotated, landed)):
         pl.when(place >= distance)(functools.partial(act, distance, here))
         pl.when(place < distance)(functools.partial(act, distance, earlier))
 
 
-def pack_kernel(latent_ref, rope_ref, key_ref, first_ref, rest_ref, sems):
+def pack_kernel(latent_ref, rope_ref, key_ref, first_ref, rest_ref, turned_ref, sems):
+    rope_copy = pltpu.make_async_copy(rope_ref, turned_ref, sems.at[3])
+    rope_copy.start()
     copies = [
         pltpu.make_async_copy(key_ref.at[:, pl.ds(0, CUT)], first_ref.at[:, pl.ds(0, CUT)], sems.at[0]),
         pltpu.make_async_copy(latent_ref, first_ref.at[:, pl.ds(CUT, LATENT)], sems.at[1]),
@@ -77,7 +86,8 @@
     ]
     for copy in copies:
         copy.start()
-    rope = rope_ref[...].astype(jnp.float32)
+    rope_copy.wait()
+    rope = turned_ref[...].astype(jnp.float32)
     both = jnp.concatenate([rope, rope], axis=0).T.astype(jnp.bfloat16)
     first_ref[:, CUT + LATENT :] = both
     for copy in copies:
@@ -216,6 +226,7 @@
 SMEM = pl.BlockSpec(memory_space=pltpu.SMEM)
 ANY = pl.BlockSpec(memory_space=pl.ANY)
 VMEM = pl.BlockSpec(memory_space=pltpu.VMEM)
+HBM = pl.BlockSpec(memory_space=pltpu.HBM)
 
 
 def call(kernel, ins, outs, scratch, flops, accessed, exps=0, kept=True):
@@ -242,12 +253,12 @@
 def pack_call(latent, key_rope, teacher_key):
     return call(
         pack_kernel,
-        [ANY, VMEM, ANY],
+        [HBM] * 3,
         [shape(TOK, CUT + WIDE), shape(TOK, REST)],
-        [pltpu.SemaphoreType.DMA((3,))],
+        [pltpu.VMEM((ROPE, TOK), jnp.bfloat16), pltpu.SemaphoreType.DMA((4,))],
         0,
         2_000_000,
-    )(latent, key_rope.T, teacher_key)
+    )(*(pltpu.with_memory_space_constraint(a, pltpu.HBM) for a in (latent, key_rope.T, teacher_key)))
 
 
 def absorb_call(nope, rope, up_weight):
@@ -345,27 +356,32 @@
     first, rest = pack_call(latent, key_rope, teacher_key)
 
     rotated = permute(rest, along_x(-1, (0, 1, 2, 3)))
-    crossed_first = permute(first, next_run)
-    crossed = permute(jnp.where(place == RING - 1, rest, rotated), next_run)
-    later = after(rest, rotated)
-    own1 = permute(later, along_x(1, (0, 1, 2)))
+    crossed_first = permute(first, across_z)
+    leaving = jnp.where(place == RING - 1, rest, rotated)
+    crossed = permute(leaving, across_z)
+    later = after(rest, leaving)
     own2 = permute(later, along_x(2, (0, 1)))
     everywhere = (0, 1, 2, 3)
     spread = [
-        permute(jnp.where(place + step >= RING, crossed_first, first), along_x(step, everywhere))
+        permute(
+            jnp.where(place + step >= RING, crossed_first, first),
+            along_x(step, everywhere, everywhere[RING - step :]),
+        )
         for step in (1, 2, 3)
     ]
-    mixed = absorb_call(query_nope, query_rope, up_weight)
+    mixed = absorb_call(after(query_nope, crossed, own2), query_rope, up_weight)
     chunk = (first, *spread)
-    p, bias, coeff, lrt = student_call(scalars, valid_len, kl_weight, mixed, chunk)
-    crossed = after(crossed, bias)
-    back = permute(crossed, along_x(-1, (1, 2)))
-    around = permute(crossed, along_x(1, (3,)))
+    p, bias, coeff, lrt = student_call(
+        scalars, valid_len, kl_weight, mixed, chunk
+    )
+    back = permute(crossed, along_x(-1, (1, 2), (1, 2)))
+    onward = permute(jnp.where(place == RING - 1, crossed, rest), along_x(1, everywhere, (3,)))
+    landed = permute(crossed, along_x(0, (0, 1, 2), (0, 1, 2)))
 
     shared = (teacher_query, p, bias, coeff, mixed)
     g0, summed = teacher_call(0, FIRST, [0] * SPAN, scalars, chunk, *shared)
-    chunk = (rest, own1, own2, rotated, crossed, back, around)
-    g1, kept, *sent = teacher_call(FIRST, PAIRS - FIRST, [0] * 7, scalars, chunk, *shared, summed)
+    chunk = (rest, onward, own2, rotated, landed, back)
+    g1, kept, *sent = teacher_call(FIRST, PAIRS - FIRST, [0] * 6, scalars, chunk, *shared, summed)
 
     received = [
         lax.ppermute(

time: 115 us -> 104 us (0.904)
  the two profiles are of different devices: /device:TPU:66 before, /device:TPU:49 now
where the time goes in v3:
time: 104 us
  starting transfers between devices  62.7 us (60%)
  waiting for transfers between devices  20 us (19%)
  Pallas kernels  17.9 us (17%)
  between operations  1.61 us (2%)
  other arithmetic  1.26 us (1%)
    ppermute x10, starting transfers between devices, permute(): return lax.ppermute(value, AXES, route(lax.axis_size(AXES)))  43 us
    ppermute x3, starting transfers between devices, on_device(): lax.ppermute(sent[distance - 1], AXES, [(b, b - distance) for b in range(...  19.7 us
    ppermute x3, waiting for transfers between devices, on_device(): lax.ppermute(sent[distance - 1], AXES, [(b, b - distance) for b in range(...  13.5 us
    ppermute x10, waiting for transfers between devices, permute(): return lax.ppermute(value, AXES, route(lax.axis_size(AXES)))  6.49 us
    pallas_call x2, Pallas kernels, teacher_call(): call(functools.partial(teacher_kernel, first, pairs, start), [SMEM] + [AN...  6.48 us
    pallas_call x1, Pallas kernels, query_call(): call(functools.partial(query_kernel, counts), [VMEM] * (len(counts) + 2),...  5.05 us
    pallas_call x1, Pallas kernels, student_call(): call(student_kernel, [SMEM, SMEM, VMEM, VMEM] + [ANY] * SPAN, [shape(KEYS...  3.55 us
  transfers between devices with their start and end apart: 13, of which 4 were waited for; matrix products, arithmetic and copies ran while one was open for 1% of the time, Pallas kernels for 12%

profile of v3, /device:TPU:49, one launch (start us, length us, event | category | flops | bytes accessed | tf_op | source)
XLA Modules:
  0.0 103.6 jit_solution(16670450631550848903)
XLA Ops:
  0.6 0.0 copy-start
  0.6 0.0 copy-start.3
  0.7 1.3 %shard_map.129 = (bf16[128,1408]{1,0:T(8,128)(2,1)S(1)}, bf16[128,1280]{1,0:T(8,128)(2,1)S(1)}) custom-call(bf16[128,512]{1,0:T(8,128)(2,1)} %latent_ref.1, bf16[64,128]{1,0:T(8,128)(2,1)} %bitcast.5, bf16[128,2048]{1,0:T(8,128)(2,1)} %key_ref.1), custom_call_target="tpu_custom_call" | custom-call | bytes 2000000 | tf_op jit(solution)/shard_map/pallas_call | solution.py:254
  2.0 4.4 %collective-permute-start.4 = (bf16[128,1280]{1,0:T(8,128)(2,1)S(1)}, bf16[128,1280]{1,0:T(8,128)(2,1)S(1)}, u32[]{:S(2)}, u32[]{:S(2)}) collective-permute-start(bf16[128,1280]{1,0:T(8,128)(2,1)S(1)} %get-tuple-element.25.refs_0_), channel_id=1, source_target_pairs={{0,3},{1,0},{2,1},{3,2},{4,7},{5,4},{6,5},{7,6},{8,11},{9,8},{10,9... | collective-permute-start | bytes 983048 | tf_op jit(solution)/shard_map/ppermute | solution.py:58
  6.4 10.6 %collective-permute-start = (bf16[128,1408]{1,0:T(8,128)(2,1)S(1)}, bf16[128,1408]{1,0:T(8,128)(2,1)}, u32[]{:S(2)}, u32[]{:S(2)}) collective-permute-start(bf16[128,1408]{1,0:T(8,128)(2,1)S(1)} %get-tuple-element.23.refs_0_), channel_id=1, source_target_pairs={{0,4},{1,5},{2,6},{3,7},{4,0},{5,1},{6,2},{7,3},{8,12},{9,13},{10,... | collective-permute-start | bytes 1081352 | tf_op jit(solution)/shard_map/ppermute | solution.py:58
  17.1 0.0 copy-start.2
  17.8 0.0 collective-permute-done.4.refs_3_
  17.8 5.6 %collective-permute-start.5 = (bf16[128,1280]{1,0:T(8,128)(2,1)S(1)}, bf16[128,1280]{1,0:T(8,128)(2,1)S(1)}, u32[]{:S(2)}, u32[]{:S(2)}) collective-permute-start(bf16[128,1280]{1,0:T(8,128)(2,1)S(1)} %broadcast_select_fusion.4), channel_id=1, source_target_pairs={{0,4},{1,5},{2,6},{3,7},{4,0},{5,1},{6,2},{7,3},{8,12},{9,13},{10,... | collective-permute-start | bytes 983048 | tf_op jit(solution)/shard_map/ppermute | solution.py:58
  23.4 4.4 %collective-permute-start.6 = (bf16[128,1280]{1,0:T(8,128)(2,1)S(1)}, bf16[128,1280]{1,0:T(8,128)(2,1)S(1)}, u32[]{:S(2)}, u32[]{:S(2)}) collective-permute-start(bf16[128,1280]{1,0:T(8,128)(2,1)S(1)} %get-tuple-element.25.refs_0_), channel_id=1, source_target_pairs={{0,2},{1,3},{4,6},{5,7},{8,10},{9,11},{12,14},{13,15},{16,18},{17,... | collective-permute-start | bytes 983048 | tf_op jit(solution)/shard_map/ppermute | solution.py:58
  27.8 0.0 collective-permute-done
  27.8 1.1 %broadcast_select_fusion = (bf16[128,1408]{1,0:T(8,128)(2,1)S(1)}, bf16[128,1408]{1,0:T(8,128)(2,1)S(1)}, bf16[128,1408]{1,0:T(8,128)(2,1)S(1)}) fusion(bf16[128,1408]{1,0:T(8,128)(2,1)} %collective-permute-done, bf16[128,1408]{1,0:T(8,128)(2,1)S(1)} %get-tuple-element.23.refs_0_, pred[]{:T(512)S(6)} %ge.11, pred[]{:T(512)S(6)} %ge.10, pred[]{:T(512)S(6)} %ge.9), kind=kLoop, calls=%fused_computation | loop fusion | flops 540672 | bytes 1802243 | tf_op jit(solution)/shard_map/jit(_where)/select_n | solution.py:367
  28.9 2.2 %collective-permute-start.3 = (bf16[128,1408]{1,0:T(8,128)(2,1)S(1)}, bf16[128,1408]{1,0:T(8,128)(2,1)S(1)}, u32[]{:S(2)}, u32[]{:S(2)}) collective-permute-start(bf16[128,1408]{1,0:T(8,128)(2,1)S(1)} %get-tuple-element.42), channel_id=1, source_target_pairs={{0,3},{1,8},{2,9},{3,10},{4,7},{5,4},{6,5},{7,6},{8,11},{9,16},{10... | collective-permute-start | bytes 1081352 | tf_op jit(solution)/shard_map/ppermute | solution.py:58
  31.2 7.0 %collective-permute-start.2 = (bf16[128,1408]{1,0:T(8,128)(2,1)S(1)}, bf16[128,1408]{1,0:T(8,128)(2,1)S(1)}, u32[]{:S(2)}, u32[]{:S(2)}) collective-permute-start(bf16[128,1408]{1,0:T(8,128)(2,1)S(1)} %get-tuple-element.43), channel_id=1, source_target_pairs={{0,2},{1,3},{2,8},{3,9},{4,6},{5,7},{6,4},{7,5},{8,10},{9,11},{10,... | collective-permute-start | bytes 1081352 | tf_op jit(solution)/shard_map/ppermute | solution.py:58
  38.2 1.9 %collective-permute-start.1 = (bf16[128,1408]{1,0:T(8,128)(2,1)S(1)}, bf16[128,1408]{1,0:T(8,128)(2,1)S(1)}, u32[]{:S(2)}, u32[]{:S(2)}) collective-permute-start(bf16[128,1408]{1,0:T(8,128)(2,1)S(1)} %get-tuple-element.44), channel_id=1, source_target_pairs={{0,1},{1,2},{2,3},{3,8},{4,5},{5,6},{6,7},{7,4},{8,9},{9,10},{10,1... | collective-permute-start | bytes 1081352 | tf_op jit(solution)/shard_map/ppermute | solution.py:58
  40.1 0.0 collective-permute-done.5
  40.2 1.9 %collective-permute-start.7 = (bf16[128,1280]{1,0:T(8,128)(2,1)S(1)}, bf16[128,1280]{1,0:T(8,128)(2,1)S(1)}, u32[]{:S(2)}, u32[]{:S(2)}) collective-permute-start(bf16[128,1280]{1,0:T(8,128)(2,1)S(1)} %broadcast_select_fusion.3), channel_id=1, source_target_pairs={{0,1},{1,2},{2,3},{3,8},{4,5},{5,6},{6,7},{7,4},{8,9},{9,10},{10,1... | collective-permute-start | bytes 983048 | tf_op jit(solution)/shard_map/ppermute | solution.py:58
  42.1 0.0 collective-permute-done.6.refs_2_
  42.1 1.3 %collective-permute-start.9 = (bf16[128,1280]{1,0:T(8,128)(2,1)S(1)}, bf16[128,1280]{1,0:T(8,128)(2,1)S(1)}, u32[]{:S(2)}, u32[]{:S(2)}) collective-permute-start(bf16[128,1280]{1,0:T(8,128)(2,1)S(1)} %collective-permute-done.5), channel_id=1, source_target_pairs={{1,8},{2,9},{5,4},{6,5},{9,16},{10,17},{13,12},{14,13},{17,24},{18... | collective-permute-start | bytes 983048 | tf_op jit(solution)/shard_map/ppermute | solution.py:58
  43.4 5.8 %collective-permute-done.3.refs_3_ = bf16[128,1408]{1,0:T(8,128)(2,1)S(1)} collective-permute-done((bf16[128,1408]{1,0:T(8,128)(2,1)S(1)}, bf16[128,1408]{1,0:T(8,128)(2,1)S(1)}, u32[]{:S(2)}, u32[]{:S(2)}) %collective-permute-start.3) | collective-permute-done | bytes 360480 | tf_op jit(solution)/shard_map/ppermute | solution.py:58
  49.2 3.7 %collective-permute-start.8 = (bf16[128,1280]{1,0:T(8,128)(2,1)S(1)}, bf16[128,1280]{1,0:T(8,128)(2,1)S(1)}, u32[]{:S(2)}, u32[]{:S(2)}) collective-permute-start(bf16[128,1280]{1,0:T(8,128)(2,1)S(1)} %collective-permute-done.5), channel_id=1, source_target_pairs={{0,8},{1,9},{2,10},{4,4},{5,5},{6,6},{8,16},{9,17},{10,18},{12,12}... | collective-permute-start | bytes 983048 | tf_op jit(solution)/shard_map/ppermute | solution.py:58
  52.9 0.1 pad_add_fusion.scalar_ref
  53.0 0.0 copy-done
  53.0 0.0 copy-done.3
  53.0 0.0 copy-done.2
  53.0 0.0 copy-start.4
  53.0 0.0 copy-start.5
  53.0 0.7 shard_map.130.mixed_ref.refs_8_.refs_10_
  53.7 0.0 collective-permute-done.2.refs_2_
  53.7 0.5 collective-permute-done.1.refs_1_
  54.2 0.0 copy-done.4
  54.2 0.0 copy-done.5
  54.2 0.0 copy-start.1
  54.2 3.5 %shard_map.131 = (f32[512,2048]{1,0:T(8,128)S(1)}, f32[512,128]{1,0:T(8,128)S(1)}, f32[16,128]{1,0:T(8,128)S(1)}, bf16[640,512]{1,0:T(8,128)(2,1)S(1)}) custom-call(s32[2]{0:T(128)S(1)} %pad_add_fusion.scalar_ref, s32[512]{0:T(512)S(1)} %copy-done.5, f32[16,128]{1,0:T(8,128)S(1)} %bitcast.4, bf16[2048,640]{1,0:T(8,128)(2,1)S(1)} %shard_map.130.mixed_ref.refs_8_.refs_10_, ...), custom_call_target="tpu_custom_call" | custom-call | flops 1342177280 | bytes 8000000 | tf_op jit(solution)/shard_map/pallas_call | solution.py:276
  57.8 0.0 copy-done.1
  57.8 2.7 %shard_map.132 = (bf16[512,768]{1,0:T(8,128)(2,1)S(1)}, f32[512,640]{1,0:T(8,128)S(1)}) custom-call(s32[2]{0:T(128)S(1)} %pad_add_fusion.scalar_ref, bf16[128,1408]{1,0:T(8,128)(2,1)S(1)} %get-tuple-element.23.refs_0_, bf16[128,1408]{1,0:T(8,128)(2,1)S(1)} %collective-permute-done.1.refs_1_, bf16[128,1408]{1,0:T(8,128)(2,1)S(1)} %collective-permute-done.2.refs_2_, ...), custom_call_target="tpu_custom_call" | custom-call | flops 704643072 | bytes 4500000 | tf_op jit(solution)/shard_map/pallas_call | solution.py:298
  60.4 0.2 collective-permute-done.7.refs_1_
  60.6 0.0 collective-permute-done.9.refs_5_
  60.6 0.0 collective-permute-done.8.refs_4_
  60.6 3.8 %shard_map.133 = (bf16[512,1280]{1,0:T(8,128)(2,1)S(1)}, f32[128,640]{1,0:T(8,128)S(1)}, bf16[128,640]{1,0:T(8,128)(2,1)S(1)}, bf16[128,640]{1,0:T(8,128)(2,1)S(1)}, bf16[128,640]{1,0:T(8,128)(2,1)S(1)}) custom-call(s32[2]{0:T(128)S(1)} %pad_add_fusion.scalar_ref, bf16[128,1280]{1,0:T(8,128)(2,1)S(1)} %get-tuple-element.25.refs_0_, ...), custom_call_target="tpu_custom_call" | custom-call | flops 1174405120 | bytes 7500000 | tf_op jit(solution)/shard_map/pallas_call | solution.py:298
  64.4 7.9 %collective-permute-start.10 = (bf16[128,640]{1,0:T(8,128)(2,1)S(1)}, bf16[128,640]{1,0:T(8,128)(2,1)S(1)}, u32[]{:S(2)}, u32[]{:S(2)}) collective-permute-start(bf16[128,640]{1,0:T(8,128)(2,1)S(1)} %get-tuple-element.37), channel_id=1, source_target_pairs={{1,0},{2,1},{3,2},{4,3},{5,4},{6,5},{7,6},{8,7},{9,8},{10,9},{11,1... | collective-permute-start | bytes 491528 | tf_op jit(solution)/shard_map/ppermute | solution.py:387
  72.3 4.0 %collective-permute-start.11 = (bf16[128,640]{1,0:T(8,128)(2,1)S(1)}, bf16[128,640]{1,0:T(8,128)(2,1)S(1)}, u32[]{:S(2)}, u32[]{:S(2)}) collective-permute-start(bf16[128,640]{1,0:T(8,128)(2,1)S(1)} %get-tuple-element.38), channel_id=1, source_target_pairs={{2,0},{3,1},{4,2},{5,3},{6,4},{7,5},{8,6},{9,7},{10,8},{11,9},{12,... | collective-permute-start | bytes 491528 | tf_op jit(solution)/shard_map/ppermute | solution.py:387
  76.3 7.8 %collective-permute-start.12 = (bf16[128,640]{1,0:T(8,128)(2,1)S(1)}, bf16[128,640]{1,0:T(8,128)(2,1)S(1)}, u32[]{:S(2)}, u32[]{:S(2)}) collective-permute-start(bf16[128,640]{1,0:T(8,128)(2,1)S(1)} %get-tuple-element.39), channel_id=1, source_target_pairs={{3,0},{4,1},{5,2},{6,3},{7,4},{8,5},{9,6},{10,7},{11,8},{12,9},{13... | collective-permute-start | bytes 491528 | tf_op jit(solution)/shard_map/ppermute | solution.py:387
  84.2 5.1 %shard_map.134 = (bf16[128,2048]{1,0:T(8,128)(2,1)}, bf16[128,1024]{1,0:T(8,128)(2,1)}) custom-call(bf16[512,768]{1,0:T(8,128)(2,1)S(1)} %get-tuple-element.30.refs_0_, bf16[512,1280]{1,0:T(8,128)(2,1)S(1)} %get-tuple-element.32.refs_1_, bf16[640,512]{1,0:T(8,128)(2,1)S(1)} %get-tuple-element.33.refs_2_, bf16[16,128,512]{2,1,0:T(8,128)(2,1)S(1)} %copy-done), custom_call_target="tpu_custom_call" | custom-call | flops 2684354560 | bytes 6000000 | tf_op jit(solution)/shard_map/pallas_call | solution.py:314
  89.2 0.0 collective-permute-done.10.one_ref
  89.2 0.0 collective-permute-done.11.two_ref
  89.2 13.5 %collective-permute-done.12.three_ref = bf16[128,640]{1,0:T(8,128)(2,1)S(1)} collective-permute-done((bf16[128,640]{1,0:T(8,128)(2,1)S(1)}, bf16[128,640]{1,0:T(8,128)(2,1)S(1)}, u32[]{:S(2)}, u32[]{:S(2)}) %collective-permute-start.12) | collective-permute-done | bytes 163872 | tf_op jit(solution)/shard_map/ppermute | solution.py:387
  102.8 0.8 shard_map.135
  (2 shorter events, 0.1 us)
Async XLA Ops:
  0.6 52.4 %copy-start = (bf16[16,128,512]{2,1,0:T(8,128)(2,1)S(1)}, bf16[16,128,512]{2,1,0:T(8,128)(2,1)}, u32[]{:S(2)}) copy-start(bf16[16,128,512]{2,1,0:T(8,128)(2,1)} %refs_3_.1) | copy-start | bytes 6291460
  0.6 52.4 %copy-start.3 = (bf16[128,1024]{1,0:T(8,128)(2,1)S(1)}, bf16[128,1024]{1,0:T(8,128)(2,1)}, u32[]{:S(2)}) copy-start(bf16[128,1024]{1,0:T(8,128)(2,1)} %rope_ref.1) | copy-start | bytes 786436
  2.0 15.8 %collective-permute-start.4 = (bf16[128,1280]{1,0:T(8,128)(2,1)S(1)}, bf16[128,1280]{1,0:T(8,128)(2,1)S(1)}, u32[]{:S(2)}, u32[]{:S(2)}) collective-permute-start(bf16[128,1280]{1,0:T(8,128)(2,1)S(1)} %get-tuple-element.25.refs_0_), channel_id=1, source_target_pairs={{0,3},{1,0},{2,1},{3,2},{4,7},{5,4},{6,5},{7,6},{8,11},{9,8},{10,9... | collective-permute-start | bytes 983048 | tf_op jit(solution)/shard_map/ppermute | solution.py:58
  6.4 21.4 %collective-permute-start = (bf16[128,1408]{1,0:T(8,128)(2,1)S(1)}, bf16[128,1408]{1,0:T(8,128)(2,1)}, u32[]{:S(2)}, u32[]{:S(2)}) collective-permute-start(bf16[128,1408]{1,0:T(8,128)(2,1)S(1)} %get-tuple-element.23.refs_0_), channel_id=1, source_target_pairs={{0,4},{1,5},{2,6},{3,7},{4,0},{5,1},{6,2},{7,3},{8,12},{9,13},{10,... | collective-permute-start | bytes 1081352 | tf_op jit(solution)/shard_map/ppermute | solution.py:58
  17.1 35.9 %copy-start.2 = (bf16[128,2048]{1,0:T(8,128)(2,1)S(1)}, bf16[128,2048]{1,0:T(8,128)(2,1)}, u32[]{:S(2)}) copy-start(bf16[128,2048]{1,0:T(8,128)(2,1)} %nope_ref) | copy-start | bytes 1572868
  17.8 22.3 %collective-permute-start.5 = (bf16[128,1280]{1,0:T(8,128)(2,1)S(1)}, bf16[128,1280]{1,0:T(8,128)(2,1)S(1)}, u32[]{:S(2)}, u32[]{:S(2)}) collective-permute-start(bf16[128,1280]{1,0:T(8,128)(2,1)S(1)} %broadcast_select_fusion.4), channel_id=1, source_target_pairs={{0,4},{1,5},{2,6},{3,7},{4,0},{5,1},{6,2},{7,3},{8,12},{9,13},{10,... | collective-permute-start | bytes 983048 | tf_op jit(solution)/shard_map/ppermute | solution.py:58
  23.4 18.7 %collective-permute-start.6 = (bf16[128,1280]{1,0:T(8,128)(2,1)S(1)}, bf16[128,1280]{1,0:T(8,128)(2,1)S(1)}, u32[]{:S(2)}, u32[]{:S(2)}) collective-permute-start(bf16[128,1280]{1,0:T(8,128)(2,1)S(1)} %get-tuple-element.25.refs_0_), channel_id=1, source_target_pairs={{0,2},{1,3},{4,6},{5,7},{8,10},{9,11},{12,14},{13,15},{16,18},{17,... | collective-permute-start | bytes 983048 | tf_op jit(solution)/shard_map/ppermute | solution.py:58
  28.9 20.3 %collective-permute-start.3 = (bf16[128,1408]{1,0:T(8,128)(2,1)S(1)}, bf16[128,1408]{1,0:T(8,128)(2,1)S(1)}, u32[]{:S(2)}, u32[]{:S(2)}) collective-permute-start(bf16[128,1408]{1,0:T(8,128)(2,1)S(1)} %get-tuple-element.42), channel_id=1, source_target_pairs={{0,3},{1,8},{2,9},{3,10},{4,7},{5,4},{6,5},{7,6},{8,11},{9,16},{10... | collective-permute-start | bytes 1081352 | tf_op jit(solution)/shard_map/ppermute | solution.py:58
  31.2 22.6 %collective-permute-start.2 = (bf16[128,1408]{1,0:T(8,128)(2,1)S(1)}, bf16[128,1408]{1,0:T(8,128)(2,1)S(1)}, u32[]{:S(2)}, u32[]{:S(2)}) collective-permute-start(bf16[128,1408]{1,0:T(8,128)(2,1)S(1)} %get-tuple-element.43), channel_id=1, source_target_pairs={{0,2},{1,3},{2,8},{3,9},{4,6},{5,7},{6,4},{7,5},{8,10},{9,11},{10,... | collective-permute-start | bytes 1081352 | tf_op jit(solution)/shard_map/ppermute | solution.py:58
  38.2 16.0 %collective-permute-start.1 = (bf16[128,1408]{1,0:T(8,128)(2,1)S(1)}, bf16[128,1408]{1,0:T(8,128)(2,1)S(1)}, u32[]{:S(2)}, u32[]{:S(2)}) collective-permute-start(bf16[128,1408]{1,0:T(8,128)(2,1)S(1)} %get-tuple-element.44), channel_id=1, source_target_pairs={{0,1},{1,2},{2,3},{3,8},{4,5},{5,6},{6,7},{7,4},{8,9},{9,10},{10,1... | collective-permute-start | bytes 1081352 | tf_op jit(solution)/shard_map/ppermute | solution.py:58
  40.2 20.4 %collective-permute-start.7 = (bf16[128,1280]{1,0:T(8,128)(2,1)S(1)}, bf16[128,1280]{1,0:T(8,128)(2,1)S(1)}, u32[]{:S(2)}, u32[]{:S(2)}) collective-permute-start(bf16[128,1280]{1,0:T(8,128)(2,1)S(1)} %broadcast_select_fusion.3), channel_id=1, source_target_pairs={{0,1},{1,2},{2,3},{3,8},{4,5},{5,6},{6,7},{7,4},{8,9},{9,10},{10,1... | collective-permute-start | bytes 983048 | tf_op jit(solution)/shard_map/ppermute | solution.py:58
  42.1 18.5 %collective-permute-start.9 = (bf16[128,1280]{1,0:T(8,128)(2,1)S(1)}, bf16[128,1280]{1,0:T(8,128)(2,1)S(1)}, u32[]{:S(2)}, u32[]{:S(2)}) collective-permute-start(bf16[128,1280]{1,0:T(8,128)(2,1)S(1)} %collective-permute-done.5), channel_id=1, source_target_pairs={{1,8},{2,9},{5,4},{6,5},{9,16},{10,17},{13,12},{14,13},{17,24},{18... | collective-permute-start | bytes 983048 | tf_op jit(solution)/shard_map/ppermute | solution.py:58
  49.2 11.3 %collective-permute-start.8 = (bf16[128,1280]{1,0:T(8,128)(2,1)S(1)}, bf16[128,1280]{1,0:T(8,128)(2,1)S(1)}, u32[]{:S(2)}, u32[]{:S(2)}) collective-permute-start(bf16[128,1280]{1,0:T(8,128)(2,1)S(1)} %collective-permute-done.5), channel_id=1, source_target_pairs={{0,8},{1,9},{2,10},{4,4},{5,5},{6,6},{8,16},{9,17},{10,18},{12,12}... | collective-permute-start | bytes 983048 | tf_op jit(solution)/shard_map/ppermute | solution.py:58
  53.0 1.2 %copy-start.4 = (f32[128,16]{0,1:T(8,128)S(1)}, f32[128,16]{0,1:T(8,128)}, u32[]{:S(2)}) copy-start(f32[128,16]{0,1:T(8,128)} %param.17) | copy-start | bytes 24580
  53.0 1.2 %copy-start.5 = (s32[512]{0:T(512)S(1)}, s32[512]{0:T(512)}, u32[]{:S(2)}) copy-start(s32[512]{0:T(512)} %length_ref.1) | copy-start | bytes 6148
  54.2 3.6 %copy-start.1 = (bf16[128,2048]{1,0:T(8,128)(2,1)S(1)}, bf16[128,2048]{1,0:T(8,128)(2,1)}, u32[]{:S(2)}) copy-start(bf16[128,2048]{1,0:T(8,128)(2,1)} %refs_6_.1) | copy-start | bytes 1572868
  64.4 24.8 %collective-permute-start.10 = (bf16[128,640]{1,0:T(8,128)(2,1)S(1)}, bf16[128,640]{1,0:T(8,128)(2,1)S(1)}, u32[]{:S(2)}, u32[]{:S(2)}) collective-permute-start(bf16[128,640]{1,0:T(8,128)(2,1)S(1)} %get-tuple-element.37), channel_id=1, source_target_pairs={{1,0},{2,1},{3,2},{4,3},{5,4},{6,5},{7,6},{8,7},{9,8},{10,9},{11,1... | collective-permute-start | bytes 491528 | tf_op jit(solution)/shard_map/ppermute | solution.py:387
  72.3 16.9 %collective-permute-start.11 = (bf16[128,640]{1,0:T(8,128)(2,1)S(1)}, bf16[128,640]{1,0:T(8,128)(2,1)S(1)}, u32[]{:S(2)}, u32[]{:S(2)}) collective-permute-start(bf16[128,640]{1,0:T(8,128)(2,1)S(1)} %get-tuple-element.38), channel_id=1, source_target_pairs={{2,0},{3,1},{4,2},{5,3},{6,4},{7,5},{8,6},{9,7},{10,8},{11,9},{12,... | collective-permute-start | bytes 491528 | tf_op jit(solution)/shard_map/ppermute | solution.py:387
  76.3 26.4 %collective-permute-start.12 = (bf16[128,640]{1,0:T(8,128)(2,1)S(1)}, bf16[128,640]{1,0:T(8,128)(2,1)S(1)}, u32[]{:S(2)}, u32[]{:S(2)}) collective-permute-start(bf16[128,640]{1,0:T(8,128)(2,1)S(1)} %get-tuple-element.39), channel_id=1, source_target_pairs={{3,0},{4,1},{5,2},{6,3},{7,4},{8,5},{9,6},{10,7},{11,8},{12,9},{13... | collective-permute-start | bytes 491528 | tf_op jit(solution)/shard_map/ppermute | solution.py:387

commit v4 on v3

--- a/solution.py
+++ b/solution.py
@@ -389,7 +389,7 @@
             AXES,
             [(b, b - distance) for b in range(distance, lax.axis_size(AXES))],
         )
-        for distance in range(1, SPAN)
+        for distance in (3, 1, 2)
     ]
     d_nope, d_rope = query_call((FIRST, PAIRS - FIRST), (g0, g1), lrt, up_weight)
     d_latent, d_key_rope = finish_call(kept, received)

time: 104 us -> 102 us (0.981)
  the two profiles are of different devices: /device:TPU:49 before, /device:TPU:189 now
where the time goes in v4:
time: 102 us
  starting transfers between devices  48.9 us (48%)
  waiting for transfers between devices  32.2 us (32%)
  Pallas kernels  17.9 us (18%)
  between operations  1.6 us (2%)
  other arithmetic  1.25 us (1%)
    ppermute x10, starting transfers between devices, permute(): return lax.ppermute(value, AXES, route(lax.axis_size(AXES)))  32 us
    ppermute x10, waiting for transfers between devices, permute(): return lax.ppermute(value, AXES, route(lax.axis_size(AXES)))  25.2 us
    ppermute x3, starting transfers between devices, on_device(): lax.ppermute(sent[distance - 1], AXES, [(b, b - distance) for b in range(...  16.9 us
    ppermute x3, waiting for transfers between devices, on_device(): lax.ppermute(sent[distance - 1], AXES, [(b, b - distance) for b in range(...  6.98 us
    pallas_call x2, Pallas kernels, teacher_call(): call(functools.partial(teacher_kernel, first, pairs, start), [SMEM] + [AN...  6.48 us
    pallas_call x1, Pallas kernels, query_call(): call(functools.partial(query_kernel, counts), [VMEM] * (len(counts) + 2),...  5.05 us
    pallas_call x1, Pallas kernels, student_call(): call(student_kernel, [SMEM, SMEM, VMEM, VMEM] + [ANY] * SPAN, [shape(KEYS...  3.55 us
  transfers between devices with their start and end apart: 13, of which 5 were waited for; matrix products, arithmetic and copies ran while one was open for 1% of the time, Pallas kernels for 12%

profile of v4, /device:TPU:189, one launch (start us, length us, event | category | flops | bytes accessed | tf_op | source)
XLA Modules:
  0.0 101.8 jit_solution(10930709280556145308)
XLA Ops:
  0.6 0.0 copy-start
  0.6 0.0 copy-start.3
  0.7 1.3 %shard_map.129 = (bf16[128,1408]{1,0:T(8,128)(2,1)S(1)}, bf16[128,1280]{1,0:T(8,128)(2,1)S(1)}) custom-call(bf16[128,512]{1,0:T(8,128)(2,1)} %latent_ref.1, bf16[64,128]{1,0:T(8,128)(2,1)} %bitcast.5, bf16[128,2048]{1,0:T(8,128)(2,1)} %key_ref.1), custom_call_target="tpu_custom_call" | custom-call | bytes 2000000 | tf_op jit(solution)/shard_map/pallas_call | solution.py:254
  2.0 2.2 %collective-permute-start.4 = (bf16[128,1280]{1,0:T(8,128)(2,1)S(1)}, bf16[128,1280]{1,0:T(8,128)(2,1)S(1)}, u32[]{:S(2)}, u32[]{:S(2)}) collective-permute-start(bf16[128,1280]{1,0:T(8,128)(2,1)S(1)} %get-tuple-element.25.refs_0_), channel_id=1, source_target_pairs={{0,3},{1,0},{2,1},{3,2},{4,7},{5,4},{6,5},{7,6},{8,11},{9,8},{10,9... | collective-permute-start | bytes 983048 | tf_op jit(solution)/shard_map/ppermute | solution.py:58
  4.2 8.8 %collective-permute-start = (bf16[128,1408]{1,0:T(8,128)(2,1)S(1)}, bf16[128,1408]{1,0:T(8,128)(2,1)}, u32[]{:S(2)}, u32[]{:S(2)}) collective-permute-start(bf16[128,1408]{1,0:T(8,128)(2,1)S(1)} %get-tuple-element.23.refs_0_), channel_id=1, source_target_pairs={{0,4},{1,5},{2,6},{3,7},{4,0},{5,1},{6,2},{7,3},{8,12},{9,13},{10,... | collective-permute-start | bytes 1081352 | tf_op jit(solution)/shard_map/ppermute | solution.py:58
  13.0 0.0 copy-start.2
  13.8 0.0 collective-permute-done.4.refs_3_
  13.8 7.5 %collective-permute-start.5 = (bf16[128,1280]{1,0:T(8,128)(2,1)S(1)}, bf16[128,1280]{1,0:T(8,128)(2,1)S(1)}, u32[]{:S(2)}, u32[]{:S(2)}) collective-permute-start(bf16[128,1280]{1,0:T(8,128)(2,1)S(1)} %broadcast_select_fusion.4), channel_id=1, source_target_pairs={{0,4},{1,5},{2,6},{3,7},{4,0},{5,1},{6,2},{7,3},{8,12},{9,13},{10,... | collective-permute-start | bytes 983048 | tf_op jit(solution)/shard_map/ppermute | solution.py:58
  21.4 1.3 %collective-permute-start.6 = (bf16[128,1280]{1,0:T(8,128)(2,1)S(1)}, bf16[128,1280]{1,0:T(8,128)(2,1)S(1)}, u32[]{:S(2)}, u32[]{:S(2)}) collective-permute-start(bf16[128,1280]{1,0:T(8,128)(2,1)S(1)} %get-tuple-element.25.refs_0_), channel_id=1, source_target_pairs={{0,2},{1,3},{4,6},{5,7},{8,10},{9,11},{12,14},{13,15},{16,18},{17,... | collective-permute-start | bytes 983048 | tf_op jit(solution)/shard_map/ppermute | solution.py:58
  22.7 14.0 %collective-permute-done = bf16[128,1408]{1,0:T(8,128)(2,1)} collective-permute-done((bf16[128,1408]{1,0:T(8,128)(2,1)S(1)}, bf16[128,1408]{1,0:T(8,128)(2,1)}, u32[]{:S(2)}, u32[]{:S(2)}) %collective-permute-start) | collective-permute-done | bytes 360480 | tf_op jit(solution)/shard_map/ppermute | solution.py:58
  36.7 1.1 %broadcast_select_fusion = (bf16[128,1408]{1,0:T(8,128)(2,1)S(1)}, bf16[128,1408]{1,0:T(8,128)(2,1)S(1)}, bf16[128,1408]{1,0:T(8,128)(2,1)S(1)}) fusion(bf16[128,1408]{1,0:T(8,128)(2,1)} %collective-permute-done, bf16[128,1408]{1,0:T(8,128)(2,1)S(1)} %get-tuple-element.23.refs_0_, pred[]{:T(512)S(6)} %ge.11, pred[]{:T(512)S(6)} %ge.10, pred[]{:T(512)S(6)} %ge.9), kind=kLoop, calls=%fused_computation | loop fusion | flops 540672 | bytes 1802243 | tf_op jit(solution)/shard_map/jit(_where)/select_n | solution.py:367
  37.8 1.9 %collective-permute-start.3 = (bf16[128,1408]{1,0:T(8,128)(2,1)S(1)}, bf16[128,1408]{1,0:T(8,128)(2,1)S(1)}, u32[]{:S(2)}, u32[]{:S(2)}) collective-permute-start(bf16[128,1408]{1,0:T(8,128)(2,1)S(1)} %get-tuple-element.42), channel_id=1, source_target_pairs={{0,3},{1,8},{2,9},{3,10},{4,7},{5,4},{6,5},{7,6},{8,11},{9,16},{10... | collective-permute-start | bytes 1081352 | tf_op jit(solution)/shard_map/ppermute | solution.py:58
  39.7 1.9 %collective-permute-start.2 = (bf16[128,1408]{1,0:T(8,128)(2,1)S(1)}, bf16[128,1408]{1,0:T(8,128)(2,1)S(1)}, u32[]{:S(2)}, u32[]{:S(2)}) collective-permute-start(bf16[128,1408]{1,0:T(8,128)(2,1)S(1)} %get-tuple-element.43), channel_id=1, source_target_pairs={{0,2},{1,3},{2,8},{3,9},{4,6},{5,7},{6,4},{7,5},{8,10},{9,11},{10,... | collective-permute-start | bytes 1081352 | tf_op jit(solution)/shard_map/ppermute | solution.py:58
  41.6 3.1 %collective-permute-start.1 = (bf16[128,1408]{1,0:T(8,128)(2,1)S(1)}, bf16[128,1408]{1,0:T(8,128)(2,1)S(1)}, u32[]{:S(2)}, u32[]{:S(2)}) collective-permute-start(bf16[128,1408]{1,0:T(8,128)(2,1)S(1)} %get-tuple-element.44), channel_id=1, source_target_pairs={{0,1},{1,2},{2,3},{3,8},{4,5},{5,6},{6,7},{7,4},{8,9},{9,10},{10,1... | collective-permute-start | bytes 1081352 | tf_op jit(solution)/shard_map/ppermute | solution.py:58
  44.8 0.0 collective-permute-done.5
  44.8 2.0 %collective-permute-start.7 = (bf16[128,1280]{1,0:T(8,128)(2,1)S(1)}, bf16[128,1280]{1,0:T(8,128)(2,1)S(1)}, u32[]{:S(2)}, u32[]{:S(2)}) collective-permute-start(bf16[128,1280]{1,0:T(8,128)(2,1)S(1)} %broadcast_select_fusion.3), channel_id=1, source_target_pairs={{0,1},{1,2},{2,3},{3,8},{4,5},{5,6},{6,7},{7,4},{8,9},{9,10},{10,1... | collective-permute-start | bytes 983048 | tf_op jit(solution)/shard_map/ppermute | solution.py:58
  46.8 0.0 collective-permute-done.6.refs_2_
  46.8 1.3 %collective-permute-start.9 = (bf16[128,1280]{1,0:T(8,128)(2,1)S(1)}, bf16[128,1280]{1,0:T(8,128)(2,1)S(1)}, u32[]{:S(2)}, u32[]{:S(2)}) collective-permute-start(bf16[128,1280]{1,0:T(8,128)(2,1)S(1)} %collective-permute-done.5), channel_id=1, source_target_pairs={{1,8},{2,9},{5,4},{6,5},{9,16},{10,17},{13,12},{14,13},{17,24},{18... | collective-permute-start | bytes 983048 | tf_op jit(solution)/shard_map/ppermute | solution.py:58
  48.1 6.5 %collective-permute-done.3.refs_3_ = bf16[128,1408]{1,0:T(8,128)(2,1)S(1)} collective-permute-done((bf16[128,1408]{1,0:T(8,128)(2,1)S(1)}, bf16[128,1408]{1,0:T(8,128)(2,1)S(1)}, u32[]{:S(2)}, u32[]{:S(2)}) %collective-permute-start.3) | collective-permute-done | bytes 360480 | tf_op jit(solution)/shard_map/ppermute | solution.py:58
  54.6 1.9 %collective-permute-start.8 = (bf16[128,1280]{1,0:T(8,128)(2,1)S(1)}, bf16[128,1280]{1,0:T(8,128)(2,1)S(1)}, u32[]{:S(2)}, u32[]{:S(2)}) collective-permute-start(bf16[128,1280]{1,0:T(8,128)(2,1)S(1)} %collective-permute-done.5), channel_id=1, source_target_pairs={{0,8},{1,9},{2,10},{4,4},{5,5},{6,6},{8,16},{9,17},{10,18},{12,12}... | collective-permute-start | bytes 983048 | tf_op jit(solution)/shard_map/ppermute | solution.py:58
  56.6 0.1 pad_add_fusion.scalar_ref
  56.6 0.0 copy-done
  56.6 0.0 copy-done.3
  56.6 0.0 copy-done.2
  56.6 0.0 copy-start.4
  56.7 0.0 copy-start.5
  56.7 0.7 shard_map.130.mixed_ref.refs_8_.refs_10_
  57.4 0.0 collective-permute-done.2.refs_2_
  57.4 3.8 %collective-permute-done.1.refs_1_ = bf16[128,1408]{1,0:T(8,128)(2,1)S(1)} collective-permute-done((bf16[128,1408]{1,0:T(8,128)(2,1)S(1)}, bf16[128,1408]{1,0:T(8,128)(2,1)S(1)}, u32[]{:S(2)}, u32[]{:S(2)}) %collective-permute-start.1) | collective-permute-done | bytes 360480 | tf_op jit(solution)/shard_map/ppermute | solution.py:58
  61.2 0.0 copy-done.4
  61.2 0.0 copy-done.5
  61.2 0.0 copy-start.1
  61.2 3.5 %shard_map.131 = (f32[512,2048]{1,0:T(8,128)S(1)}, f32[512,128]{1,0:T(8,128)S(1)}, f32[16,128]{1,0:T(8,128)S(1)}, bf16[640,512]{1,0:T(8,128)(2,1)S(1)}) custom-call(s32[2]{0:T(128)S(1)} %pad_add_fusion.scalar_ref, s32[512]{0:T(512)S(1)} %copy-done.5, f32[16,128]{1,0:T(8,128)S(1)} %bitcast.4, bf16[2048,640]{1,0:T(8,128)(2,1)S(1)} %shard_map.130.mixed_ref.refs_8_.refs_10_, ...), custom_call_target="tpu_custom_call" | custom-call | flops 1342177280 | bytes 8000000 | tf_op jit(solution)/shard_map/pallas_call | solution.py:276
  64.8 0.0 copy-done.1
  64.8 2.7 %shard_map.132 = (bf16[512,768]{1,0:T(8,128)(2,1)S(1)}, f32[512,640]{1,0:T(8,128)S(1)}) custom-call(s32[2]{0:T(128)S(1)} %pad_add_fusion.scalar_ref, bf16[128,1408]{1,0:T(8,128)(2,1)S(1)} %get-tuple-element.23.refs_0_, bf16[128,1408]{1,0:T(8,128)(2,1)S(1)} %collective-permute-done.1.refs_1_, bf16[128,1408]{1,0:T(8,128)(2,1)S(1)} %collective-permute-done.2.refs_2_, ...), custom_call_target="tpu_custom_call" | custom-call | flops 704643072 | bytes 4500000 | tf_op jit(solution)/shard_map/pallas_call | solution.py:298
  67.4 0.8 collective-permute-done.7.refs_1_
  68.2 0.0 collective-permute-done.9.refs_5_
  68.2 0.0 collective-permute-done.8.refs_4_
  68.2 3.8 %shard_map.133 = (bf16[512,1280]{1,0:T(8,128)(2,1)S(1)}, f32[128,640]{1,0:T(8,128)S(1)}, bf16[128,640]{1,0:T(8,128)(2,1)S(1)}, bf16[128,640]{1,0:T(8,128)(2,1)S(1)}, bf16[128,640]{1,0:T(8,128)(2,1)S(1)}) custom-call(s32[2]{0:T(128)S(1)} %pad_add_fusion.scalar_ref, bf16[128,1280]{1,0:T(8,128)(2,1)S(1)} %get-tuple-element.25.refs_0_, ...), custom_call_target="tpu_custom_call" | custom-call | flops 1174405120 | bytes 7500000 | tf_op jit(solution)/shard_map/pallas_call | solution.py:298
  72.1 9.3 %collective-permute-start.10 = (bf16[128,640]{1,0:T(8,128)(2,1)S(1)}, bf16[128,640]{1,0:T(8,128)(2,1)S(1)}, u32[]{:S(2)}, u32[]{:S(2)}) collective-permute-start(bf16[128,640]{1,0:T(8,128)(2,1)S(1)} %get-tuple-element.37), channel_id=1, source_target_pairs={{3,0},{4,1},{5,2},{6,3},{7,4},{8,5},{9,6},{10,7},{11,8},{12,9},{13... | collective-permute-start | bytes 491528 | tf_op jit(solution)/shard_map/ppermute | solution.py:387
  81.4 1.9 %collective-permute-start.11 = (bf16[128,640]{1,0:T(8,128)(2,1)S(1)}, bf16[128,640]{1,0:T(8,128)(2,1)S(1)}, u32[]{:S(2)}, u32[]{:S(2)}) collective-permute-start(bf16[128,640]{1,0:T(8,128)(2,1)S(1)} %get-tuple-element.38), channel_id=1, source_target_pairs={{1,0},{2,1},{3,2},{4,3},{5,4},{6,5},{7,6},{8,7},{9,8},{10,9},{11,1... | collective-permute-start | bytes 491528 | tf_op jit(solution)/shard_map/ppermute | solution.py:387
  83.3 5.7 %collective-permute-start.12 = (bf16[128,640]{1,0:T(8,128)(2,1)S(1)}, bf16[128,640]{1,0:T(8,128)(2,1)S(1)}, u32[]{:S(2)}, u32[]{:S(2)}) collective-permute-start(bf16[128,640]{1,0:T(8,128)(2,1)S(1)} %get-tuple-element.39), channel_id=1, source_target_pairs={{2,0},{3,1},{4,2},{5,3},{6,4},{7,5},{8,6},{9,7},{10,8},{11,9},{12,... | collective-permute-start | bytes 491528 | tf_op jit(solution)/shard_map/ppermute | solution.py:387
  89.0 5.1 %shard_map.134 = (bf16[128,2048]{1,0:T(8,128)(2,1)}, bf16[128,1024]{1,0:T(8,128)(2,1)}) custom-call(bf16[512,768]{1,0:T(8,128)(2,1)S(1)} %get-tuple-element.30.refs_0_, bf16[512,1280]{1,0:T(8,128)(2,1)S(1)} %get-tuple-element.32.refs_1_, bf16[640,512]{1,0:T(8,128)(2,1)S(1)} %get-tuple-element.33.refs_2_, bf16[16,128,512]{2,1,0:T(8,128)(2,1)S(1)} %copy-done), custom_call_target="tpu_custom_call" | custom-call | flops 2684354560 | bytes 6000000 | tf_op jit(solution)/shard_map/pallas_call | solution.py:314
  94.0 0.0 collective-permute-done.10.one_ref
  94.0 0.0 collective-permute-done.11.two_ref
  94.0 7.0 %collective-permute-done.12.three_ref = bf16[128,640]{1,0:T(8,128)(2,1)S(1)} collective-permute-done((bf16[128,640]{1,0:T(8,128)(2,1)S(1)}, bf16[128,640]{1,0:T(8,128)(2,1)S(1)}, u32[]{:S(2)}, u32[]{:S(2)}) %collective-permute-start.12) | collective-permute-done | bytes 163872 | tf_op jit(solution)/shard_map/ppermute | solution.py:387
  101.0 0.8 shard_map.135
  (2 shorter events, 0.1 us)
Async XLA Ops:
  0.6 56.0 %copy-start = (bf16[16,128,512]{2,1,0:T(8,128)(2,1)S(1)}, bf16[16,128,512]{2,1,0:T(8,128)(2,1)}, u32[]{:S(2)}) copy-start(bf16[16,128,512]{2,1,0:T(8,128)(2,1)} %refs_3_.1) | copy-start | bytes 6291460
  0.6 56.0 %copy-start.3 = (bf16[128,1024]{1,0:T(8,128)(2,1)S(1)}, bf16[128,1024]{1,0:T(8,128)(2,1)}, u32[]{:S(2)}) copy-start(bf16[128,1024]{1,0:T(8,128)(2,1)} %rope_ref.1) | copy-start | bytes 786436
  2.0 11.8 %collective-permute-start.4 = (bf16[128,1280]{1,0:T(8,128)(2,1)S(1)}, bf16[128,1280]{1,0:T(8,128)(2,1)S(1)}, u32[]{:S(2)}, u32[]{:S(2)}) collective-permute-start(bf16[128,1280]{1,0:T(8,128)(2,1)S(1)} %get-tuple-element.25.refs_0_), channel_id=1, source_target_pairs={{0,3},{1,0},{2,1},{3,2},{4,7},{5,4},{6,5},{7,6},{8,11},{9,8},{10,9... | collective-permute-start | bytes 983048 | tf_op jit(solution)/shard_map/ppermute | solution.py:58
  4.2 32.5 %collective-permute-start = (bf16[128,1408]{1,0:T(8,128)(2,1)S(1)}, bf16[128,1408]{1,0:T(8,128)(2,1)}, u32[]{:S(2)}, u32[]{:S(2)}) collective-permute-start(bf16[128,1408]{1,0:T(8,128)(2,1)S(1)} %get-tuple-element.23.refs_0_), channel_id=1, source_target_pairs={{0,4},{1,5},{2,6},{3,7},{4,0},{5,1},{6,2},{7,3},{8,12},{9,13},{10,... | collective-permute-start | bytes 1081352 | tf_op jit(solution)/shard_map/ppermute | solution.py:58
  13.0 43.6 %copy-start.2 = (bf16[128,2048]{1,0:T(8,128)(2,1)S(1)}, bf16[128,2048]{1,0:T(8,128)(2,1)}, u32[]{:S(2)}) copy-start(bf16[128,2048]{1,0:T(8,128)(2,1)} %nope_ref) | copy-start | bytes 1572868
  13.8 31.0 %collective-permute-start.5 = (bf16[128,1280]{1,0:T(8,128)(2,1)S(1)}, bf16[128,1280]{1,0:T(8,128)(2,1)S(1)}, u32[]{:S(2)}, u32[]{:S(2)}) collective-permute-start(bf16[128,1280]{1,0:T(8,128)(2,1)S(1)} %broadcast_select_fusion.4), channel_id=1, source_target_pairs={{0,4},{1,5},{2,6},{3,7},{4,0},{5,1},{6,2},{7,3},{8,12},{9,13},{10,... | collective-permute-start | bytes 983048 | tf_op jit(solution)/shard_map/ppermute | solution.py:58
  21.4 25.4 %collective-permute-start.6 = (bf16[128,1280]{1,0:T(8,128)(2,1)S(1)}, bf16[128,1280]{1,0:T(8,128)(2,1)S(1)}, u32[]{:S(2)}, u32[]{:S(2)}) collective-permute-start(bf16[128,1280]{1,0:T(8,128)(2,1)S(1)} %get-tuple-element.25.refs_0_), channel_id=1, source_target_pairs={{0,2},{1,3},{4,6},{5,7},{8,10},{9,11},{12,14},{13,15},{16,18},{17,... | collective-permute-start | bytes 983048 | tf_op jit(solution)/shard_map/ppermute | solution.py:58
  37.8 16.9 %collective-permute-start.3 = (bf16[128,1408]{1,0:T(8,128)(2,1)S(1)}, bf16[128,1408]{1,0:T(8,128)(2,1)S(1)}, u32[]{:S(2)}, u32[]{:S(2)}) collective-permute-start(bf16[128,1408]{1,0:T(8,128)(2,1)S(1)} %get-tuple-element.42), channel_id=1, source_target_pairs={{0,3},{1,8},{2,9},{3,10},{4,7},{5,4},{6,5},{7,6},{8,11},{9,16},{10... | collective-permute-start | bytes 1081352 | tf_op jit(solution)/shard_map/ppermute | solution.py:58
  39.7 17.7 %collective-permute-start.2 = (bf16[128,1408]{1,0:T(8,128)(2,1)S(1)}, bf16[128,1408]{1,0:T(8,128)(2,1)S(1)}, u32[]{:S(2)}, u32[]{:S(2)}) collective-permute-start(bf16[128,1408]{1,0:T(8,128)(2,1)S(1)} %get-tuple-element.43), channel_id=1, source_target_pairs={{0,2},{1,3},{2,8},{3,9},{4,6},{5,7},{6,4},{7,5},{8,10},{9,11},{10,... | collective-permute-start | bytes 1081352 | tf_op jit(solution)/shard_map/ppermute | solution.py:58
  41.6 19.6 %collective-permute-start.1 = (bf16[128,1408]{1,0:T(8,128)(2,1)S(1)}, bf16[128,1408]{1,0:T(8,128)(2,1)S(1)}, u32[]{:S(2)}, u32[]{:S(2)}) collective-permute-start(bf16[128,1408]{1,0:T(8,128)(2,1)S(1)} %get-tuple-element.44), channel_id=1, source_target_pairs={{0,1},{1,2},{2,3},{3,8},{4,5},{5,6},{6,7},{7,4},{8,9},{9,10},{10,1... | collective-permute-start | bytes 1081352 | tf_op jit(solution)/shard_map/ppermute | solution.py:58
  44.8 23.4 %collective-permute-start.7 = (bf16[128,1280]{1,0:T(8,128)(2,1)S(1)}, bf16[128,1280]{1,0:T(8,128)(2,1)S(1)}, u32[]{:S(2)}, u32[]{:S(2)}) collective-permute-start(bf16[128,1280]{1,0:T(8,128)(2,1)S(1)} %broadcast_select_fusion.3), channel_id=1, source_target_pairs={{0,1},{1,2},{2,3},{3,8},{4,5},{5,6},{6,7},{7,4},{8,9},{9,10},{10,1... | collective-permute-start | bytes 983048 | tf_op jit(solution)/shard_map/ppermute | solution.py:58
  46.8 21.4 %collective-permute-start.9 = (bf16[128,1280]{1,0:T(8,128)(2,1)S(1)}, bf16[128,1280]{1,0:T(8,128)(2,1)S(1)}, u32[]{:S(2)}, u32[]{:S(2)}) collective-permute-start(bf16[128,1280]{1,0:T(8,128)(2,1)S(1)} %collective-permute-done.5), channel_id=1, source_target_pairs={{1,8},{2,9},{5,4},{6,5},{9,16},{10,17},{13,12},{14,13},{17,24},{18... | collective-permute-start | bytes 983048 | tf_op jit(solution)/shard_map/ppermute | solution.py:58
  54.6 13.6 %collective-permute-start.8 = (bf16[128,1280]{1,0:T(8,128)(2,1)S(1)}, bf16[128,1280]{1,0:T(8,128)(2,1)S(1)}, u32[]{:S(2)}, u32[]{:S(2)}) collective-permute-start(bf16[128,1280]{1,0:T(8,128)(2,1)S(1)} %collective-permute-done.5), channel_id=1, source_target_pairs={{0,8},{1,9},{2,10},{4,4},{5,5},{6,6},{8,16},{9,17},{10,18},{12,12}... | collective-permute-start | bytes 983048 | tf_op jit(solution)/shard_map/ppermute | solution.py:58
  56.6 4.6 %copy-start.4 = (f32[128,16]{0,1:T(8,128)S(1)}, f32[128,16]{0,1:T(8,128)}, u32[]{:S(2)}) copy-start(f32[128,16]{0,1:T(8,128)} %param.17) | copy-start | bytes 24580
  56.7 4.5 %copy-start.5 = (s32[512]{0:T(512)S(1)}, s32[512]{0:T(512)}, u32[]{:S(2)}) copy-start(s32[512]{0:T(512)} %length_ref.1) | copy-start | bytes 6148
  61.2 3.6 %copy-start.1 = (bf16[128,2048]{1,0:T(8,128)(2,1)S(1)}, bf16[128,2048]{1,0:T(8,128)(2,1)}, u32[]{:S(2)}) copy-start(bf16[128,2048]{1,0:T(8,128)(2,1)} %refs_6_.1) | copy-start | bytes 1572868
  72.1 22.0 %collective-permute-start.10 = (bf16[128,640]{1,0:T(8,128)(2,1)S(1)}, bf16[128,640]{1,0:T(8,128)(2,1)S(1)}, u32[]{:S(2)}, u32[]{:S(2)}) collective-permute-start(bf16[128,640]{1,0:T(8,128)(2,1)S(1)} %get-tuple-element.37), channel_id=1, source_target_pairs={{3,0},{4,1},{5,2},{6,3},{7,4},{8,5},{9,6},{10,7},{11,8},{12,9},{13... | collective-permute-start | bytes 491528 | tf_op jit(solution)/shard_map/ppermute | solution.py:387
  81.4 12.7 %collective-permute-start.11 = (bf16[128,640]{1,0:T(8,128)(2,1)S(1)}, bf16[128,640]{1,0:T(8,128)(2,1)S(1)}, u32[]{:S(2)}, u32[]{:S(2)}) collective-permute-start(bf16[128,640]{1,0:T(8,128)(2,1)S(1)} %get-tuple-element.38), channel_id=1, source_target_pairs={{1,0},{2,1},{3,2},{4,3},{5,4},{6,5},{7,6},{8,7},{9,8},{10,9},{11,1... | collective-permute-start | bytes 491528 | tf_op jit(solution)/shard_map/ppermute | solution.py:387
  83.3 17.7 %collective-permute-start.12 = (bf16[128,640]{1,0:T(8,128)(2,1)S(1)}, bf16[128,640]{1,0:T(8,128)(2,1)S(1)}, u32[]{:S(2)}, u32[]{:S(2)}) collective-permute-start(bf16[128,640]{1,0:T(8,128)(2,1)S(1)} %get-tuple-element.39), channel_id=1, source_target_pairs={{2,0},{3,1},{4,2},{5,3},{6,4},{7,5},{8,6},{9,7},{10,8},{11,9},{12,... | collective-permute-start | bytes 491528 | tf_op jit(solution)/shard_map/ppermute | solution.py:387

commit v5 on v4

--- a/solution.py
+++ b/solution.py
@@ -389,7 +389,7 @@
             AXES,
             [(b, b - distance) for b in range(distance, lax.axis_size(AXES))],
         )
-        for distance in (3, 1, 2)
+        for distance in (2, 3, 1)
     ]
     d_nope, d_rope = query_call((FIRST, PAIRS - FIRST), (g0, g1), lrt, up_weight)
     d_latent, d_key_rope = finish_call(kept, received)

time: 102 us -> 108 us (1.059)
  the two profiles are of different devices: /device:TPU:189 before, /device:TPU:191 now
where the time goes in v5:
time: 108 us; the launch traced here: 107 us
  starting transfers between devices  45.7 us (42%)
  waiting for transfers between devices  40.5 us (38%)
  Pallas kernels  17.9 us (17%)
  between operations  1.62 us (2%)
  other arithmetic  1.25 us (1%)
    ppermute x10, starting transfers between devices, permute(): return lax.ppermute(value, AXES, route(lax.axis_size(AXES)))  30.1 us
    ppermute x10, waiting for transfers between devices, permute(): return lax.ppermute(value, AXES, route(lax.axis_size(AXES)))  26.2 us
    ppermute x3, starting transfers between devices, on_device(): lax.ppermute(sent[distance - 1], AXES, [(b, b - distance) for b in range(...  15.6 us
    ppermute x3, waiting for transfers between devices, on_device(): lax.ppermute(sent[distance - 1], AXES, [(b, b - distance) for b in range(...  14.3 us
    pallas_call x2, Pallas kernels, teacher_call(): call(functools.partial(teacher_kernel, first, pairs, start), [SMEM] + [AN...  6.49 us
    pallas_call x1, Pallas kernels, query_call(): call(functools.partial(query_kernel, counts), [VMEM] * (len(counts) + 2),...  5.05 us
    pallas_call x1, Pallas kernels, student_call(): call(student_kernel, [SMEM, SMEM, VMEM, VMEM] + [ANY] * SPAN, [shape(KEYS...  3.55 us
  transfers between devices with their start and end apart: 13, of which 4 were waited for; matrix products, arithmetic and copies ran while one was open for 1% of the time, Pallas kernels for 11%

profile of v5, /device:TPU:191, one launch (start us, length us, event | category | flops | bytes accessed | tf_op | source)
XLA Modules:
  0.0 107.0 jit_solution(40444306788079065)
XLA Ops:
  0.6 0.0 copy-start
  0.6 0.0 copy-start.3
  0.7 1.3 %shard_map.129 = (bf16[128,1408]{1,0:T(8,128)(2,1)S(1)}, bf16[128,1280]{1,0:T(8,128)(2,1)S(1)}) custom-call(bf16[128,512]{1,0:T(8,128)(2,1)} %latent_ref.1, bf16[64,128]{1,0:T(8,128)(2,1)} %bitcast.5, bf16[128,2048]{1,0:T(8,128)(2,1)} %key_ref.1), custom_call_target="tpu_custom_call" | custom-call | bytes 2000000 | tf_op jit(solution)/shard_map/pallas_call | solution.py:254
  2.0 2.5 %collective-permute-start.4 = (bf16[128,1280]{1,0:T(8,128)(2,1)S(1)}, bf16[128,1280]{1,0:T(8,128)(2,1)S(1)}, u32[]{:S(2)}, u32[]{:S(2)}) collective-permute-start(bf16[128,1280]{1,0:T(8,128)(2,1)S(1)} %get-tuple-element.25.refs_0_), channel_id=1, source_target_pairs={{0,3},{1,0},{2,1},{3,2},{4,7},{5,4},{6,5},{7,6},{8,11},{9,8},{10,9... | collective-permute-start | bytes 983048 | tf_op jit(solution)/shard_map/ppermute | solution.py:58
  4.5 8.8 %collective-permute-start = (bf16[128,1408]{1,0:T(8,128)(2,1)S(1)}, bf16[128,1408]{1,0:T(8,128)(2,1)}, u32[]{:S(2)}, u32[]{:S(2)}) collective-permute-start(bf16[128,1408]{1,0:T(8,128)(2,1)S(1)} %get-tuple-element.23.refs_0_), channel_id=1, source_target_pairs={{0,4},{1,5},{2,6},{3,7},{4,0},{5,1},{6,2},{7,3},{8,12},{9,13},{10,... | collective-permute-start | bytes 1081352 | tf_op jit(solution)/shard_map/ppermute | solution.py:58
  13.3 0.0 copy-start.2
  14.0 0.0 collective-permute-done.4.refs_3_
  14.1 8.5 %collective-permute-start.5 = (bf16[128,1280]{1,0:T(8,128)(2,1)S(1)}, bf16[128,1280]{1,0:T(8,128)(2,1)S(1)}, u32[]{:S(2)}, u32[]{:S(2)}) collective-permute-start(bf16[128,1280]{1,0:T(8,128)(2,1)S(1)} %broadcast_select_fusion.4), channel_id=1, source_target_pairs={{0,4},{1,5},{2,6},{3,7},{4,0},{5,1},{6,2},{7,3},{8,12},{9,13},{10,... | collective-permute-start | bytes 983048 | tf_op jit(solution)/shard_map/ppermute | solution.py:58
  22.6 1.3 %collective-permute-start.6 = (bf16[128,1280]{1,0:T(8,128)(2,1)S(1)}, bf16[128,1280]{1,0:T(8,128)(2,1)S(1)}, u32[]{:S(2)}, u32[]{:S(2)}) collective-permute-start(bf16[128,1280]{1,0:T(8,128)(2,1)S(1)} %get-tuple-element.25.refs_0_), channel_id=1, source_target_pairs={{0,2},{1,3},{4,6},{5,7},{8,10},{9,11},{12,14},{13,15},{16,18},{17,... | collective-permute-start | bytes 983048 | tf_op jit(solution)/shard_map/ppermute | solution.py:58
  23.9 13.1 %collective-permute-done = bf16[128,1408]{1,0:T(8,128)(2,1)} collective-permute-done((bf16[128,1408]{1,0:T(8,128)(2,1)S(1)}, bf16[128,1408]{1,0:T(8,128)(2,1)}, u32[]{:S(2)}, u32[]{:S(2)}) %collective-permute-start) | collective-permute-done | bytes 360480 | tf_op jit(solution)/shard_map/ppermute | solution.py:58
  37.0 1.1 %broadcast_select_fusion = (bf16[128,1408]{1,0:T(8,128)(2,1)S(1)}, bf16[128,1408]{1,0:T(8,128)(2,1)S(1)}, bf16[128,1408]{1,0:T(8,128)(2,1)S(1)}) fusion(bf16[128,1408]{1,0:T(8,128)(2,1)} %collective-permute-done, bf16[128,1408]{1,0:T(8,128)(2,1)S(1)} %get-tuple-element.23.refs_0_, pred[]{:T(512)S(6)} %ge.11, pred[]{:T(512)S(6)} %ge.10, pred[]{:T(512)S(6)} %ge.9), kind=kLoop, calls=%fused_computation | loop fusion | flops 540672 | bytes 1802243 | tf_op jit(solution)/shard_map/jit(_where)/select_n | solution.py:367
  38.1 1.9 %collective-permute-start.3 = (bf16[128,1408]{1,0:T(8,128)(2,1)S(1)}, bf16[128,1408]{1,0:T(8,128)(2,1)S(1)}, u32[]{:S(2)}, u32[]{:S(2)}) collective-permute-start(bf16[128,1408]{1,0:T(8,128)(2,1)S(1)} %get-tuple-element.42), channel_id=1, source_target_pairs={{0,3},{1,8},{2,9},{3,10},{4,7},{5,4},{6,5},{7,6},{8,11},{9,16},{10... | collective-permute-start | bytes 1081352 | tf_op jit(solution)/shard_map/ppermute | solution.py:58
  40.0 1.9 %collective-permute-start.2 = (bf16[128,1408]{1,0:T(8,128)(2,1)S(1)}, bf16[128,1408]{1,0:T(8,128)(2,1)S(1)}, u32[]{:S(2)}, u32[]{:S(2)}) collective-permute-start(bf16[128,1408]{1,0:T(8,128)(2,1)S(1)} %get-tuple-element.43), channel_id=1, source_target_pairs={{0,2},{1,3},{2,8},{3,9},{4,6},{5,7},{6,4},{7,5},{8,10},{9,11},{10,... | collective-permute-start | bytes 1081352 | tf_op jit(solution)/shard_map/ppermute | solution.py:58
  41.9 1.9 %collective-permute-start.1 = (bf16[128,1408]{1,0:T(8,128)(2,1)S(1)}, bf16[128,1408]{1,0:T(8,128)(2,1)S(1)}, u32[]{:S(2)}, u32[]{:S(2)}) collective-permute-start(bf16[128,1408]{1,0:T(8,128)(2,1)S(1)} %get-tuple-element.44), channel_id=1, source_target_pairs={{0,1},{1,2},{2,3},{3,8},{4,5},{5,6},{6,7},{7,4},{8,9},{9,10},{10,1... | collective-permute-start | bytes 1081352 | tf_op jit(solution)/shard_map/ppermute | solution.py:58
  43.9 0.0 collective-permute-done.5
  44.0 1.9 %collective-permute-start.7 = (bf16[128,1280]{1,0:T(8,128)(2,1)S(1)}, bf16[128,1280]{1,0:T(8,128)(2,1)S(1)}, u32[]{:S(2)}, u32[]{:S(2)}) collective-permute-start(bf16[128,1280]{1,0:T(8,128)(2,1)S(1)} %broadcast_select_fusion.3), channel_id=1, source_target_pairs={{0,1},{1,2},{2,3},{3,8},{4,5},{5,6},{6,7},{7,4},{8,9},{9,10},{10,1... | collective-permute-start | bytes 983048 | tf_op jit(solution)/shard_map/ppermute | solution.py:58
  45.9 0.0 collective-permute-done.6.refs_2_
  45.9 0.7 collective-permute-start.9
  46.6 4.3 %collective-permute-done.3.refs_3_ = bf16[128,1408]{1,0:T(8,128)(2,1)S(1)} collective-permute-done((bf16[128,1408]{1,0:T(8,128)(2,1)S(1)}, bf16[128,1408]{1,0:T(8,128)(2,1)S(1)}, u32[]{:S(2)}, u32[]{:S(2)}) %collective-permute-start.3) | collective-permute-done | bytes 360480 | tf_op jit(solution)/shard_map/ppermute | solution.py:58
  50.9 0.7 collective-permute-start.8
  51.6 0.1 pad_add_fusion.scalar_ref
  51.7 0.0 copy-done
  51.7 0.0 copy-done.3
  51.7 0.0 copy-done.2
  51.7 0.0 copy-start.4
  51.7 0.0 copy-start.5
  51.7 0.7 shard_map.130.mixed_ref.refs_8_.refs_10_
  52.4 8.7 %collective-permute-done.2.refs_2_ = bf16[128,1408]{1,0:T(8,128)(2,1)S(1)} collective-permute-done((bf16[128,1408]{1,0:T(8,128)(2,1)S(1)}, bf16[128,1408]{1,0:T(8,128)(2,1)S(1)}, u32[]{:S(2)}, u32[]{:S(2)}) %collective-permute-start.2) | collective-permute-done | bytes 360480 | tf_op jit(solution)/shard_map/ppermute | solution.py:58
  61.1 0.0 collective-permute-done.1.refs_1_
  61.1 0.0 copy-done.4
  61.1 0.0 copy-done.5
  61.1 0.0 copy-start.1
  61.1 3.5 %shard_map.131 = (f32[512,2048]{1,0:T(8,128)S(1)}, f32[512,128]{1,0:T(8,128)S(1)}, f32[16,128]{1,0:T(8,128)S(1)}, bf16[640,512]{1,0:T(8,128)(2,1)S(1)}) custom-call(s32[2]{0:T(128)S(1)} %pad_add_fusion.scalar_ref, s32[512]{0:T(512)S(1)} %copy-done.5, f32[16,128]{1,0:T(8,128)S(1)} %bitcast.4, bf16[2048,640]{1,0:T(8,128)(2,1)S(1)} %shard_map.130.mixed_ref.refs_8_.refs_10_, ...), custom_call_target="tpu_custom_call" | custom-call | flops 1342177280 | bytes 8000000 | tf_op jit(solution)/shard_map/pallas_call | solution.py:276
  64.7 0.0 copy-done.1
  64.7 2.7 %shard_map.132 = (bf16[512,768]{1,0:T(8,128)(2,1)S(1)}, f32[512,640]{1,0:T(8,128)S(1)}) custom-call(s32[2]{0:T(128)S(1)} %pad_add_fusion.scalar_ref, bf16[128,1408]{1,0:T(8,128)(2,1)S(1)} %get-tuple-element.23.refs_0_, bf16[128,1408]{1,0:T(8,128)(2,1)S(1)} %collective-permute-done.1.refs_1_, bf16[128,1408]{1,0:T(8,128)(2,1)S(1)} %collective-permute-done.2.refs_2_, ...), custom_call_target="tpu_custom_call" | custom-call | flops 704643072 | bytes 4500000 | tf_op jit(solution)/shard_map/pallas_call | solution.py:298
  67.3 0.0 collective-permute-done.7.refs_1_
  67.4 0.0 collective-permute-done.9.refs_5_
  67.4 0.0 collective-permute-done.8.refs_4_
  67.4 3.8 %shard_map.133 = (bf16[512,1280]{1,0:T(8,128)(2,1)S(1)}, f32[128,640]{1,0:T(8,128)S(1)}, bf16[128,640]{1,0:T(8,128)(2,1)S(1)}, bf16[128,640]{1,0:T(8,128)(2,1)S(1)}, bf16[128,640]{1,0:T(8,128)(2,1)S(1)}) custom-call(s32[2]{0:T(128)S(1)} %pad_add_fusion.scalar_ref, bf16[128,1280]{1,0:T(8,128)(2,1)S(1)} %get-tuple-element.25.refs_0_, ...), custom_call_target="tpu_custom_call" | custom-call | flops 1174405120 | bytes 7500000 | tf_op jit(solution)/shard_map/pallas_call | solution.py:298
  71.2 4.7 %collective-permute-start.10 = (bf16[128,640]{1,0:T(8,128)(2,1)S(1)}, bf16[128,640]{1,0:T(8,128)(2,1)S(1)}, u32[]{:S(2)}, u32[]{:S(2)}) collective-permute-start(bf16[128,640]{1,0:T(8,128)(2,1)S(1)} %get-tuple-element.37), channel_id=1, source_target_pairs={{2,0},{3,1},{4,2},{5,3},{6,4},{7,5},{8,6},{9,7},{10,8},{11,9},{12,... | collective-permute-start | bytes 491528 | tf_op jit(solution)/shard_map/ppermute | solution.py:387
  75.9 8.4 %collective-permute-start.11 = (bf16[128,640]{1,0:T(8,128)(2,1)S(1)}, bf16[128,640]{1,0:T(8,128)(2,1)S(1)}, u32[]{:S(2)}, u32[]{:S(2)}) collective-permute-start(bf16[128,640]{1,0:T(8,128)(2,1)S(1)} %get-tuple-element.38), channel_id=1, source_target_pairs={{3,0},{4,1},{5,2},{6,3},{7,4},{8,5},{9,6},{10,7},{11,8},{12,9},{13... | collective-permute-start | bytes 491528 | tf_op jit(solution)/shard_map/ppermute | solution.py:387
  84.3 2.5 %collective-permute-start.12 = (bf16[128,640]{1,0:T(8,128)(2,1)S(1)}, bf16[128,640]{1,0:T(8,128)(2,1)S(1)}, u32[]{:S(2)}, u32[]{:S(2)}) collective-permute-start(bf16[128,640]{1,0:T(8,128)(2,1)S(1)} %get-tuple-element.39), channel_id=1, source_target_pairs={{1,0},{2,1},{3,2},{4,3},{5,4},{6,5},{7,6},{8,7},{9,8},{10,9},{11,1... | collective-permute-start | bytes 491528 | tf_op jit(solution)/shard_map/ppermute | solution.py:387
  86.9 5.1 %shard_map.134 = (bf16[128,2048]{1,0:T(8,128)(2,1)}, bf16[128,1024]{1,0:T(8,128)(2,1)}) custom-call(bf16[512,768]{1,0:T(8,128)(2,1)S(1)} %get-tuple-element.30.refs_0_, bf16[512,1280]{1,0:T(8,128)(2,1)S(1)} %get-tuple-element.32.refs_1_, bf16[640,512]{1,0:T(8,128)(2,1)S(1)} %get-tuple-element.33.refs_2_, bf16[16,128,512]{2,1,0:T(8,128)(2,1)S(1)} %copy-done), custom_call_target="tpu_custom_call" | custom-call | flops 2684354560 | bytes 6000000 | tf_op jit(solution)/shard_map/pallas_call | solution.py:314
  91.9 0.0 collective-permute-done.10.one_ref
  91.9 0.0 collective-permute-done.11.two_ref
  91.9 14.3 %collective-permute-done.12.three_ref = bf16[128,640]{1,0:T(8,128)(2,1)S(1)} collective-permute-done((bf16[128,640]{1,0:T(8,128)(2,1)S(1)}, bf16[128,640]{1,0:T(8,128)(2,1)S(1)}, u32[]{:S(2)}, u32[]{:S(2)}) %collective-permute-start.12) | collective-permute-done | bytes 163872 | tf_op jit(solution)/shard_map/ppermute | solution.py:387
  106.2 0.8 shard_map.135
  (2 shorter events, 0.1 us)
Async XLA Ops:
  0.6 51.1 %copy-start = (bf16[16,128,512]{2,1,0:T(8,128)(2,1)S(1)}, bf16[16,128,512]{2,1,0:T(8,128)(2,1)}, u32[]{:S(2)}) copy-start(bf16[16,128,512]{2,1,0:T(8,128)(2,1)} %refs_3_.1) | copy-start | bytes 6291460
  0.6 51.1 %copy-start.3 = (bf16[128,1024]{1,0:T(8,128)(2,1)S(1)}, bf16[128,1024]{1,0:T(8,128)(2,1)}, u32[]{:S(2)}) copy-start(bf16[128,1024]{1,0:T(8,128)(2,1)} %rope_ref.1) | copy-start | bytes 786436
  2.0 12.1 %collective-permute-start.4 = (bf16[128,1280]{1,0:T(8,128)(2,1)S(1)}, bf16[128,1280]{1,0:T(8,128)(2,1)S(1)}, u32[]{:S(2)}, u32[]{:S(2)}) collective-permute-start(bf16[128,1280]{1,0:T(8,128)(2,1)S(1)} %get-tuple-element.25.refs_0_), channel_id=1, source_target_pairs={{0,3},{1,0},{2,1},{3,2},{4,7},{5,4},{6,5},{7,6},{8,11},{9,8},{10,9... | collective-permute-start | bytes 983048 | tf_op jit(solution)/shard_map/ppermute | solution.py:58
  4.5 32.5 %collective-permute-start = (bf16[128,1408]{1,0:T(8,128)(2,1)S(1)}, bf16[128,1408]{1,0:T(8,128)(2,1)}, u32[]{:S(2)}, u32[]{:S(2)}) collective-permute-start(bf16[128,1408]{1,0:T(8,128)(2,1)S(1)} %get-tuple-element.23.refs_0_), channel_id=1, source_target_pairs={{0,4},{1,5},{2,6},{3,7},{4,0},{5,1},{6,2},{7,3},{8,12},{9,13},{10,... | collective-permute-start | bytes 1081352 | tf_op jit(solution)/shard_map/ppermute | solution.py:58
  13.3 38.4 %copy-start.2 = (bf16[128,2048]{1,0:T(8,128)(2,1)S(1)}, bf16[128,2048]{1,0:T(8,128)(2,1)}, u32[]{:S(2)}) copy-start(bf16[128,2048]{1,0:T(8,128)(2,1)} %nope_ref) | copy-start | bytes 1572868
  14.1 29.8 %collective-permute-start.5 = (bf16[128,1280]{1,0:T(8,128)(2,1)S(1)}, bf16[128,1280]{1,0:T(8,128)(2,1)S(1)}, u32[]{:S(2)}, u32[]{:S(2)}) collective-permute-start(bf16[128,1280]{1,0:T(8,128)(2,1)S(1)} %broadcast_select_fusion.4), channel_id=1, source_target_pairs={{0,4},{1,5},{2,6},{3,7},{4,0},{5,1},{6,2},{7,3},{8,12},{9,13},{10,... | collective-permute-start | bytes 983048 | tf_op jit(solution)/shard_map/ppermute | solution.py:58
  22.6 23.3 %collective-permute-start.6 = (bf16[128,1280]{1,0:T(8,128)(2,1)S(1)}, bf16[128,1280]{1,0:T(8,128)(2,1)S(1)}, u32[]{:S(2)}, u32[]{:S(2)}) collective-permute-start(bf16[128,1280]{1,0:T(8,128)(2,1)S(1)} %get-tuple-element.25.refs_0_), channel_id=1, source_target_pairs={{0,2},{1,3},{4,6},{5,7},{8,10},{9,11},{12,14},{13,15},{16,18},{17,... | collective-permute-start | bytes 983048 | tf_op jit(solution)/shard_map/ppermute | solution.py:58
  38.1 12.9 %collective-permute-start.3 = (bf16[128,1408]{1,0:T(8,128)(2,1)S(1)}, bf16[128,1408]{1,0:T(8,128)(2,1)S(1)}, u32[]{:S(2)}, u32[]{:S(2)}) collective-permute-start(bf16[128,1408]{1,0:T(8,128)(2,1)S(1)} %get-tuple-element.42), channel_id=1, source_target_pairs={{0,3},{1,8},{2,9},{3,10},{4,7},{5,4},{6,5},{7,6},{8,11},{9,16},{10... | collective-permute-start | bytes 1081352 | tf_op jit(solution)/shard_map/ppermute | solution.py:58
  40.0 21.1 %collective-permute-start.2 = (bf16[128,1408]{1,0:T(8,128)(2,1)S(1)}, bf16[128,1408]{1,0:T(8,128)(2,1)S(1)}, u32[]{:S(2)}, u32[]{:S(2)}) collective-permute-start(bf16[128,1408]{1,0:T(8,128)(2,1)S(1)} %get-tuple-element.43), channel_id=1, source_target_pairs={{0,2},{1,3},{2,8},{3,9},{4,6},{5,7},{6,4},{7,5},{8,10},{9,11},{10,... | collective-permute-start | bytes 1081352 | tf_op jit(solution)/shard_map/ppermute | solution.py:58
  41.9 19.2 %collective-permute-start.1 = (bf16[128,1408]{1,0:T(8,128)(2,1)S(1)}, bf16[128,1408]{1,0:T(8,128)(2,1)S(1)}, u32[]{:S(2)}, u32[]{:S(2)}) collective-permute-start(bf16[128,1408]{1,0:T(8,128)(2,1)S(1)} %get-tuple-element.44), channel_id=1, source_target_pairs={{0,1},{1,2},{2,3},{3,8},{4,5},{5,6},{6,7},{7,4},{8,9},{9,10},{10,1... | collective-permute-start | bytes 1081352 | tf_op jit(solution)/shard_map/ppermute | solution.py:58
  44.0 23.4 %collective-permute-start.7 = (bf16[128,1280]{1,0:T(8,128)(2,1)S(1)}, bf16[128,1280]{1,0:T(8,128)(2,1)S(1)}, u32[]{:S(2)}, u32[]{:S(2)}) collective-permute-start(bf16[128,1280]{1,0:T(8,128)(2,1)S(1)} %broadcast_select_fusion.3), channel_id=1, source_target_pairs={{0,1},{1,2},{2,3},{3,8},{4,5},{5,6},{6,7},{7,4},{8,9},{9,10},{10,1... | collective-permute-start | bytes 983048 | tf_op jit(solution)/shard_map/ppermute | solution.py:58
  45.9 21.5 %collective-permute-start.9 = (bf16[128,1280]{1,0:T(8,128)(2,1)S(1)}, bf16[128,1280]{1,0:T(8,128)(2,1)S(1)}, u32[]{:S(2)}, u32[]{:S(2)}) collective-permute-start(bf16[128,1280]{1,0:T(8,128)(2,1)S(1)} %collective-permute-done.5), channel_id=1, source_target_pairs={{1,8},{2,9},{5,4},{6,5},{9,16},{10,17},{13,12},{14,13},{17,24},{18... | collective-permute-start | bytes 983048 | tf_op jit(solution)/shard_map/ppermute | solution.py:58
  50.9 16.4 %collective-permute-start.8 = (bf16[128,1280]{1,0:T(8,128)(2,1)S(1)}, bf16[128,1280]{1,0:T(8,128)(2,1)S(1)}, u32[]{:S(2)}, u32[]{:S(2)}) collective-permute-start(bf16[128,1280]{1,0:T(8,128)(2,1)S(1)} %collective-permute-done.5), channel_id=1, source_target_pairs={{0,8},{1,9},{2,10},{4,4},{5,5},{6,6},{8,16},{9,17},{10,18},{12,12}... | collective-permute-start | bytes 983048 | tf_op jit(solution)/shard_map/ppermute | solution.py:58
  51.7 9.4 %copy-start.4 = (f32[128,16]{0,1:T(8,128)S(1)}, f32[128,16]{0,1:T(8,128)}, u32[]{:S(2)}) copy-start(f32[128,16]{0,1:T(8,128)} %param.17) | copy-start | bytes 24580
  51.7 9.4 %copy-start.5 = (s32[512]{0:T(512)S(1)}, s32[512]{0:T(512)}, u32[]{:S(2)}) copy-start(s32[512]{0:T(512)} %length_ref.1) | copy-start | bytes 6148
  61.1 3.6 %copy-start.1 = (bf16[128,2048]{1,0:T(8,128)(2,1)S(1)}, bf16[128,2048]{1,0:T(8,128)(2,1)}, u32[]{:S(2)}) copy-start(bf16[128,2048]{1,0:T(8,128)(2,1)} %refs_6_.1) | copy-start | bytes 1572868
  71.2 20.7 %collective-permute-start.10 = (bf16[128,640]{1,0:T(8,128)(2,1)S(1)}, bf16[128,640]{1,0:T(8,128)(2,1)S(1)}, u32[]{:S(2)}, u32[]{:S(2)}) collective-permute-start(bf16[128,640]{1,0:T(8,128)(2,1)S(1)} %get-tuple-element.37), channel_id=1, source_target_pairs={{2,0},{3,1},{4,2},{5,3},{6,4},{7,5},{8,6},{9,7},{10,8},{11,9},{12,... | collective-permute-start | bytes 491528 | tf_op jit(solution)/shard_map/ppermute | solution.py:387
  75.9 16.0 %collective-permute-start.11 = (bf16[128,640]{1,0:T(8,128)(2,1)S(1)}, bf16[128,640]{1,0:T(8,128)(2,1)S(1)}, u32[]{:S(2)}, u32[]{:S(2)}) collective-permute-start(bf16[128,640]{1,0:T(8,128)(2,1)S(1)} %get-tuple-element.38), channel_id=1, source_target_pairs={{3,0},{4,1},{5,2},{6,3},{7,4},{8,5},{9,6},{10,7},{11,8},{12,9},{13... | collective-permute-start | bytes 491528 | tf_op jit(solution)/shard_map/ppermute | solution.py:387
  84.3 21.9 %collective-permute-start.12 = (bf16[128,640]{1,0:T(8,128)(2,1)S(1)}, bf16[128,640]{1,0:T(8,128)(2,1)S(1)}, u32[]{:S(2)}, u32[]{:S(2)}) collective-permute-start(bf16[128,640]{1,0:T(8,128)(2,1)S(1)} %get-tuple-element.39), channel_id=1, source_target_pairs={{1,0},{2,1},{3,2},{4,3},{5,4},{6,5},{7,6},{8,7},{9,8},{10,9},{11,1... | collective-permute-start | bytes 491528 | tf_op jit(solution)/shard_map/ppermute | solution.py:387
